TPU v7x, 32 devices: a whole 2x2x4 slice. The times are simulated.
32 devices in a mesh: group: 8 (over y, x, core), peer: 4 (over z).
Axes of the slice: x: 2, y: 2, z: 4, core: 2. Of those that a mesh axis runs over, the one named last changes fastest.
Arguments:
- table: bfloat16 [131072, 256], P(('group', 'peer')), may hold values from -6 to 6
- behaviour_ids: int32 [64, 1024], P(('group', 'peer')), may hold values from 0 to 131071, as said below
- lengths: int32 [64], P(('group', 'peer')), may hold values from 256 to 1024, as said below
- candidates: bfloat16 [64, 64, 256], P('group', 'peer'), may hold values from -6 to 6
- labels: float32 [64, 64], P('group', 'peer'), may hold values from 0 to 1
- cand_counts: int32 [64], P(('group', 'peer')), may hold values from 4 to 64, as said below
- w_query: bfloat16 [256, 256], replicated, may hold values from -0.375 to 0.375
- w_key: bfloat16 [256, 256], replicated, may hold values from -0.375 to 0.375
- w_value: bfloat16 [256, 256], replicated, may hold values from -0.375 to 0.375
- w_out: bfloat16 [256, 256], replicated, may hold values from -0.375 to 0.375
Outputs:
- table_grad: bfloat16 [131072, 256], P(('group', 'peer'))
- weight_grads: float32 [4, 256, 256], replicated
Inputs may be any that keep to these rules, and one draw needn't show every extreme that they name: `behaviour_ids`: device d of group+peer (group slowest) holds table rows 4096 * d to 4096 * (d + 1) - 1. Among the 2048 behaviour slots of the users of one device, at most 96 name rows held by any one device, and for every device some device's rows are named exactly 96 times. Ids may repeat. `lengths`: some user has 1024 live slots. `cand_counts`: some user has 64 live candidates.
All inputs are finite; a program needn't handle non-finite values.
Results may differ from a plain program's by a relative error of at most 0.018.
Values may be sent and summed in bfloat16 or wider, within the bound.
No kernel may reach another device: no remote copies, remote signals or barrier semaphores. Data moves between devices by JAX's collectives and lax.ppermute only.
A program may use at most 64 MiB of HBM per device.

v0:
```python
import jax
import jax.numpy as jnp
from jax import lax
from jax.sharding import PartitionSpec as P

HEADS = 4
USERS_DEV = 2
ROWS_DEV = 4096


def bucket_plan(behaviour_ids, shards, capacity):
    flat = behaviour_ids.reshape(-1)
    total = flat.shape[0]
    owner = flat // ROWS_DEV
    local_row = flat - owner * ROWS_DEV
    order = jnp.argsort(owner, stable=True)
    sorted_owner = owner[order]
    onehot = (owner[:, None] == jnp.arange(shards, dtype=jnp.int32)[None, :]).astype(jnp.int32)
    counts = jnp.sum(onehot, axis=0)
    starts = jnp.cumsum(counts) - counts
    rank = jnp.arange(total, dtype=jnp.int32) - starts[sorted_owner]
    slot_sorted = sorted_owner * capacity + rank
    position = jnp.zeros((total,), jnp.int32).at[order].set(slot_sorted)
    requests = jnp.zeros((shards * capacity,), jnp.int32).at[slot_sorted].set(local_row[order])
    return (position, requests.reshape(shards, capacity))


def local(
    table, behaviour_ids, lengths, candidates, labels, cand_counts, w_query, w_key, w_value, w_out
):
    shards = lax.axis_size(("group", "peer"))
    users, seq = behaviour_ids.shape
    width = table.shape[1]
    head_size = width // HEADS
    total = users * seq
    capacity = total // shards + total // (2 * shards)
    scale = float(head_size) ** (-0.5)
    root = float(width) ** 0.5
    position, requests = bucket_plan(behaviour_ids, shards, capacity)
    wanted = lax.all_to_all(requests, ("group", "peer"), split_axis=0, concat_axis=0, tiled=True)
    served = table[wanted.reshape(-1)].reshape(shards, capacity, width)
    arrived = lax.all_to_all(served, ("group", "peer"), split_axis=0, concat_axis=0, tiled=True)
    rows = arrived.reshape(shards * capacity, width)[position].reshape(users, seq, width)
    cands, label = (
        lax.all_to_all(candidates, "peer", split_axis=0, concat_axis=1, tiled=True),
        lax.all_to_all(
            labels.astype(jnp.bfloat16), "peer", split_axis=0, concat_axis=1, tiled=True
        ).astype(labels.dtype),
    )
    num = cands.shape[1]
    query = jnp.einsum("uce,ef->ucf", cands, w_query, preferred_element_type=jnp.float32).astype(
        jnp.bfloat16
    )
    keys = jnp.einsum("ule,ef->ulf", rows, w_key, preferred_element_type=jnp.float32).astype(
        jnp.bfloat16
    )
    values = jnp.einsum("ule,ef->ulf", rows, w_value, preferred_element_type=jnp.float32).astype(
        jnp.bfloat16
    )
    q_heads = query.reshape(users, num, HEADS, head_size)
    k_heads = keys.reshape(users, seq, HEADS, head_size)
    v_heads = values.reshape(users, seq, HEADS, head_size)
    scores = (
        jnp.einsum("uchd,ulhd->uhcl", q_heads, k_heads, preferred_element_type=jnp.float32) * scale
    )
    live_key = jnp.arange(seq, dtype=jnp.int32)[None, :] < lengths[:, None]
    scores = jnp.where(live_key[:, None, None, :], scores, jnp.float32(-1e30))
    probs = jax.nn.softmax(scores, axis=-1)
    probs_b = probs.astype(jnp.bfloat16)
    mixed = (
        jnp.einsum("uhcl,ulhd->uchd", probs_b, v_heads, preferred_element_type=jnp.float32)
        .reshape(users, num, width)
        .astype(jnp.bfloat16)
    )
    proj = jnp.einsum("uce,ef->ucf", mixed, w_out, preferred_element_type=jnp.float32)
    cand_f = cands.astype(jnp.float32)
    logit = jnp.sum(proj * cand_f, axis=2) / root
    live_cand = (jnp.arange(num, dtype=jnp.int32)[None, :] < cand_counts[:, None]).astype(
        jnp.float32
    )
    grad_logit = (jax.nn.sigmoid(logit) - label) * live_cand / USERS_DEV
    grad_proj = (grad_logit[:, :, None] * cand_f / root).astype(jnp.bfloat16)
    grad_wo = jnp.einsum("uce,ucf->ef", mixed, grad_proj, preferred_element_type=jnp.float32)
    grad_mixed = jnp.einsum(
        "ucf,ef->uce", grad_proj, w_out, preferred_element_type=jnp.float32
    ).astype(jnp.bfloat16)
    g_heads = grad_mixed.reshape(users, num, HEADS, head_size)
    grad_probs = jnp.einsum("uchd,ulhd->uhcl", g_heads, v_heads, preferred_element_type=jnp.float32)
    inner = jnp.sum(probs * grad_probs, axis=-1, keepdims=True)
    grad_scores = (probs * (grad_probs - inner) * scale).astype(jnp.bfloat16)
    grad_query = (
        jnp.einsum("uhcl,ulhd->uchd", grad_scores, k_heads, preferred_element_type=jnp.float32)
        .reshape(users, num, width)
        .astype(jnp.bfloat16)
    )
    grad_keys = (
        jnp.einsum("uhcl,uchd->ulhd", grad_scores, q_heads, preferred_element_type=jnp.float32)
        .reshape(users, seq, width)
        .astype(jnp.bfloat16)
    )
    grad_values = (
        jnp.einsum("uhcl,uchd->ulhd", probs_b, g_heads, preferred_element_type=jnp.float32)
        .reshape(users, seq, width)
        .astype(jnp.bfloat16)
    )
    grad_wq = jnp.einsum("uce,ucf->ef", cands, grad_query, preferred_element_type=jnp.float32)
    grad_wk = jnp.einsum("ule,ulf->ef", rows, grad_keys, preferred_element_type=jnp.float32)
    grad_wv = jnp.einsum("ule,ulf->ef", rows, grad_values, preferred_element_type=jnp.float32)
    grad_rows = (
        jnp.einsum("ulf,ef->ule", grad_keys, w_key, preferred_element_type=jnp.float32)
        + jnp.einsum("ulf,ef->ule", grad_values, w_value, preferred_element_type=jnp.float32)
    ).astype(jnp.bfloat16)
    weight_grads = lax.psum(jnp.stack([grad_wq, grad_wk, grad_wv, grad_wo]), ("group", "peer"))
    outgoing = (
        jnp.zeros((shards * capacity, width), jnp.bfloat16)
        .at[position]
        .set(grad_rows.reshape(total, width))
    )
    outgoing = outgoing.reshape(shards, capacity, width)
    returned = lax.all_to_all(outgoing, ("group", "peer"), split_axis=0, concat_axis=0, tiled=True)
    table_sum = (
        jnp.zeros((table.shape[0], width), jnp.float32)
        .at[wanted.reshape(-1)]
        .add(returned.reshape(shards * capacity, width).astype(jnp.float32))
    )
    return (table_sum.astype(jnp.bfloat16), weight_grads)


def solution(mesh):
    in_specs = (
        P(("group", "peer"), None),
        P(("group", "peer"), None),
        P(("group", "peer")),
        P("group", "peer", None),
        P("group", "peer"),
        P(("group", "peer")),
        P(),
        P(),
        P(),
        P(),
    )
    out_specs = (P(("group", "peer"), None), P())
    return jax.shard_map(local, mesh=mesh, in_specs=in_specs, out_specs=out_specs, check_vma=False)
```

profile of v0, /device:TPU:0, one launch (start us, length us, event | category | flops | bytes accessed | tf_op | source)
XLA Modules:
  0.0 376.1 jit_solution(7502773527087919561)
XLA Ops:
  9.9 5.0 %sort.17 = (s32[2048]{0:T(1024)}, s32[2048]{0:T(1024)S(1)}) sort(s32[2048]{0:T(1024)S(1)} %get-tuple-element.44, s32[2048]{0:T(1024)S(1)} %iota.28), dimensions={0}, to_apply=%region_0.1 | sort | flops 22528 | bytes 32768 | tf_op jit(solution)/shard_map/jit(argsort)/sort | solution.py:16
  14.9 11.8 %gather_fusion = s32[2048]{0:T(1024)S(1)} fusion(s32[2048]{0:T(1024)S(1)} %get-tuple-element.44, s32[2048]{0:T(1024)S(1)} %get-tuple-element.42), kind=kCustom, calls=%fused_computation | custom fusion | bytes 24576 | tf_op jit(solution)/shard_map/gather | solution.py:17
  26.7 11.8 %gather_fusion.1 = s32[2048]{0:T(1024)S(1)} fusion(s32[2048]{0:T(1024)S(1)} %get-tuple-element.43, s32[2048]{0:T(1024)S(1)} %get-tuple-element.42), kind=kCustom, calls=%fused_computation.1 | custom fusion | bytes 24576 | tf_op jit(solution)/shard_map/gather | solution.py:24
  38.5 4.4 %compare_select_fusion.3 = (s32[2048,1]{0,1:T(1,128)S(1)}, s32[2048,1]{0,1:T(1,128)S(1)}) fusion(s32[]{:T(128)} %bitcast.27, s32[]{:T(128)} %bitcast.28, s32[]{:T(128)} %bitcast.29, s32[]{:T(128)} %bitcast.30, s32[]{:T(128)} %bitcast.31, s32[]{:T(128)} %bitcast.33, s32[]{:T(128)} %bitcast.32, s32[2048,1]{0,1:T(1,128)S(1)} %bitcast.175), kind=kLoop, calls=%fused_computation.89 | loop fusion | flops 30720 | bytes 24604 | tf_op jit(solution)/shard_map/gather | solution.py:21
  43.5 15.7 %subtract_add_fusion = (s32[2048]{0:T(1024)S(1)}, s32[2048]{0:T(1024)S(1)}) fusion(s32[2048]{0:T(1024)S(1)} %gather_fusion, pred[2048]{0:T(1024)(128)(4,1)S(1)} %get-tuple-element.34, pred[2048]{0:T(1024)(128)(4,1)S(1)} %get-tuple-element.33, pred[2048]{0:T(1024)(128)(4,1)S(1)} %get-tuple-element.32, pred[2048]{0:T(1024)(128)(4,1)S(1)} %get-tuple-element.31, ...), kind=kLoop, calls=%fused_computation.108 | loop fusion | flops 57344 | bytes 84068 | tf_op jit(solution)/shard_map/add | solution.py:22
  59.3 8.1 %scatter_custom_fusion = s32[3072]{0:T(1024)S(1)} fusion(s32[2048]{0:T(1024)S(1)} %bitcast.182, s32[2048]{0:T(1024)S(1)} %gather_fusion.1, s32[]{:T(128)} %constant.19.clone.1), kind=kCustom, calls=%fused_computation.111 | custom fusion | bytes 12292 | tf_op jit(solution)/shard_map/scatter | solution.py:24
  68.0 7.3 %all-to-all-start = ((s32[32,1,96]{2,1,0:T(1,128)}), s32[32,1,96]{2,1,0:T(1,128)S(1)}, u32[]{:S(2)}, u32[]{:S(2)}) async-start(s32[32,1,96]{2,1,0:T(1,128)} %all_to_all.35), calls=%async_computation | async-start | bytes 32768 | tf_op jit(solution)/shard_map/all_to_all | solution.py:40
  75.9 6.5 %all-to-all-done = s32[32,1,96]{2,1,0:T(1,128)S(1)} async-done(((s32[32,1,96]{2,1,0:T(1,128)}), s32[32,1,96]{2,1,0:T(1,128)S(1)}, u32[]{:S(2)}, u32[]{:S(2)}) %all-to-all-start) | async-done | bytes 12320 | tf_op jit(solution)/shard_map/all_to_all | solution.py:40
  82.4 3.2 all-to-all-start.3
  87.0 4.1 %all-to-all-done.3 = bf16[4,2,16]{2,1,0:T(2,128)(2,1)S(1)} async-done(((bf16[4,2,16]{2,1,0:T(2,128)(2,1)}), bf16[4,2,16]{2,1,0:T(2,128)(2,1)S(1)}, u32[]{:S(2)}, u32[]{:S(2)}) %all-to-all-start.3) | async-done | bytes 288 | tf_op jit(solution)/shard_map/all_to_all | solution.py:46
  91.1 3.3 all-to-all-start.1
  94.4 13.0 %gather_fusion.2 = bf16[3072,256]{1,0:T(8,128)(2,1)} fusion(bf16[4096,256]{1,0:T(8,128)(2,1)S(1)} %copy-done, s32[3072]{0:T(1024)S(1)} %broadcast_clamp_fusion), kind=kCustom, calls=%fused_computation.2 | custom fusion | bytes 3158016 | tf_op jit(solution)/shard_map/gather | solution.py:41
  107.5 4.3 %all-to-all-start.2 = ((bf16[32,96,256]{2,1,0:T(8,128)(2,1)}), bf16[32,96,256]{2,1,0:T(8,128)(2,1)}, u32[]{:S(2)}, u32[]{:S(2)}) async-start(bf16[32,96,256]{2,1,0:T(8,128)(2,1)} %bitcast.152), calls=%async_computation.2 | async-start | bytes 3145728 | tf_op jit(solution)/shard_map/all_to_all | solution.py:42
  111.8 8.2 %scatter_custom_fusion.1 = s32[2048]{0:T(1024)S(1)} fusion(s32[2048]{0:T(1024)S(1)} %get-tuple-element.41, s32[2048]{0:T(1024)S(1)} %get-tuple-element.35, s32[]{:T(128)} %constant.19.clone.1), kind=kCustom, calls=%fused_computation.116 | custom fusion | bytes 8196 | tf_op jit(solution)/shard_map/scatter | solution.py:23
  121.7 26.0 %all-to-all-done.2 = bf16[32,96,256]{2,1,0:T(8,128)(2,1)} async-done(((bf16[32,96,256]{2,1,0:T(8,128)(2,1)}), bf16[32,96,256]{2,1,0:T(8,128)(2,1)}, u32[]{:S(2)}, u32[]{:S(2)}) %all-to-all-start.2) | async-done | bytes 1572896 | tf_op jit(solution)/shard_map/all_to_all | solution.py:42
  147.7 8.3 %gather_fusion.3 = bf16[2048,256]{1,0:T(8,128)(2,1)S(1)} fusion(bf16[3072,256]{1,0:T(8,128)(2,1)} %bitcast.43, s32[2048]{0:T(1024)S(1)} %get-tuple-element.39), kind=kCustom, calls=%fused_computation.3 | custom fusion | bytes 2105344 | tf_op jit(solution)/shard_map/gather | solution.py:43
  157.5 1.5 convolution_convert_fusion.2
  159.0 3.4 fusion.63
  162.4 2.5 convolution_convert_fusion.3
  166.9 3.2 fusion.64
  170.1 1.5 convolution_convert_fusion
  171.7 7.1 %fusion.15 = bf16[2,4,64,1024]{3,2,1,0:T(8,128)(2,1)} fusion(bf16[2,64,4,64]{1,3,2,0:T(8,128)(2,1)} %bitcast.174, f32[2,4,64,1024]{3,2,1,0:T(8,128)} %fusion.64, f32[2,4,64,1024]{3,2,1,0:T(8,128)} %get-tuple-element.78, f32[2,4,64]{2,1,0:T(4,128)S(1)} %copy-done.15), kind=kOutput, calls=%fused_computation.22 | convolution fusion | flops 71304704 | bytes 5310464 | tf_op jit(solution)/shard_map/uhcl,uchd->ulhd/dot_general | solution.py:97
  178.7 1.8 fusion.37
  180.6 1.5 add_convert_fusion
  182.1 11.0 %scatter_custom_fusion.2 = bf16[3072,256]{1,0:T(8,128)(2,1)} fusion(s32[2048]{0:T(1024)} %get-tuple-element.40, bf16[2048,256]{1,0:T(8,128)(2,1)} %bitcast.166, bf16[]{:T(256)} %constant.49.clone.1), kind=kCustom, calls=%fused_computation.43 | custom fusion | bytes 1573376 | tf_op jit(solution)/shard_map/scatter | solution.py:117
  193.0 4.7 %all-to-all-start.4 = ((bf16[32,96,256]{2,1,0:T(8,128)(2,1)}), bf16[32,96,256]{2,1,0:T(8,128)(2,1)}, u32[]{:S(2)}, u32[]{:S(2)}) async-start(bf16[32,96,256]{2,1,0:T(8,128)(2,1)} %bitcast.151), calls=%async_computation.4 | async-start | bytes 3145728 | tf_op jit(solution)/shard_map/all_to_all | solution.py:120
  198.0 6.2 %fusion.18 = bf16[2,4,64,64]{3,2,1,0:T(8,128)(2,1)S(1)} fusion(bf16[2,1024,4,64]{1,3,2,0:T(8,128)(2,1)} %bitcast.165, f32[2,4,64,1024]{3,2,1,0:T(8,128)} %fusion.64, f32[2,4,64,1024]{3,2,1,0:T(8,128)} %get-tuple-element.78, f32[2,4,64]{2,1,0:T(4,128)S(1)} %copy-done.15), kind=kOutput, calls=%fused_computation.30 | convolution fusion | flops 70813184 | bytes 5310464 | tf_op jit(solution)/shard_map/uhcl,ulhd->uchd/dot_general | solution.py:92
  204.8 1.7 convolution_bitcast_fusion.3
  208.0 135.4 %all-reduce.2.cloned.1.call-done = f32[4,256,256]{1,2,0:T(8,128)} async-done(((f32[4,256,256]{1,2,0:T(8,128)}), f32[4,256,256]{1,2,0:T(8,128)}) %all-reduce.2.cloned.1.call-update) | async-done | bytes 1048592 | tf_op jit(solution)/shard_map/psum | solution.py:113
  343.4 2.5 copy.77
  345.9 19.6 %scatter_custom_fusion.3 = f32[4096,256]{1,0:T(8,128)} fusion(s32[3072]{0:T(1024)S(1)} %bitcast.178, bf16[3072,256]{1,0:T(8,128)(2,1)} %bitcast.78, f32[]{:T(128)} %constant.18.clone.1), kind=kCustom, calls=%fused_computation.10 | custom fusion | flops 1572864 | bytes 5767172 | tf_op jit(solution)/shard_map/scatter-add | solution.py:124
  365.5 3.7 convert_element_type.117
  (72 shorter events, 13.4 us)
Async XLA Ops:
  7.2 87.3 %copy-start = (bf16[4096,256]{1,0:T(8,128)(2,1)S(1)}, bf16[4096,256]{1,0:T(8,128)(2,1)}, u32[]{:S(2)}) copy-start(bf16[4096,256]{1,0:T(8,128)(2,1)} %param.10) | copy-start | bytes 6291460
  26.7 48.6 %copy-start.10 = (f32[8,16]{1,0:T(8,128)S(1)}, f32[8,16]{1,0:T(8,128)}, u32[]{:S(2)}) copy-start(f32[8,16]{1,0:T(8,128)} %param.14) | copy-start | bytes 1540
  68.0 14.4 %all-to-all-start = ((s32[32,1,96]{2,1,0:T(1,128)}), s32[32,1,96]{2,1,0:T(1,128)S(1)}, u32[]{:S(2)}, u32[]{:S(2)}) async-start(s32[32,1,96]{2,1,0:T(1,128)} %all_to_all.35), calls=%async_computation | async-start | bytes 32768 | tf_op jit(solution)/shard_map/all_to_all | solution.py:40
  82.4 8.7 %all-to-all-start.3 = ((bf16[4,2,16]{2,1,0:T(2,128)(2,1)}), bf16[4,2,16]{2,1,0:T(2,128)(2,1)S(1)}, u32[]{:S(2)}, u32[]{:S(2)}) async-start(bf16[4,2,16]{2,1,0:T(2,128)(2,1)} %bitcast.53), calls=%async_computation.3 | async-start | bytes 4096 | tf_op jit(solution)/shard_map/all_to_all | solution.py:46
  91.1 16.4 %all-to-all-start.1 = ((bf16[8,16,256]{2,1,0:T(8,128)(2,1)}), bf16[8,16,256]{2,1,0:T(8,128)(2,1)S(1)}, u32[]{:S(2)}, u32[]{:S(2)}) async-start(bf16[8,16,256]{2,1,0:T(8,128)(2,1)} %param.13), calls=%async_computation.1 | async-start | bytes 131072 | tf_op jit(solution)/shard_map/all_to_all | solution.py:45
  107.5 12.5 %copy-start.11 = (s32[2]{0:T(128)S(1)}, s32[2]{0:T(128)}, u32[]{:S(2)}) copy-start(s32[2]{0:T(128)} %param.12) | copy-start | bytes 28
  107.5 13.3 %copy-start.9 = (bf16[256,256]{1,0:T(8,128)(2,1)S(1)}, bf16[256,256]{1,0:T(8,128)(2,1)}, u32[]{:S(2)}) copy-start(bf16[256,256]{1,0:T(8,128)(2,1)} %param.16) | copy-start | bytes 393220
  107.5 40.2 %all-to-all-start.2 = ((bf16[32,96,256]{2,1,0:T(8,128)(2,1)}), bf16[32,96,256]{2,1,0:T(8,128)(2,1)}, u32[]{:S(2)}, u32[]{:S(2)}) async-start(bf16[32,96,256]{2,1,0:T(8,128)(2,1)} %bitcast.152), calls=%async_computation.2 | async-start | bytes 3145728 | tf_op jit(solution)/shard_map/all_to_all | solution.py:42
  147.7 8.3 %copy-start.4 = (bf16[256,256]{1,0:T(8,128)(2,1)S(1)}, bf16[256,256]{1,0:T(8,128)(2,1)}, u32[]{:S(2)}) copy-start(bf16[256,256]{1,0:T(8,128)(2,1)} %param.18) | copy-start | bytes 393220
  156.0 1.5 copy-start.3
  162.4 2.5 copy-start.14
  162.4 3.1 copy-start.8
  162.4 3.4 copy-start.12
  164.9 0.6 copy-start.5
  166.9 3.3 copy-start.7
  166.9 3.3 copy-start.13
  166.9 3.3 copy-start.15
  178.7 1.8 copy-start.1
  193.0 152.9 %all-to-all-start.4 = ((bf16[32,96,256]{2,1,0:T(8,128)(2,1)}), bf16[32,96,256]{2,1,0:T(8,128)(2,1)}, u32[]{:S(2)}, u32[]{:S(2)}) async-start(bf16[32,96,256]{2,1,0:T(8,128)(2,1)} %bitcast.151), calls=%async_computation.4 | async-start | bytes 3145728 | tf_op jit(solution)/shard_map/all_to_all | solution.py:120
  197.7 6.7 %copy-start.6 = (bf16[2,4,64,64]{3,2,1,0:T(8,128)(2,1)S(1)}, bf16[2,4,64,64]{3,2,1,0:T(8,128)(2,1)}, u32[]{:S(2)}) copy-start(bf16[2,4,64,64]{3,2,1,0:T(8,128)(2,1)} %copy-done.5) | copy-start | bytes 196612
  197.7 145.6 %all-reduce.2.cloned.1.call-start = ((), (), s32[]{:S(2)}) async-start(), calls=%async_computation.5 | async-start | bytes 2097152 | tf_op jit(solution)/shard_map/psum | solution.py:113
  204.2 2.2 copy-start.2
Sparse Core Ops, SparseCore 0:
  208.1 135.2 all-reduce.1
where the time goes:
time: 377 us; the launch traced here: 376 us
  waiting for transfers between devices  172 us (46%)
  local copies, waits for them, and re-layouts  79.8 us (21%)
  other arithmetic  53.3 us (14%)
  matrix products  33.4 us (9%)
  starting transfers between devices  23 us (6%)
  between operations  14.4 us (4%)
    psum x1, waiting for transfers between devices, local(): lax.psum(jnp.stack([grad_wq, grad_wk, grad_wv, grad_wo]), ('group', 'peer'))  135 us
    all_to_all x1, waiting for transfers between devices, local(): lax.all_to_all(served, ('group', 'peer'), split_axis=0, concat_axis=0, ti...  26 us
    scatter-add x1, other arithmetic, local(): table_sum = jnp.zeros((table.shape[0], width), jnp.float32).at[wanted.res...  19.6 us
    add x1, other arithmetic, bucket_plan(): slot_sorted = sorted_owner * capacity + rank  15.7 us
    gather x1, local copies, waits for them, and re-layouts, local(): served = table[wanted.reshape(-1)].reshape(shards, capacity, width)  13 us
    gather x1, local copies, waits for them, and re-layouts, bucket_plan(): local_row[order]  11.8 us
    gather x1, local copies, waits for them, and re-layouts, bucket_plan(): sorted_owner = owner[order]  11.8 us
    scatter x1, local copies, waits for them, and re-layouts, local(): outgoing = jnp.zeros((shards * capacity, width), jnp.bfloat16).at[positio...  11 us
  transfers between devices with their start and end apart: 6, of which 4 were waited for; matrix products, arithmetic and copies ran while one was open for 10% of the time, Pallas kernels for 0%

commit v1 on v0

v1 whole, which is shorter than its diff:
```python
import functools

import jax
import jax.numpy as jnp
from jax import lax
from jax.experimental import pallas as pl
from jax.experimental.pallas import tpu as pltpu
from jax.sharding import PartitionSpec as P

HEADS = 4
USERS_DEV = 2
ALL = ("group", "peer")
BF16 = jnp.bfloat16
F32 = jnp.float32
VMEM_LIMIT = 48 * 1024 * 1024


def nt(a, b):
    return lax.dot_general(a, b, (((1,), (1,)), ((), ())), preferred_element_type=F32)


def nn(a, b):
    return jnp.dot(a, b, preferred_element_type=F32)


def plan_kernel(rows_dev, lengths_ref, ids_ref, requests_ref, flags_ref):
    users, seq = ids_ref.shape
    shards, capacity = requests_ref.shape
    block = 256
    shift = rows_dev.bit_length() - 1
    before = (
        lax.broadcasted_iota(jnp.int32, (block, block), 0)
        < lax.broadcasted_iota(jnp.int32, (block, block), 1)
    ).astype(BF16)
    device = lax.broadcasted_iota(jnp.int32, (shards, block), 0)
    place = lax.broadcasted_iota(jnp.int32, (capacity, block), 0).astype(F32)
    lane = lax.broadcasted_iota(jnp.int32, (1, block), 1)
    count = jnp.zeros((shards, 1), F32)
    rows = jnp.zeros((2 * shards, capacity), F32)
    flags = jnp.zeros((capacity, shards), F32)
    for user in range(users):
        for start in range(0, seq, block):
            ids = ids_ref[user : user + 1, start : start + block]
            owner = lax.shift_right_logical(ids, shift)
            row = ids & (rows_dev - 1)
            live = lane + start < lengths_ref[user]
            owner = jnp.where(live, owner, shards)
            hot = (device == owner).astype(F32)
            hot_b = hot.astype(BF16)
            earlier = nn(hot_b, before) + count
            count = count + jnp.sum(hot, axis=1, keepdims=True)
            rank = jnp.sum(hot * earlier, axis=0, keepdims=True)
            ranked = (place == rank).astype(F32).astype(BF16)
            high = lax.shift_right_logical(row, 6).astype(F32)
            low = (row & 63).astype(F32)
            parts = jnp.concatenate([hot * high, hot * low], axis=0).astype(BF16)
            rows = rows + nt(parts, ranked)
            flags = flags + nt(ranked, (hot * float(user + 1)).astype(BF16))
    requests_ref[...] = (rows[:shards] * 64.0 + rows[shards:]).astype(jnp.int32)
    flags_ref[...] = flags


def plan(behaviour_ids, lengths, rows_dev, shards, capacity):
    return pl.pallas_call(
        functools.partial(plan_kernel, rows_dev),
        out_shape=(
            jax.ShapeDtypeStruct((shards, capacity), jnp.int32),
            jax.ShapeDtypeStruct((capacity, shards), F32),
        ),
        in_specs=[
            pl.BlockSpec(memory_space=pltpu.SMEM),
            pl.BlockSpec(memory_space=pltpu.VMEM),
        ],
        out_specs=(
            pl.BlockSpec(memory_space=pltpu.VMEM),
            pl.BlockSpec(memory_space=pltpu.VMEM),
        ),
        compiler_params=pltpu.CompilerParams(vmem_limit_bytes=VMEM_LIMIT),
        name="plan",
    )(lengths, behaviour_ids)


def gather_kernel(wanted_ref, table_ref, out_ref, wide, some):
    step = some.shape[0]
    wide[...] = table_ref[...].astype(F32)

    def body(t, carry):
        start = pl.multiple_of(t * step, step)
        for k in range(step):
            row = wanted_ref[start + k]
            some[pl.ds(k, 1), :] = wide[pl.ds(row, 1), :]
        out_ref[pl.ds(start, step), :] = some[...].astype(BF16)
        return carry

    lax.fori_loop(0, out_ref.shape[0] // step, body, 0)


def gather(wanted, table):
    slots = wanted.shape[0]
    width = table.shape[1]
    return pl.pallas_call(
        gather_kernel,
        out_shape=jax.ShapeDtypeStruct((slots, width), BF16),
        in_specs=[
            pl.BlockSpec(memory_space=pltpu.SMEM),
            pl.BlockSpec(memory_space=pltpu.VMEM),
        ],
        out_specs=pl.BlockSpec(memory_space=pltpu.VMEM),
        scratch_shapes=[pltpu.VMEM(table.shape, F32), pltpu.VMEM((64, width), F32)],
        compiler_params=pltpu.CompilerParams(vmem_limit_bytes=VMEM_LIMIT),
        name="gather_rows",
    )(wanted, table)


def scatter_kernel(wanted_ref, grads_ref, out_ref):
    tile = out_ref.shape[0]
    slots = grads_ref.shape[0]
    block = 256
    row = lax.broadcasted_iota(jnp.int32, (tile, block), 0) + pl.program_id(0) * tile
    total = jnp.zeros(out_ref.shape, F32)
    for start in range(0, slots, block):
        hot = (row == wanted_ref[:, start : start + block]).astype(F32).astype(BF16)
        total = total + nn(hot, grads_ref[start : start + block, :])
    out_ref[...] = total.astype(BF16)


def scatter(wanted, grads, rows_dev):
    slots, width = grads.shape
    tile = 512
    return pl.pallas_call(
        scatter_kernel,
        grid=(rows_dev // tile,),
        out_shape=jax.ShapeDtypeStruct((rows_dev, width), BF16),
        in_specs=[
            pl.BlockSpec((1, slots), lambda t: (0, 0)),
            pl.BlockSpec((slots, width), lambda t: (0, 0)),
        ],
        out_specs=pl.BlockSpec((tile, width), lambda t: (t, 0)),
        compiler_params=pltpu.CompilerParams(vmem_limit_bytes=VMEM_LIMIT),
        name="scatter_rows",
    )(wanted, grads)


def by_head(x):
    head_size = x.shape[1] // HEADS
    head = lax.broadcasted_iota(jnp.int32, x.shape, 1) // head_size
    return jnp.concatenate([jnp.where(head == h, x, 0.0) for h in range(HEADS)], axis=0)


def attend_kernel(
    num,
    counts_ref,
    rows_ref,
    flags_ref,
    cands_ref,
    label_ref,
    wq_ref,
    wk_ref,
    wv_ref,
    wo_ref,
    grad_rows_ref,
    weights_ref,
    turned,
    scores,
    expo,
):
    slots, width = rows_ref.shape
    capacity, shards = flags_ref.shape
    live = cands_ref.shape[0]
    users = live // num
    head_size = width // HEADS
    scale = float(head_size) ** (-0.5)
    root = float(width) ** 0.5
    cols = HEADS * live
    tile = 384
    tiles = range(0, slots, tile)
    per_tile = tile // capacity

    cands = cands_ref[...]
    cand_f = cands.astype(F32)
    wq, wk, wv, wo = wq_ref[...], wk_ref[...], wv_ref[...], wo_ref[...]
    query = by_head(nn(cands, wq).astype(BF16).astype(F32) * scale).astype(BF16)
    query_w = nt(query, wk).astype(BF16)

    user_of = lax.rem(lax.broadcasted_iota(jnp.int32, (1, cols), 1), live) // num + 1
    user_of = user_of.astype(F32)
    top = jnp.full((1, cols), -1e30, F32)
    for i, start in enumerate(tiles):
        rows = rows_ref[start : start + tile, :]
        turned[:, start : start + tile] = rows.T
        flag = jnp.concatenate(
            [flags_ref[:, o : o + 1] for o in range(i * per_tile, (i + 1) * per_tile)], axis=0
        )
        score = jnp.where(flag == user_of, nt(rows, query_w), -1e30)
        scores[start : start + tile, :] = score
        top = jnp.maximum(top, jnp.max(score, axis=0, keepdims=True))

    norm = jnp.zeros((1, cols), F32)
    rows_e = jnp.zeros((width, cols), F32)
    for start in tiles:
        e = jnp.exp(scores[start : start + tile, :] - top)
        norm = norm + jnp.sum(e, axis=0, keepdims=True)
        e = e.astype(BF16)
        expo[start : start + tile, :] = e
        rows_e = rows_e + nn(turned[:, start : start + tile], e)

    inv = 1.0 / norm
    rows_e = (rows_e * inv).astype(BF16)
    wv_t = wv.T
    mixed_t = jnp.concatenate(
        [
            nn(wv_t[h * head_size : (h + 1) * head_size, :], rows_e[:, h * live : (h + 1) * live])
            for h in range(HEADS)
        ],
        axis=0,
    )
    mixed_tb = mixed_t.astype(BF16)
    proj = nn(mixed_tb.T, wo)
    logit = jnp.sum(proj * cand_f, axis=1, keepdims=True) / root
    index = lax.broadcasted_iota(jnp.int32, (live, 1), 0)
    alive = jnp.zeros((live, 1), jnp.bool_)
    for user in range(users):
        alive = alive | ((index >= user * num) & (index < user * num + counts_ref[user]))
    grad_logit = jnp.where(alive, (jax.nn.sigmoid(logit) - label_ref[...]) / USERS_DEV, 0.0)
    grad_proj = (grad_logit * cand_f / root).astype(BF16)
    weights_ref[3 * width :, :] = nn(mixed_tb, grad_proj).astype(weights_ref.dtype)
    grad_mixed = nt(grad_proj, wo).astype(BF16).astype(F32)
    both = grad_mixed.T * mixed_t
    inner = jnp.concatenate(
        [
            jnp.sum(both[h * head_size : (h + 1) * head_size, :], axis=0, keepdims=True)
            for h in range(HEADS)
        ],
        axis=1,
    )
    inner = inner * inv
    inv_col = jnp.broadcast_to(inv, (128, cols)).T[:, :1]
    grad_heads = by_head(grad_mixed)
    grad_scaled = (grad_heads * inv_col).astype(BF16)
    grad_w = nt(grad_scaled, wv).astype(BF16)

    rows_s = jnp.zeros((width, cols), F32)
    for start in tiles:
        rows = rows_ref[start : start + tile, :]
        e = expo[start : start + tile, :]
        grad_score = (e.astype(F32) * (nt(rows, grad_w) - inner)).astype(BF16)
        rows_s = rows_s + nn(turned[:, start : start + tile], grad_score)
        grad_rows_ref[start : start + tile, :] = (
            nn(grad_score, query_w) + nn(e, grad_w)
        ).astype(BF16)

    rows_s = rows_s.astype(BF16)
    wk_t = wk.T
    grad_query_t = (
        jnp.concatenate(
            [
                nn(
                    wk_t[h * head_size : (h + 1) * head_size, :],
                    rows_s[:, h * live : (h + 1) * live],
                )
                for h in range(HEADS)
            ],
            axis=0,
        )
        * scale
    ).astype(BF16)
    weights_ref[:width, :] = nt(cands.T, grad_query_t).astype(weights_ref.dtype)
    weights_ref[width : 2 * width, :] = nn(rows_s, query).astype(weights_ref.dtype)
    weights_ref[2 * width : 3 * width, :] = nn(rows_e, grad_heads.astype(BF16)).astype(
        weights_ref.dtype
    )


def attend(rows, flags, cands, label, cand_counts, w_query, w_key, w_value, w_out):
    slots, width = rows.shape
    users, num, _ = cands.shape
    cols = HEADS * users * num
    vmem = pl.BlockSpec(memory_space=pltpu.VMEM)
    return pl.pallas_call(
        functools.partial(attend_kernel, num),
        out_shape=(
            jax.ShapeDtypeStruct((slots, width), BF16),
            jax.ShapeDtypeStruct((4 * width, width), BF16),
        ),
        in_specs=[pl.BlockSpec(memory_space=pltpu.SMEM)] + [vmem] * 8,
        out_specs=(vmem, vmem),
        scratch_shapes=[
            pltpu.VMEM((width, slots), BF16),
            pltpu.VMEM((slots, cols), F32),
            pltpu.VMEM((slots, cols), BF16),
        ],
        compiler_params=pltpu.CompilerParams(vmem_limit_bytes=VMEM_LIMIT),
        name="attend",
    )(
        cand_counts,
        rows,
        flags,
        cands.reshape(users * num, width),
        label.reshape(users * num, 1),
        w_query,
        w_key,
        w_value,
        w_out,
    )


def exchange(x):
    return lax.all_to_all(x, ALL, split_axis=0, concat_axis=0, tiled=True)


def local(
    table, behaviour_ids, lengths, candidates, labels, cand_counts, w_query, w_key, w_value, w_out
):
    shards = lax.axis_size(ALL)
    users, seq = behaviour_ids.shape
    rows_dev, width = table.shape
    total = users * seq
    capacity = total // shards + total // (2 * shards)
    slots = shards * capacity
    requests, flags = plan(behaviour_ids, lengths, rows_dev, shards, capacity)
    wanted = exchange(requests)
    served = gather(wanted.reshape(slots), table)
    arrived = exchange(served.reshape(shards, capacity, width)).reshape(slots, width)
    cands = lax.all_to_all(candidates, "peer", split_axis=0, concat_axis=1, tiled=True)
    label = lax.all_to_all(
        labels.astype(BF16), "peer", split_axis=0, concat_axis=1, tiled=True
    ).astype(F32)
    grad_rows, weights = attend(
        arrived, flags, cands, label, cand_counts, w_query, w_key, w_value, w_out
    )
    returned = exchange(grad_rows.reshape(shards, capacity, width)).reshape(slots, width)
    share = 4 * width // shards
    parts = exchange(weights.reshape(shards, share, width))
    part = jnp.sum(parts.astype(F32), axis=0).astype(BF16)
    weight_grads = exchange(jnp.broadcast_to(part[None], (shards, share, width)))
    table_grad = scatter(wanted.reshape(1, slots), returned, rows_dev)
    return table_grad, weight_grads.reshape(4, width, width).astype(F32)


def solution(mesh):
    in_specs = (
        P(ALL, None),
        P(ALL, None),
        P(ALL),
        P("group", "peer", None),
        P("group", "peer"),
        P(ALL),
        P(),
        P(),
        P(),
        P(),
    )
    out_specs = (P(ALL, None), P())
    return jax.shard_map(local, mesh=mesh, in_specs=in_specs, out_specs=out_specs, check_vma=False)
```

time: 377 us -> 176 us (0.47)
  waiting for transfers between devices: 172 us -> 71.6 us
  local copies, waits for them, and re-layouts: 79.8 us -> 3.79 us
  other arithmetic: 53.3 us -> 3.1 us
  blocking collectives: 0 us -> 47.9 us
  matrix products: 33.4 us -> 0 us
  Pallas kernels: 0 us -> 28.8 us
  between operations: 14.4 us -> 0.77 us
  starting transfers between devices: 23 us -> 17.9 us
    psum x1 -> x0, waiting for transfers between devices: 135 us -> none  [local(): lax.psum(jnp.stack([grad_wq, grad_wk, grad_wv, grad_wo]), ('group', 'peer'))]
    all_to_all x0 -> x3, blocking collectives: none -> 47.9 us  [exchange(): return lax.all_to_all(x, ALL, split_axis=0, concat_axis=0, tiled=True)]
    gather x6 -> x0, local copies, waits for them, and re-layouts: 46.3 us -> none  [the longest x1 13 us: local(): served = table[wanted.reshape(-1)].reshape(shards, capacity, width)]
    all_to_all x4 -> x3, waiting for transfers between devices: 36.6 us -> 71.6 us  [the longest x2 69.4 us: exchange(): return lax.all_to_all(x, ALL, split_axis=0, concat_axis=0, tiled=True)]
    dot_general x16 -> x0, matrix products: 30 us -> none  [the longest x1 7.07 us: local(): jnp.einsum('uhcl,uchd->ulhd', grad_scores, q_heads, preferred_element_typ...]
    pallas_call x0 -> x4, Pallas kernels: none -> 28.8 us  [the longest x1 10.2 us: attend(): pl.pallas_call(functools.partial(attend_kernel, num), out_shape=(jax.Shap...]
    scatter x3 -> x0, local copies, waits for them, and re-layouts: 27.3 us -> none  [the longest x1 11 us: local(): outgoing = jnp.zeros((shards * capacity, width), jnp.bfloat16).at[positio...]
    scatter-add x1 -> x0, other arithmetic: 19.6 us -> none  [local(): table_sum = jnp.zeros((table.shape[0], width), jnp.float32).at[wanted.res...]
  transfers between devices with their start and end apart: 6 -> 4, of which waited for: 4 -> 3; matrix products, arithmetic and copies ran while one was open for 10% -> 1% of each run, Pallas kernels for 0% -> 6%
where the time goes in v1:
time: 176 us; the launch traced here: 174 us
  waiting for transfers between devices  71.6 us (41%)
  blocking collectives  47.9 us (27%)
  Pallas kernels  28.8 us (16%)
  starting transfers between devices  17.9 us (10%)
  local copies, waits for them, and re-layouts  3.79 us (2%)
  other arithmetic  3.1 us (2%)
    all_to_all x2, waiting for transfers between devices, exchange(): return lax.all_to_all(x, ALL, split_axis=0, concat_axis=0, tiled=True)  69.4 us
    all_to_all x3, blocking collectives, exchange(): return lax.all_to_all(x, ALL, split_axis=0, concat_axis=0, tiled=True)  47.9 us
    pallas_call x1, Pallas kernels, attend(): pl.pallas_call(functools.partial(attend_kernel, num), out_shape=(jax.Shap...  10.2 us
    pallas_call x1, Pallas kernels, scatter(): pl.pallas_call(scatter_kernel, grid=(rows_dev // tile,), out_shape=jax.Sh...  8.59 us
    all_to_all x2, starting transfers between devices, exchange(): return lax.all_to_all(x, ALL, split_axis=0, concat_axis=0, tiled=True)  8.26 us
    pallas_call x1, Pallas kernels, gather(): pl.pallas_call(gather_kernel, out_shape=jax.ShapeDtypeStruct((slots, widt...  8.14 us
    all_to_all x1, starting transfers between devices, local(): lax.all_to_all(labels.astype(BF16), 'peer', split_axis=0, concat_axis=1,...  6.32 us
  transfers between devices with their start and end apart: 4, of which 3 were waited for; matrix products, arithmetic and copies ran while one was open for 1% of the time, Pallas kernels for 6%

profile of v1, /device:TPU:0, one launch (start us, length us, event | category | flops | bytes accessed | tf_op | source)
XLA Modules:
  0.0 173.8 jit_solution(4090942763562733301)
XLA Ops:
  0.6 1.3 convert_element_type.27
  1.9 6.3 %all-to-all-start.3 = ((bf16[4,2,16]{2,1,0:T(2,128)(2,1)}), bf16[4,2,16]{2,1,0:T(2,128)(2,1)S(1)}, u32[]{:S(2)}, u32[]{:S(2)}) async-start(bf16[4,2,16]{2,1,0:T(2,128)(2,1)} %bitcast.7), calls=%async_computation.3 | async-start | bytes 4096 | tf_op jit(solution)/shard_map/all_to_all | solution.py:325
  8.2 0.7 copy-done.5
  8.9 0.7 copy-done.7
  9.6 1.9 %plan.1 = (s32[32,96]{1,0:T(8,128)S(1)}, f32[96,32]{1,0:T(8,128)S(1)}) custom-call(s32[2]{0:T(128)S(1)} %copy-done.7, s32[2,1024]{1,0:T(2,128)S(1)} %copy-done.5), custom_call_target="tpu_custom_call" | custom-call | tf_op jit(solution)/shard_map/plan/pallas_call | solution.py:64
  11.5 2.2 %all-to-all-done.3 = bf16[4,2,16]{2,1,0:T(2,128)(2,1)S(1)} async-done(((bf16[4,2,16]{2,1,0:T(2,128)(2,1)}), bf16[4,2,16]{2,1,0:T(2,128)(2,1)S(1)}, u32[]{:S(2)}, u32[]{:S(2)}) %all-to-all-start.3) | async-done | bytes 288 | tf_op jit(solution)/shard_map/all_to_all | solution.py:325
  13.7 10.9 %all_to_all.57 = s32[32,1,96]{2,1,0:T(1,128)S(1)} all-to-all(s32[32,1,96]{2,1,0:T(1,128)S(1)} %bitcast.24), channel_id=1, replica_groups=mesh['group'=8,'peer'=4] {'group','peer'}, dimensions={0} | all-to-all | bytes 24576 | tf_op jit(solution)/shard_map/all_to_all | solution.py:308
  24.6 3.3 %all-to-all-start.2 = ((bf16[8,16,256]{2,1,0:T(8,128)(2,1)}), bf16[8,16,256]{2,1,0:T(8,128)(2,1)S(1)}, u32[]{:S(2)}, u32[]{:S(2)}) async-start(bf16[8,16,256]{2,1,0:T(8,128)(2,1)} %param.13), calls=%async_computation.2 | async-start | bytes 131072 | tf_op jit(solution)/shard_map/all_to_all | solution.py:324
  27.9 0.1 reshape.54.wanted_ref
  27.9 1.6 copy-done
  29.5 8.1 %gather_rows.1 = bf16[3072,256]{1,0:T(8,128)(2,1)} custom-call(s32[3072]{0:T(1024)S(1)} %reshape.54.wanted_ref, bf16[4096,256]{1,0:T(8,128)(2,1)S(1)} %copy-done), custom_call_target="tpu_custom_call" | custom-call | tf_op jit(solution)/shard_map/gather_rows/pallas_call | solution.py:101
  37.7 0.0 all-to-all-done.2
  37.7 0.0 copy-start.4
  37.7 0.0 copy-start.6
  37.7 4.2 %all-to-all-start.1 = ((bf16[32,96,256]{2,1,0:T(8,128)(2,1)}), bf16[32,96,256]{2,1,0:T(8,128)(2,1)S(1)}, u32[]{:S(2)}, u32[]{:S(2)}) async-start(bf16[32,96,256]{2,1,0:T(8,128)(2,1)} %bitcast.2), calls=%async_computation.1 | async-start | bytes 3145728 | tf_op jit(solution)/shard_map/all_to_all | solution.py:308
  41.9 0.1 reshape.63.label_ref
  42.0 35.8 %all-to-all-done.1 = bf16[32,96,256]{2,1,0:T(8,128)(2,1)S(1)} async-done(((bf16[32,96,256]{2,1,0:T(8,128)(2,1)}), bf16[32,96,256]{2,1,0:T(8,128)(2,1)S(1)}, u32[]{:S(2)}, u32[]{:S(2)}) %all-to-all-start.1) | async-done | bytes 1572896 | tf_op jit(solution)/shard_map/all_to_all | solution.py:308
  77.9 0.0 copy-done.1
  77.9 0.0 copy-done.4
  77.9 0.0 copy-done.6
  77.9 10.2 %attend.1 = (bf16[3072,256]{1,0:T(8,128)(2,1)}, bf16[1024,256]{1,0:T(8,128)(2,1)S(1)}) custom-call(s32[2]{0:T(128)S(1)} %copy-done.6, bf16[3072,256]{1,0:T(8,128)(2,1)S(1)} %bitcast.20, f32[96,32]{1,0:T(8,128)S(1)} %get-tuple-element.7.flags_ref, bf16[128,256]{1,0:T(8,128)(2,1)S(1)} %bitcast.23, f32[128,1]{1,0:T(8,128)S(1)} %reshape.63.label_ref, ...), custom_call_target="tpu_custom_call" | custom-call | tf_op jit(solution)/shard_map/attend/pallas_call | solution.py:279
  88.1 18.7 %all_to_all.58 = bf16[32,32,256]{2,1,0:T(8,128)(2,1)S(1)} all-to-all(bf16[32,32,256]{2,1,0:T(8,128)(2,1)S(1)} %bitcast.22), channel_id=1, replica_groups=mesh['group'=8,'peer'=4] {'group','peer'}, dimensions={0} | all-to-all | bytes 1048576 | tf_op jit(solution)/shard_map/all_to_all | solution.py:308
  106.8 0.1 reduce_sum.12
  106.9 0.1 broadcast_in_dim.2
  107.0 18.3 %all_to_all.59 = bf16[32,32,256]{2,1,0:T(8,128)(2,1)S(1)} all-to-all(bf16[32,32,256]{2,1,0:T(8,128)(2,1)S(1)} %broadcast_in_dim.2), channel_id=1, replica_groups=mesh['group'=8,'peer'=4] {'group','peer'}, dimensions={0} | all-to-all | bytes 1048576 | tf_op jit(solution)/shard_map/all_to_all | solution.py:308
  125.2 4.1 %all-to-all-start.4 = ((bf16[32,96,256]{2,1,0:T(8,128)(2,1)}), bf16[32,96,256]{2,1,0:T(8,128)(2,1)S(1)}, u32[]{:S(2)}, u32[]{:S(2)}) async-start(bf16[32,96,256]{2,1,0:T(8,128)(2,1)} %bitcast.9), calls=%async_computation.4 | async-start | bytes 3145728 | tf_op jit(solution)/shard_map/all_to_all | solution.py:308
  129.3 0.5 broadcast.6
  129.8 0.7 reduce.6
  130.5 0.1 reshape.53.wanted_ref
  130.6 1.1 bitcast_convert_fusion
  131.7 33.6 %all-to-all-done.4 = bf16[32,96,256]{2,1,0:T(8,128)(2,1)S(1)} async-done(((bf16[32,96,256]{2,1,0:T(8,128)(2,1)}), bf16[32,96,256]{2,1,0:T(8,128)(2,1)S(1)}, u32[]{:S(2)}, u32[]{:S(2)}) %all-to-all-start.4) | async-done | bytes 1572896 | tf_op jit(solution)/shard_map/all_to_all | solution.py:308
  165.2 8.6 %scatter_rows.1 = bf16[4096,256]{1,0:T(8,128)(2,1)} custom-call(s32[1,3072]{1,0:T(1,128)S(1)} %reshape.53.wanted_ref, bf16[3072,256]{1,0:T(8,128)(2,1)S(1)} %bitcast.21), custom_call_target="tpu_custom_call" | custom-call | tf_op jit(solution)/shard_map/scatter_rows/pallas_call | solution.py:130
  (11 shorter events, 0.0 us)
Async XLA Ops:
  1.9 11.8 %all-to-all-start.3 = ((bf16[4,2,16]{2,1,0:T(2,128)(2,1)}), bf16[4,2,16]{2,1,0:T(2,128)(2,1)S(1)}, u32[]{:S(2)}, u32[]{:S(2)}) async-start(bf16[4,2,16]{2,1,0:T(2,128)(2,1)} %bitcast.7), calls=%async_computation.3 | async-start | bytes 4096 | tf_op jit(solution)/shard_map/all_to_all | solution.py:325
  8.2 0.7 copy-start.5
  8.9 0.7 copy-start.7
  24.6 13.1 %all-to-all-start.2 = ((bf16[8,16,256]{2,1,0:T(8,128)(2,1)}), bf16[8,16,256]{2,1,0:T(8,128)(2,1)S(1)}, u32[]{:S(2)}, u32[]{:S(2)}) async-start(bf16[8,16,256]{2,1,0:T(8,128)(2,1)} %param.13), calls=%async_computation.2 | async-start | bytes 131072 | tf_op jit(solution)/shard_map/all_to_all | solution.py:324
  27.9 1.6 copy-start
  37.7 40.2 %copy-start.1 = (bf16[256,256]{1,0:T(8,128)(2,1)S(1)}, bf16[256,256]{1,0:T(8,128)(2,1)}, u32[]{:S(2)}) copy-start(bf16[256,256]{1,0:T(8,128)(2,1)} %wq_ref.1) | copy-start | bytes 393220
  37.7 40.2 %copy-start.2 = (bf16[256,256]{1,0:T(8,128)(2,1)S(1)}, bf16[256,256]{1,0:T(8,128)(2,1)}, u32[]{:S(2)}) copy-start(bf16[256,256]{1,0:T(8,128)(2,1)} %wk_ref.1) | copy-start | bytes 393220
  37.7 40.2 %copy-start.3 = (bf16[256,256]{1,0:T(8,128)(2,1)S(1)}, bf16[256,256]{1,0:T(8,128)(2,1)}, u32[]{:S(2)}) copy-start(bf16[256,256]{1,0:T(8,128)(2,1)} %wv_ref.1) | copy-start | bytes 393220
  37.7 40.2 %copy-start.4 = (bf16[256,256]{1,0:T(8,128)(2,1)S(1)}, bf16[256,256]{1,0:T(8,128)(2,1)}, u32[]{:S(2)}) copy-start(bf16[256,256]{1,0:T(8,128)(2,1)} %wo_ref.1) | copy-start | bytes 393220
  37.7 40.2 %copy-start.6 = (s32[2]{0:T(128)S(1)}, s32[2]{0:T(128)}, u32[]{:S(2)}) copy-start(s32[2]{0:T(128)} %counts_ref.1) | copy-start | bytes 28
  37.7 40.1 %all-to-all-start.1 = ((bf16[32,96,256]{2,1,0:T(8,128)(2,1)}), bf16[32,96,256]{2,1,0:T(8,128)(2,1)S(1)}, u32[]{:S(2)}, u32[]{:S(2)}) async-start(bf16[32,96,256]{2,1,0:T(8,128)(2,1)} %bitcast.2), calls=%async_computation.1 | async-start | bytes 3145728 | tf_op jit(solution)/shard_map/all_to_all | solution.py:308
  125.2 40.0 %all-to-all-start.4 = ((bf16[32,96,256]{2,1,0:T(8,128)(2,1)}), bf16[32,96,256]{2,1,0:T(8,128)(2,1)S(1)}, u32[]{:S(2)}, u32[]{:S(2)}) async-start(bf16[32,96,256]{2,1,0:T(8,128)(2,1)} %bitcast.9), calls=%async_computation.4 | async-start | bytes 3145728 | tf_op jit(solution)/shard_map/all_to_all | solution.py:308

commit v2 on v1

v2 whole, which is shorter than its diff:
```python
import functools
import math

import jax
import jax.numpy as jnp
from jax import lax
from jax.experimental import pallas as pl
from jax.experimental.pallas import tpu as pltpu
from jax.sharding import Mesh
from jax.sharding import PartitionSpec as P

HEADS = 4
USERS_DEV = 2
ALL = ("group", "hi", "lo")
BY_HALF = ("hi", "group", "lo")
HALF = ("group", "lo")
PEERS = ("hi", "lo")
BF16 = jnp.bfloat16
F32 = jnp.float32
VMEM_LIMIT = 12 * 1024 * 1024
LOWEST = -1e30
LINE = 8


def nt(a, b):
    return lax.dot_general(a, b, (((1,), (1,)), ((), ())), preferred_element_type=F32)


def nn(a, b):
    return jnp.dot(a, b, preferred_element_type=F32)


def cost(flops, transcendentals):
    return pl.CostEstimate(flops=flops, bytes_accessed=0, transcendentals=transcendentals)


def log2(n):
    return n.bit_length() - 1


def plan_kernel(
    rows_dev,
    sizes,
    lengths_hbm,
    counts_hbm,
    ids_hbm,
    cands_hbm,
    labels_hbm,
    requests_ref,
    flags_ref,
    labelled_ref,
    lengths_ref,
    counts_ref,
    ids_ref,
    cands_ref,
    labels_ref,
    sems,
):
    copies = [
        pltpu.make_async_copy(source, target, sems.at[k])
        for k, (source, target) in enumerate(
            (
                (lengths_hbm, lengths_ref),
                (counts_hbm, counts_ref),
                (ids_hbm, ids_ref),
                (cands_hbm, cands_ref),
                (labels_hbm, labels_ref),
            )
        )
    ]
    for copy in copies:
        copy.start()
    for copy in copies:
        copy.wait()
    groups, low = sizes
    users, seq = ids_ref.shape
    shards = requests_ref.shape[0]
    capacity = requests_ref.shape[1] - LINE
    half = shards // 2
    block = 256
    before = (
        lax.broadcasted_iota(jnp.int32, (block, block), 0)
        < lax.broadcasted_iota(jnp.int32, (block, block), 1)
    ).astype(BF16)
    device = lax.broadcasted_iota(jnp.int32, (shards, block), 0)
    place = lax.broadcasted_iota(jnp.int32, (capacity, block), 0).astype(F32)
    lane = lax.broadcasted_iota(jnp.int32, (1, block), 1)
    count = jnp.zeros((shards, 1), F32)
    rows = jnp.zeros((2 * shards, capacity), F32)
    flags = jnp.zeros((capacity, shards), F32)
    for user in range(users):
        for start in range(0, seq, block):
            ids = ids_ref[user : user + 1, start : start + block]
            owner = lax.shift_right_logical(ids, log2(rows_dev))
            row = ids & (rows_dev - 1)
            group = lax.shift_right_logical(owner, log2(2 * low))
            high = lax.shift_right_logical(owner, log2(low)) & 1
            owner = high * half + group * low + (owner & (low - 1))
            live = lane + start < lengths_ref[user]
            owner = jnp.where(live, owner, shards)
            hot = (device == owner).astype(F32)
            hot_b = hot.astype(BF16)
            earlier = nn(hot_b, before) + count
            count = count + jnp.sum(hot, axis=1, keepdims=True)
            rank = jnp.sum(hot * earlier, axis=0, keepdims=True)
            ranked = (place == rank).astype(F32).astype(BF16)
            upper = lax.shift_right_logical(row, 6).astype(F32)
            lower = (row & 63).astype(F32)
            parts = jnp.concatenate([hot * upper, hot * lower], axis=0).astype(BF16)
            rows = rows + nt(parts, ranked)
            flags = flags + nt(ranked, (hot * float(user + 1)).astype(BF16))
    requests = jnp.concatenate(
        [rows[:shards] * 64.0 + rows[shards:], jnp.broadcast_to(count, (shards, LINE))], axis=1
    )
    requests_ref[...] = requests.astype(jnp.int32)
    below = lax.broadcasted_iota(jnp.int32, (8, half), 0)
    counts = jnp.zeros((8, half), F32)
    for user in range(users):
        counts = jnp.where(below == user, counts_ref[user].astype(F32), counts)
    for h in range(2):
        flags_ref[h, :capacity, :] = flags[:, h * half : (h + 1) * half]
        flags_ref[h, capacity:, :] = counts
    _, held, width = cands_ref.shape
    square = lax.broadcasted_iota(jnp.int32, (held, held), 0)
    square = square == lax.broadcasted_iota(jnp.int32, (held, held), 1)
    lane = lax.broadcasted_iota(jnp.int32, (held, 128), 1)
    for user in range(cands_ref.shape[0]):
        label = jnp.sum(
            jnp.where(square, labels_ref[user : user + 1, :], 0.0), axis=1, keepdims=True
        )
        labelled_ref[user, :, :width] = cands_ref[user]
        labelled_ref[user, :, width:] = jnp.where(lane == 0, label, 0.0).astype(BF16)


def plan(behaviour_ids, lengths, cand_counts, candidates, labels, rows_dev, sizes, capacity):
    half = sizes[0] * sizes[1]
    vmem = pl.BlockSpec(memory_space=pltpu.VMEM)
    operands = (lengths, cand_counts, behaviour_ids, candidates, labels)
    return pl.pallas_call(
        functools.partial(plan_kernel, rows_dev, sizes),
        out_shape=(
            jax.ShapeDtypeStruct((2 * half, capacity + LINE), jnp.int32),
            jax.ShapeDtypeStruct((2, capacity + 8, half), F32),
            jax.ShapeDtypeStruct(candidates.shape[:2] + (candidates.shape[2] + 128,), BF16),
        ),
        in_specs=[pl.BlockSpec(memory_space=pltpu.HBM)] * 5,
        out_specs=(vmem,) * 3,
        scratch_shapes=[
            pltpu.SMEM(lengths.shape, jnp.int32),
            pltpu.SMEM(cand_counts.shape, jnp.int32),
            pltpu.VMEM(behaviour_ids.shape, jnp.int32),
            pltpu.VMEM(candidates.shape, BF16),
            pltpu.VMEM(labels.shape, F32),
            pltpu.SemaphoreType.DMA((5,)),
        ],
        compiler_params=pltpu.CompilerParams(vmem_limit_bytes=VMEM_LIMIT),
        name="plan",
    )(*(pltpu.with_memory_space_constraint(x, pltpu.HBM) for x in operands))


def gather_kernel(blocks, wanted_ref, table_hbm, out_hbm, narrow, wide, out, in_sems, out_sems):
    slots = out.shape[0]
    capacity = slots // blocks
    line = capacity + LINE
    joint = 1 if capacity % 16 == 0 else math.lcm(capacity, 16) // capacity
    step = 16 if joint == 1 else joint * capacity
    loads = in_sems.shape[0]
    size = narrow.shape[0] // loads
    copies = []
    for k in range(loads):
        part = pl.ds(k * size, size)
        copies.append(pltpu.make_async_copy(table_hbm.at[part], narrow.at[part], in_sems.at[k]))
        copies[-1].start()
    out[...] = jnp.zeros(out.shape, BF16)
    for k, copy in enumerate(copies):
        copy.wait()
        part = slice(k * size, (k + 1) * size)
        wide[part, :] = narrow[part, :].astype(F32)

    def bucket(b, carry):
        first = b * joint * line

        def fetch(c, carry):
            at = c * step
            start = pl.multiple_of(b * joint * capacity + at, 16)
            for k in range(0, step, 16):
                rows = [
                    wide[pl.ds(wanted_ref[first + at + n + n // capacity * LINE], 1), :]
                    for n in range(k, k + 16)
                ]
                out[pl.ds(start + k, 16), :] = jnp.concatenate(rows, axis=0).astype(BF16)
            return carry

        steps = 1 if joint > 1 else lax.div(wanted_ref[first + capacity] + step - 1, step)
        return lax.fori_loop(0, steps, fetch, carry)

    copies = []
    groups = out_sems.shape[0]
    each = blocks // joint // groups
    for g in range(groups):
        lax.fori_loop(g * each, (g + 1) * each, bucket, 0)
        part = pl.ds(g * each * joint * capacity, each * joint * capacity)
        copies.append(pltpu.make_async_copy(out.at[part], out_hbm.at[part], out_sems.at[g]))
        copies[-1].start()
    for copy in copies:
        copy.wait()


def gather(wanted, table, blocks):
    width = table.shape[1]
    slots = wanted.shape[0] - blocks * LINE
    return pl.pallas_call(
        functools.partial(gather_kernel, blocks),
        out_shape=jax.ShapeDtypeStruct((slots, width), BF16),
        in_specs=[
            pl.BlockSpec(memory_space=pltpu.SMEM),
            pl.BlockSpec(memory_space=pltpu.HBM),
        ],
        out_specs=pl.BlockSpec(memory_space=pltpu.HBM),
        scratch_shapes=[
            pltpu.VMEM(table.shape, BF16),
            pltpu.VMEM(table.shape, F32),
            pltpu.VMEM((slots, width), BF16),
            pltpu.SemaphoreType.DMA((8,)),
            pltpu.SemaphoreType.DMA((4,)),
        ],
        compiler_params=pltpu.CompilerParams(vmem_limit_bytes=VMEM_LIMIT),
        name="gather_rows",
    )(wanted, pltpu.with_memory_space_constraint(table, pltpu.HBM))


def scatter_kernel(wanted_ref, returned_ref, out_ref, grads):
    tile = out_ref.shape[0]
    slots = grads.shape[0]
    blocks = returned_ref.shape[0]
    each = slots // blocks
    block = 256

    @pl.when(pl.program_id(0) == 0)
    def _():
        for b in range(blocks):
            grads[b * each : (b + 1) * each, :] = returned_ref[b, :each, :]

    row = lax.broadcasted_iota(jnp.int32, (tile, block), 0) + pl.program_id(0) * tile
    total = jnp.zeros(out_ref.shape, F32)
    for start in range(0, slots, block):
        hot = (row == wanted_ref[:, start : start + block]).astype(F32).astype(BF16)
        total = total + nn(hot, grads[start : start + block, :])
    out_ref[...] = total.astype(BF16)


def scatter(wanted, returned, rows_dev):
    slots = wanted.shape[1]
    width = returned.shape[-1]
    tile = 512
    return pl.pallas_call(
        scatter_kernel,
        grid=(rows_dev // tile,),
        out_shape=jax.ShapeDtypeStruct((rows_dev, width), BF16),
        in_specs=[
            pl.BlockSpec((1, slots), lambda t: (0, 0)),
            pl.BlockSpec(returned.shape, lambda t: (0, 0, 0)),
        ],
        out_specs=pl.BlockSpec((tile, width), lambda t: (t, 0)),
        scratch_shapes=[pltpu.VMEM((slots, width), BF16)],
        compiler_params=pltpu.CompilerParams(vmem_limit_bytes=VMEM_LIMIT),
        name="scatter_rows",
    )(wanted, returned)


def by_head(x):
    head_size = x.shape[1] // HEADS
    head = lax.broadcasted_iota(jnp.int32, x.shape, 1) // head_size
    return jnp.concatenate([jnp.where(head == h, x, 0.0) for h in range(HEADS)], axis=0)


def head_blocks(a_t, b, live):
    size = a_t.shape[0] // HEADS
    return jnp.concatenate(
        [nn(a_t[h * size : (h + 1) * size, :], b[:, h * live : (h + 1) * live]) for h in range(HEADS)],
        axis=0,
    )


def pieces(x):
    a = x.astype(BF16)
    x = x - a.astype(F32)
    b = x.astype(BF16)
    return [a, b, (x - b.astype(F32)).astype(BF16)]


def stacked(x, live):
    return jnp.concatenate([x[:, h * live : (h + 1) * live] for h in range(HEADS)], axis=0)


def flat(x):
    return jnp.concatenate([x[h : h + 1, :] for h in range(HEADS)], axis=1)


def query_kernel(cands_ref, wq_ref, wk_ref, query_ref, query_w_ref):
    width = wq_ref.shape[0]
    live = cands_ref.shape[1]
    scale = float(width // HEADS) ** (-0.5)
    cands = jnp.concatenate([cands_ref[r, :, :width] for r in range(2)], axis=0)
    query = nn(cands, wq_ref[...]).astype(BF16).astype(F32) * scale
    for r in range(2):
        heads = by_head(query[r * live : (r + 1) * live]).astype(BF16)
        query_ref[r] = heads
        query_w_ref[r] = nt(heads, wk_ref[...]).astype(BF16)


def queries(cands, w_query, w_key):
    width = w_query.shape[0]
    shape = jax.ShapeDtypeStruct((2, HEADS * cands.shape[1], width), BF16)
    vmem = pl.BlockSpec(memory_space=pltpu.VMEM)
    return pl.pallas_call(
        query_kernel,
        out_shape=(shape, shape),
        in_specs=[vmem] * 3,
        out_specs=(vmem, vmem),
        compiler_params=pltpu.CompilerParams(vmem_limit_bytes=VMEM_LIMIT),
        name="queries",
    )(cands, w_query, w_key)


def take_tile(rows_ref, r, t, per_tile, capacity):
    return jnp.concatenate(
        [
            rows_ref[b, r * capacity : (r + 1) * capacity, :]
            for b in range(t * per_tile, (t + 1) * per_tile)
        ],
        axis=0,
    )


TILE = 384


def forward_kernel(
    r, num, rows_ref, flags_ref, query_w_ref, wv_ref, expo_ref, part_ref, mean_ref, turned_ref, scores
):
    blocks, both, width = rows_ref.shape
    capacity = both // 2
    cols = query_w_ref.shape[1]
    live = cols // HEADS
    per_tile = TILE // capacity
    tiles = blocks // per_tile
    user_of = lax.rem(lax.broadcasted_iota(jnp.int32, (1, cols), 1), live) // num + 1
    user_of = user_of.astype(F32)
    query_w = query_w_ref[r]
    top = jnp.full((1, cols), LOWEST, F32)
    for t in range(tiles):
        rows = take_tile(rows_ref, r, t, per_tile, capacity)
        turned_ref[:, t * TILE : (t + 1) * TILE] = rows.T
        flag = jnp.concatenate(
            [flags_ref[r, :capacity, o : o + 1] for o in range(t * per_tile, (t + 1) * per_tile)],
            axis=0,
        )
        score = jnp.where(flag == user_of, nt(rows, query_w), LOWEST)
        scores[t * TILE : (t + 1) * TILE, :] = score
        top = jnp.maximum(top, jnp.max(score, axis=0, keepdims=True))
    norm = jnp.zeros((1, cols), F32)
    rows_e = jnp.zeros((width, cols), F32)
    for t in range(tiles):
        e = jnp.exp(scores[t * TILE : (t + 1) * TILE, :] - top)
        norm = norm + jnp.sum(e, axis=0, keepdims=True)
        e = e.astype(BF16)
        expo_ref[t * TILE : (t + 1) * TILE, :] = e
        rows_e = rows_e + nn(turned_ref[:, t * TILE : (t + 1) * TILE], e)
    mean = (rows_e * (1.0 / norm)).astype(BF16)
    mean_ref[...] = mean
    part_ref[:width, :] = head_blocks(wv_ref[...].T, mean, live).astype(BF16)
    rest = pieces(stacked(top, live)) + pieces(stacked(norm, live))
    rest.append(jnp.zeros((8, live), BF16))
    part_ref[width:, :] = jnp.concatenate([x.astype(F32) for x in rest], axis=0).astype(BF16)


def forward(r, rows, flags, query_w, num, w_value):
    blocks, both, width = rows.shape
    cols = query_w.shape[1]
    slots = blocks * both // 2
    vmem = pl.BlockSpec(memory_space=pltpu.VMEM)
    return pl.pallas_call(
        functools.partial(forward_kernel, r, num),
        out_shape=(
            jax.ShapeDtypeStruct((slots, cols), BF16),
            jax.ShapeDtypeStruct((width + 32, cols // HEADS), BF16),
            jax.ShapeDtypeStruct((width, cols), BF16),
            jax.ShapeDtypeStruct((width, slots), BF16),
        ),
        in_specs=[vmem] * 4,
        out_specs=(vmem,) * 4,
        scratch_shapes=[pltpu.VMEM((slots, cols), F32)],
        compiler_params=pltpu.CompilerParams(vmem_limit_bytes=VMEM_LIMIT),
        cost_estimate=cost(4 * slots * width * cols, slots * cols),
        name="forward",
    )(rows, flags, query_w, w_value)


def opened(part_ref, width):
    rest = part_ref[width:, :].astype(F32)
    top = rest[0:4] + rest[4:8] + rest[8:12]
    norm = rest[12:16] + rest[16:20] + rest[20:24]
    return part_ref[:width, :].astype(F32), top, norm


def backward_kernel(
    r,
    users,
    rows_ref,
    flags_ref,
    cands_ref,
    place_ref,
    query_ref,
    query_w_ref,
    wk_ref,
    wv_ref,
    wo_ref,
    expo_ref,
    own_ref,
    other_ref,
    mean_ref,
    turned_ref,
    *refs,
):
    if r == 0:
        out_ref, weights = refs
    else:
        first_ref, first_weights, out_ref, weights = refs
    blocks, both, width = rows_ref.shape
    capacity = both // 2
    live = cands_ref.shape[1]
    num = live // users
    cols = HEADS * live
    head_size = width // HEADS
    scale = float(head_size) ** (-0.5)
    root = float(width) ** 0.5
    per_tile = TILE // capacity
    tiles = blocks // per_tile
    wv, wo = wv_ref[...], wo_ref[...]

    mixed_own, top_own, norm_own = opened(own_ref, width)
    mixed_other, top_other, norm_other = opened(other_ref, width)
    top = jnp.maximum(top_own, top_other)
    factor = jnp.exp(top_own - top)
    part_own = norm_own * factor
    part_other = norm_other * jnp.exp(top_other - top)
    inv = 1.0 / (part_own + part_other)
    factor = factor * inv
    part_own = part_own * inv
    part_other = part_other * inv
    mixed_t = jnp.concatenate(
        [
            mixed_own[h * head_size : (h + 1) * head_size] * part_own[h : h + 1]
            + mixed_other[h * head_size : (h + 1) * head_size] * part_other[h : h + 1]
            for h in range(HEADS)
        ],
        axis=0,
    )
    mixed_tb = mixed_t.astype(BF16)
    cands = cands_ref[r, :, :width]
    cand_f = cands.astype(F32)
    proj = nn(mixed_tb.T, wo)
    logit = jnp.sum(proj * cand_f, axis=1, keepdims=True) / root
    label = cands_ref[r, :, width:].astype(F32)[:, 0:1]
    index = lax.broadcasted_iota(jnp.int32, (live, 1), 0)
    limit = jnp.zeros((live, 1), F32)
    for user in range(users):
        count = flags_ref[r, capacity + user : capacity + user + 1, 0:1]
        limit = jnp.where(index >= user * num, count, limit)
    alive = place_ref[...] < limit
    grad_logit = jnp.where(alive, (jax.nn.sigmoid(logit) - label) / USERS_DEV, 0.0)
    grad_proj = (grad_logit * cand_f / root).astype(BF16)
    grad_mixed = nt(grad_proj, wo).astype(BF16).astype(F32)
    joint = grad_mixed.T * mixed_t
    inner = jnp.concatenate(
        [
            jnp.sum(joint[h * head_size : (h + 1) * head_size, :], axis=0, keepdims=True)
            for h in range(HEADS)
        ],
        axis=0,
    )
    inner = flat(inner * factor)
    factor = flat(factor)
    factor_col = jnp.broadcast_to(factor, (128, cols)).T[:, :1]
    grad_heads = by_head(grad_mixed)
    grad_w = nt((grad_heads * factor_col).astype(BF16), wv).astype(BF16)

    query_w = query_w_ref[r]
    rows_s = jnp.zeros((width, cols), F32)
    for t in range(tiles):
        rows = take_tile(rows_ref, r, t, per_tile, capacity)
        e = expo_ref[t * TILE : (t + 1) * TILE, :]
        grad_score = (e.astype(F32) * (nt(rows, grad_w) - inner)).astype(BF16)
        rows_s = rows_s + nn(turned_ref[:, t * TILE : (t + 1) * TILE], grad_score)
        grad_rows = (nn(grad_score, query_w) + nn(e, grad_w)).astype(BF16)
        for k in range(per_tile):
            out_ref[t * per_tile + k, r * capacity : (r + 1) * capacity, :] = grad_rows[
                k * capacity : (k + 1) * capacity, :
            ]

    rows_s = rows_s.astype(BF16)
    grad_query_t = (head_blocks(wk_ref[...].T, rows_s, live) * scale).astype(BF16)
    share = flat(part_own)
    parts = (
        nt(cands.T, grad_query_t),
        nn(rows_s, query_ref[r]),
        nn((mean_ref[...].astype(F32) * share).astype(BF16), grad_heads.astype(BF16)),
        nn(mixed_tb, grad_proj) * 0.5,
    )
    for k, part in enumerate(parts):
        if r == 0:
            weights[k * width : (k + 1) * width, :] = part
        else:
            weights[k * width : (k + 1) * width, :] = (
                first_weights[k * width : (k + 1) * width, :] + part
            )
    if r == 1:
        rows_each = 4 * width // blocks
        for b in range(blocks):
            out_ref[b, :capacity, :] = first_ref[b]
            out_ref[b, both:, :] = weights[b * rows_each : (b + 1) * rows_each, :].astype(BF16)


def backward(r, users, rows, *operands):
    blocks, both, width = rows.shape
    vmem = pl.BlockSpec(memory_space=pltpu.VMEM)
    weights = jax.ShapeDtypeStruct((4 * width, width), F32)
    if r == 0:
        out_shape = (jax.ShapeDtypeStruct((blocks, both // 2, width), BF16), weights)
        scratch_shapes = []
    else:
        out_shape = jax.ShapeDtypeStruct((blocks, both + 4 * width // blocks, width), BF16)
        scratch_shapes = [pltpu.VMEM(weights.shape, F32)]
    return pl.pallas_call(
        functools.partial(backward_kernel, r, users),
        out_shape=out_shape,
        in_specs=[vmem] * (1 + len(operands)),
        out_specs=(vmem, vmem) if r == 0 else vmem,
        scratch_shapes=scratch_shapes,
        compiler_params=pltpu.CompilerParams(vmem_limit_bytes=VMEM_LIMIT),
        cost_estimate=cost(6 * blocks * both * width * width * HEADS, 0),
        name="backward",
    )(rows, *operands)


def exchange(x, axes):
    return lax.all_to_all(x, axes, split_axis=0, concat_axis=0, tiled=True)


def swap_halves(x):
    return lax.ppermute(x, "hi", [(0, 1), (1, 0)])


def swap(x):
    peers = lax.axis_size(PEERS)
    return lax.ppermute(x, PEERS, [(i, peers - 1 - i) for i in range(peers)])


def half_candidates(mine, users):
    peers, low = lax.axis_size(PEERS), lax.axis_size("lo")
    hi, lo = lax.axis_index("hi"), lax.axis_index("lo")
    mine = mine.reshape((peers, users) + mine.shape[1:])

    def for_pair(to):
        lower = jnp.minimum(to, peers - 1 - to)
        return jnp.stack(
            [
                lax.dynamic_index_in_dim(mine, lower, 0, keepdims=False),
                lax.dynamic_index_in_dim(mine, peers - 1 - lower, 0, keepdims=False),
            ]
        )

    got = [for_pair(hi * low + lo)]
    for step in range(1, low):
        got.append(
            lax.ppermute(
                for_pair(hi * low + lax.rem(lo + step, low)),
                "lo",
                [(i, (i + step) % low) for i in range(low)],
            )
        )
    return jnp.concatenate(got, axis=2)


def local(
    table, behaviour_ids, lengths, candidates, labels, cand_counts, w_query, w_key, w_value, w_out
):
    shards = lax.axis_size(ALL)
    half = shards // 2
    sizes = (lax.axis_size("group"), lax.axis_size("lo"))
    first = lax.axis_index("hi") == 0
    users, seq = behaviour_ids.shape
    rows_dev, width = table.shape
    total = users * seq
    capacity = total // shards + total // (2 * shards)
    slots = shards * capacity
    num = candidates.shape[1] * lax.axis_size("hi") * lax.axis_size("lo")

    requests, flags, mine = plan(
        behaviour_ids, lengths, cand_counts, candidates, labels, rows_dev, sizes, capacity
    )
    wanted = exchange(requests, BY_HALF)
    here = half_candidates(mine, users)
    there = swap(here)
    flags_kept = jnp.where(first, flags[0], flags[1])
    swapped = swap(jnp.where(first, flags[1], flags[0]))

    wanted = wanted.reshape(2, sizes[0], sizes[1], capacity + LINE)
    lower = jnp.where(first, wanted[0], wanted[0, :, ::-1])
    upper = jnp.where(first, wanted[1, :, ::-1], wanted[1])
    wanted = jnp.stack([lower, upper], axis=2).reshape(shards, capacity + LINE)
    served = gather(wanted.reshape(-1), table, shards)
    wanted = wanted[:, :capacity]
    served, there, swapped = lax.optimization_barrier((served, there, swapped))
    rows = exchange(served.reshape(half, 2 * capacity, width), HALF)
    flags = jnp.stack(
        [jnp.where(first, flags_kept, swapped), jnp.where(first, swapped, flags_kept)]
    )
    cands = jnp.concatenate([jnp.where(first, here, there), jnp.where(first, there, here)], axis=2)
    cands = cands.reshape(2, users * num, width + 128)
    query, query_w = queries(cands, w_query, w_key)
    low, held = lax.axis_size("lo"), candidates.shape[1]
    step = lax.broadcasted_iota(jnp.int32, (2, low, held), 1)
    upper_half = lax.broadcasted_iota(jnp.int32, (2, low, held), 0)
    start = jnp.where(first == (upper_half == 0), lax.axis_index("lo"), low - 1 - lax.axis_index("lo"))
    place = upper_half * low + lax.rem(start - step + low, low)
    place = place * held + lax.broadcasted_iota(jnp.int32, (2, low, held), 2)
    place = jnp.broadcast_to(place.astype(F32).reshape(1, num), (users, num)).reshape(users * num, 1)

    ahead = [forward(r, rows, flags, query_w, num, w_value) for r in range(2)]
    back = []
    for r, (expo, own, mean, turned) in enumerate(ahead):
        back = backward(
            r,
            users,
            rows,
            flags,
            cands,
            place,
            query,
            query_w,
            w_key,
            w_value,
            w_out,
            expo,
            own,
            swap(own),
            mean,
            turned,
            *back,
        )
    outgoing = back
    returned = exchange(outgoing, HALF)
    table_grad = scatter(wanted.reshape(1, slots), returned, rows_dev)

    part = jnp.sum(returned[:, 2 * capacity :, :].astype(F32), axis=0).astype(BF16)
    part = (part.astype(F32) + swap_halves(part).astype(F32)).astype(BF16)
    weight_grads = exchange(jnp.broadcast_to(part[None], (half,) + part.shape), HALF)
    return table_grad, weight_grads.reshape(4, width, width).astype(F32)


def solution(mesh):
    groups, peers = mesh.shape["group"], mesh.shape["peer"]
    mesh = Mesh(mesh.devices.reshape(groups, 2, peers // 2), ALL)
    in_specs = (
        P(ALL, None),
        P(ALL, None),
        P(ALL),
        P("group", ("hi", "lo"), None),
        P("group", ("hi", "lo")),
        P(ALL),
        P(),
        P(),
        P(),
        P(),
    )
    out_specs = (P(ALL, None), P())
    return jax.shard_map(local, mesh=mesh, in_specs=in_specs, out_specs=out_specs, check_vma=False)
```

time: 176 us -> 116 us (0.66); the launches traced: 174 us -> 116 us
  waiting for transfers between devices: 71.6 us -> 28.1 us
  blocking collectives: 47.9 us -> 28.7 us
  starting transfers between devices: 17.9 us -> 24.8 us
  local copies, waits for them, and re-layouts: 3.79 us -> 1.61 us
    all_to_all x4 -> x3, waiting for transfers between devices: 71.6 us -> 22.9 us  [exchange(): return lax.all_to_all(x, axes, split_axis=0, concat_axis=0, tiled=True)]
    all_to_all x3 -> x1, blocking collectives: 47.9 us -> 28.7 us  [exchange(): return lax.all_to_all(x, axes, split_axis=0, concat_axis=0, tiled=True)]
    ppermute x0 -> x6, starting transfers between devices: none -> 10.1 us  [the longest x4 6.93 us: swap(): return lax.ppermute(x, PEERS, [(i, peers - 1 - i) for i in range(peers)])]
    ppermute x0 -> x6, waiting for transfers between devices: none -> 5.16 us  [the longest x1 3.77 us: swap_halves(): return lax.ppermute(x, 'hi', [(0, 1), (1, 0)])]
    all_to_all x4 -> x3, starting transfers between devices: 17.9 us -> 14.7 us  [exchange(): return lax.all_to_all(x, axes, split_axis=0, concat_axis=0, tiled=True)]
    unnamed x16 -> x8, local copies, waits for them, and re-layouts: 2.97 us -> 0.03 us
    pallas_call x3 -> x7, Pallas kernels: 20.3 us -> 21.6 us  [the longest x1 7.07 us: gather(): pl.pallas_call(functools.partial(gather_kernel, blocks), out_shape=jax.Sh...]
  transfers between devices with their start and end apart: 4 -> 9, of which waited for: 3 -> 5; matrix products, arithmetic and copies ran while one was open for 1% -> 1% of each run, Pallas kernels for 6% -> 19%
where the time goes in v2:
time: 116 us
  Pallas kernels  30.4 us (26%)
  blocking collectives  28.7 us (25%)
  waiting for transfers between devices  28.1 us (24%)
  starting transfers between devices  24.8 us (21%)
  local copies, waits for them, and re-layouts  1.61 us (1%)
  other arithmetic  1.4 us (1%)
    all_to_all x1, blocking collectives, exchange(): return lax.all_to_all(x, axes, split_axis=0, concat_axis=0, tiled=True)  28.7 us
    all_to_all x3, waiting for transfers between devices, exchange(): return lax.all_to_all(x, axes, split_axis=0, concat_axis=0, tiled=True)  22.9 us
    all_to_all x3, starting transfers between devices, exchange(): return lax.all_to_all(x, axes, split_axis=0, concat_axis=0, tiled=True)  14.7 us
    pallas_call x1, Pallas kernels, scatter(): pl.pallas_call(scatter_kernel, grid=(rows_dev // tile,), out_shape=jax.Sh...  8.75 us
    pallas_call x1, Pallas kernels, gather(): pl.pallas_call(functools.partial(gather_kernel, blocks), out_shape=jax.Sh...  7.07 us
    ppermute x4, starting transfers between devices, swap(): return lax.ppermute(x, PEERS, [(i, peers - 1 - i) for i in range(peers)])  6.93 us
    pallas_call x2, Pallas kernels, backward(): pl.pallas_call(functools.partial(backward_kernel, r, users), out_shape=ou...  6.72 us
    pallas_call x2, Pallas kernels, forward(): pl.pallas_call(functools.partial(forward_kernel, r, num), out_shape=(jax....  4.46 us
  transfers between devices with their start and end apart: 9, of which 5 were waited for; matrix products, arithmetic and copies ran while one was open for 1% of the time, Pallas kernels for 19%

profile of v2, /device:TPU:0, one launch (start us, length us, event | category | flops | bytes accessed | tf_op | source)
XLA Modules:
  0.0 115.9 jit_solution(12559635753959174220)
XLA Ops:
  0.6 2.9 %plan.1 = (s32[32,104]{1,0:T(8,128)}, f32[2,104,16]{2,1,0:T(8,128)S(1)}, bf16[8,16,384]{2,1,0:T(8,128)(2,1)S(1)}) custom-call(s32[2]{0:T(128)} %lengths_hbm.1, s32[2]{0:T(128)} %counts_hbm.1, s32[2,1024]{1,0:T(2,128)} %ids_hbm.1, bf16[8,16,256]{2,1,0:T(8,128)(2,1)} %cands_hbm.1, f32[8,16]{1,0:T(8,128)} %labels_hbm.1), custom_call_target="tpu_custom_call" | custom-call | tf_op jit(solution)/shard_map/plan/pallas_call | solution.py:139
  3.6 7.3 %all-to-all-start = ((s32[32,1,104]{2,1,0:T(1,128)}), s32[32,1,104]{2,1,0:T(1,128)S(1)}, u32[]{:S(2)}, u32[]{:S(2)}) async-start(s32[32,1,104]{2,1,0:T(1,128)} %bitcast.1), calls=%async_computation | async-start | bytes 32768 | tf_op jit(solution)/shard_map/all_to_all | solution.py:548
  10.9 1.8 %collective-permute-start = (bf16[2,2,16,384]{3,2,1,0:T(8,128)(2,1)S(1)}, bf16[2,2,16,384]{3,2,1,0:T(8,128)(2,1)S(1)}, u32[]{:S(2)}, u32[]{:S(2)}) collective-permute-start(bf16[2,2,16,384]{3,2,1,0:T(8,128)(2,1)S(1)} %pad_maximum_fusion.3), channel_id=1, source_target_pairs={{0,1},{1,0},{2,3},{3,2},{4,5},{5,4},{6,7},{7,6},{8,9},{9,8},{10,11... | collective-permute-start | bytes 147464 | tf_op jit(solution)/shard_map/ppermute | solution.py:577
  12.8 2.4 %collective-permute-start.2 = (f32[104,16]{1,0:T(8,128)S(1)}, f32[104,16]{1,0:T(8,128)S(1)}, u32[]{:S(2)}, u32[]{:S(2)}) collective-permute-start(f32[104,16]{1,0:T(8,128)S(1)} %select_bitcast_fusion), channel_id=1, source_target_pairs={{0,3},{1,2},{2,1},{3,0},{4,7},{5,6},{6,5},{7,4},{8,11},{9,10},{10,... | collective-permute-start | bytes 19976 | tf_op jit(solution)/shard_map/ppermute | solution.py:557
  15.2 2.9 %all-to-all-done = s32[32,1,104]{2,1,0:T(1,128)S(1)} async-done(((s32[32,1,104]{2,1,0:T(1,128)}), s32[32,1,104]{2,1,0:T(1,128)S(1)}, u32[]{:S(2)}, u32[]{:S(2)}) %all-to-all-start) | async-done | bytes 13344 | tf_op jit(solution)/shard_map/all_to_all | solution.py:548
  18.2 0.5 collective-permute-start.1
  18.8 0.1 reshape_reshape.3.wanted_ref
  18.9 7.1 %gather_rows.1 = bf16[3072,256]{1,0:T(8,128)(2,1)} custom-call(s32[3328]{0:T(1024)S(1)} %reshape_reshape.3.wanted_ref, bf16[4096,256]{1,0:T(8,128)(2,1)} %table_hbm.1), custom_call_target="tpu_custom_call" | custom-call | tf_op jit(solution)/shard_map/gather_rows/pallas_call | solution.py:212
  26.0 3.9 %all-to-all-start.1 = ((bf16[16,192,256]{2,1,0:T(8,128)(2,1)}), bf16[16,192,256]{2,1,0:T(8,128)(2,1)S(1)}, u32[]{:S(2)}, u32[]{:S(2)}) async-start(bf16[16,192,256]{2,1,0:T(8,128)(2,1)} %bitcast.13), calls=%async_computation.1 | async-start | bytes 3145728 | tf_op jit(solution)/shard_map/all_to_all | solution.py:548
  30.0 0.1 iota.30
  30.1 0.1 subtract_add_fusion
  30.1 0.1 add.59
  30.2 0.1 iota.35
  30.3 0.1 reshape.128.place_ref
  30.6 0.4 queries.1
  31.1 20.0 %all-to-all-done.1.rows_ref = bf16[16,192,256]{2,1,0:T(8,128)(2,1)S(1)} async-done(((bf16[16,192,256]{2,1,0:T(8,128)(2,1)}), bf16[16,192,256]{2,1,0:T(8,128)(2,1)S(1)}, u32[]{:S(2)}, u32[]{:S(2)}) %all-to-all-start.1) | async-done | bytes 1572896 | tf_op jit(solution)/shard_map/all_to_all | solution.py:548
  51.1 2.2 %forward.3 = (bf16[1536,512]{1,0:T(8,128)(2,1)S(1)}, bf16[288,128]{1,0:T(8,128)(2,1)S(1)}, bf16[256,512]{1,0:T(8,128)(2,1)S(1)}, bf16[256,1536]{1,0:T(8,128)(2,1)S(1)}) custom-call(bf16[16,192,256]{2,1,0:T(8,128)(2,1)S(1)} %all-to-all-done.1.rows_ref, f32[2,104,16]{2,1,0:T(8,128)S(1)} %pad_maximum_fusion.1.flags_ref, ...), custom_call_target="tpu_custom_call" | custom-call | flops 805306368 | tf_op jit(solution)/shard_map/forward/pallas_call | solution.py:383
  53.3 2.5 %collective-permute-start.4 = (bf16[288,128]{1,0:T(8,128)(2,1)S(1)}, bf16[288,128]{1,0:T(8,128)(2,1)S(1)}, u32[]{:S(2)}, u32[]{:S(2)}) collective-permute-start(bf16[288,128]{1,0:T(8,128)(2,1)S(1)} %get-tuple-element.33.own_ref), channel_id=1, source_target_pairs={{0,3},{1,2},{2,1},{3,0},{4,7},{5,6},{6,5},{7,4},{8,11},{9,10},{10,... | collective-permute-start | bytes 221192 | tf_op jit(solution)/shard_map/ppermute | solution.py:557
  55.8 2.2 %forward.2 = (bf16[1536,512]{1,0:T(8,128)(2,1)S(1)}, bf16[288,128]{1,0:T(8,128)(2,1)S(1)}, bf16[256,512]{1,0:T(8,128)(2,1)S(1)}, bf16[256,1536]{1,0:T(8,128)(2,1)S(1)}) custom-call(bf16[16,192,256]{2,1,0:T(8,128)(2,1)S(1)} %all-to-all-done.1.rows_ref, f32[2,104,16]{2,1,0:T(8,128)S(1)} %pad_maximum_fusion.1.flags_ref, ...), custom_call_target="tpu_custom_call" | custom-call | flops 805306368 | tf_op jit(solution)/shard_map/forward/pallas_call | solution.py:383
  58.1 1.5 %collective-permute-start.3 = (bf16[288,128]{1,0:T(8,128)(2,1)S(1)}, bf16[288,128]{1,0:T(8,128)(2,1)S(1)}, u32[]{:S(2)}, u32[]{:S(2)}) collective-permute-start(bf16[288,128]{1,0:T(8,128)(2,1)S(1)} %get-tuple-element.29.own_ref), channel_id=1, source_target_pairs={{0,3},{1,2},{2,1},{3,0},{4,7},{5,6},{6,5},{7,4},{8,11},{9,10},{10,... | collective-permute-start | bytes 221192 | tf_op jit(solution)/shard_map/ppermute | solution.py:557
  59.5 0.1 collective-permute-done.4.other_ref
  59.7 3.4 %backward.2 = (bf16[16,96,256]{2,1,0:T(8,128)(2,1)S(1)}, f32[1024,256]{1,0:T(8,128)S(1)}) custom-call(bf16[16,192,256]{2,1,0:T(8,128)(2,1)S(1)} %all-to-all-done.1.rows_ref, f32[2,104,16]{2,1,0:T(8,128)S(1)} %pad_maximum_fusion.1.flags_ref, bf16[2,128,384]{2,1,0:T(8,128)(2,1)S(1)} %bitcast.36, f32[128,1]{1,0:T(8,128)S(1)} %reshape.128.place_ref, ...), custom_call_target="tpu_custom_call" | custom-call | flops 4831838208 | tf_op jit(solution)/shard_map/backward/pallas_call | solution.py:535
  63.0 1.3 %collective-permute-done.3.other_ref = bf16[288,128]{1,0:T(8,128)(2,1)S(1)} collective-permute-done((bf16[288,128]{1,0:T(8,128)(2,1)S(1)}, bf16[288,128]{1,0:T(8,128)(2,1)S(1)}, u32[]{:S(2)}, u32[]{:S(2)}) %collective-permute-start.3) | collective-permute-done | bytes 73760 | tf_op jit(solution)/shard_map/ppermute | solution.py:557
  64.3 3.4 %backward.3 = bf16[16,256,256]{2,1,0:T(8,128)(2,1)S(1)} custom-call(bf16[16,192,256]{2,1,0:T(8,128)(2,1)S(1)} %all-to-all-done.1.rows_ref, f32[2,104,16]{2,1,0:T(8,128)S(1)} %pad_maximum_fusion.1.flags_ref, bf16[2,128,384]{2,1,0:T(8,128)(2,1)S(1)} %bitcast.37, f32[128,1]{1,0:T(8,128)S(1)} %reshape.128.place_ref, ...), custom_call_target="tpu_custom_call" | custom-call | flops 4831838208 | tf_op jit(solution)/shard_map/backward/pallas_call | solution.py:535
  67.7 28.7 %all_to_all.24.returned_ref = bf16[16,256,256]{2,1,0:T(8,128)(2,1)S(1)} all-to-all(bf16[16,256,256]{2,1,0:T(8,128)(2,1)S(1)} %backward.3), channel_id=1, replica_groups=mesh['group'=8,'hi'=2,'lo'=2] {'group','lo'}, dimensions={0} | all-to-all | bytes 4194304 | tf_op jit(solution)/shard_map/all_to_all | solution.py:548
  96.4 1.3 %collective-permute-start.5 = (bf16[64,256]{1,0:T(8,128)(2,1)S(1)}, bf16[64,256]{1,0:T(8,128)(2,1)S(1)}, u32[]{:S(2)}, u32[]{:S(2)}) collective-permute-start(bf16[64,256]{1,0:T(8,128)(2,1)S(1)} %slice_reduce_fusion), channel_id=1, source_target_pairs={{0,2},{2,0},{1,3},{3,1},{4,6},{6,4},{5,7},{7,5},{8,10},{10,8},{9,1... | collective-permute-start | bytes 98312 | tf_op jit(solution)/shard_map/ppermute | solution.py:552
  97.7 3.8 %collective-permute-done.5 = bf16[64,256]{1,0:T(8,128)(2,1)S(1)} collective-permute-done((bf16[64,256]{1,0:T(8,128)(2,1)S(1)}, bf16[64,256]{1,0:T(8,128)(2,1)S(1)}, u32[]{:S(2)}, u32[]{:S(2)}) %collective-permute-start.5) | collective-permute-done | bytes 32800 | tf_op jit(solution)/shard_map/ppermute | solution.py:552
  101.5 0.8 broadcast_in_dim.22
  102.4 3.6 %all-to-all-start.3 = ((bf16[16,64,256]{2,1,0:T(8,128)(2,1)}), bf16[16,64,256]{2,1,0:T(8,128)(2,1)S(1)}, u32[]{:S(2)}, u32[]{:S(2)}) async-start(bf16[16,64,256]{2,1,0:T(8,128)(2,1)} %broadcast_in_dim.22), calls=%async_computation.3 | async-start | bytes 1048576 | tf_op jit(solution)/shard_map/all_to_all | solution.py:548
  106.0 0.1 reshape.122.wanted_ref
  106.1 8.8 %scatter_rows.1 = bf16[4096,256]{1,0:T(8,128)(2,1)} custom-call(s32[1,3072]{1,0:T(1,128)S(1)} %reshape.122.wanted_ref, bf16[16,256,256]{2,1,0:T(8,128)(2,1)S(1)} %all_to_all.24.returned_ref), custom_call_target="tpu_custom_call" | custom-call | tf_op jit(solution)/shard_map/scatter_rows/pallas_call | solution.py:256
  114.8 1.1 bitcast_convert_fusion
  (33 shorter events, 0.5 us)
Async XLA Ops:
  3.6 14.6 %all-to-all-start = ((s32[32,1,104]{2,1,0:T(1,128)}), s32[32,1,104]{2,1,0:T(1,128)S(1)}, u32[]{:S(2)}, u32[]{:S(2)}) async-start(s32[32,1,104]{2,1,0:T(1,128)} %bitcast.1), calls=%async_computation | async-start | bytes 32768 | tf_op jit(solution)/shard_map/all_to_all | solution.py:548
  10.9 7.3 %collective-permute-start = (bf16[2,2,16,384]{3,2,1,0:T(8,128)(2,1)S(1)}, bf16[2,2,16,384]{3,2,1,0:T(8,128)(2,1)S(1)}, u32[]{:S(2)}, u32[]{:S(2)}) collective-permute-start(bf16[2,2,16,384]{3,2,1,0:T(8,128)(2,1)S(1)} %pad_maximum_fusion.3), channel_id=1, source_target_pairs={{0,1},{1,0},{2,3},{3,2},{4,5},{5,4},{6,7},{7,6},{8,9},{9,8},{10,11... | collective-permute-start | bytes 147464 | tf_op jit(solution)/shard_map/ppermute | solution.py:577
  12.8 13.2 %collective-permute-start.2 = (f32[104,16]{1,0:T(8,128)S(1)}, f32[104,16]{1,0:T(8,128)S(1)}, u32[]{:S(2)}, u32[]{:S(2)}) collective-permute-start(f32[104,16]{1,0:T(8,128)S(1)} %select_bitcast_fusion), channel_id=1, source_target_pairs={{0,3},{1,2},{2,1},{3,0},{4,7},{5,6},{6,5},{7,4},{8,11},{9,10},{10,... | collective-permute-start | bytes 19976 | tf_op jit(solution)/shard_map/ppermute | solution.py:557
  18.2 7.8 %collective-permute-start.1 = (bf16[2,2,32,384]{3,2,1,0:T(8,128)(2,1)S(1)}, bf16[2,2,32,384]{3,2,1,0:T(8,128)(2,1)S(1)}, u32[]{:S(2)}, u32[]{:S(2)}) collective-permute-start(bf16[2,2,32,384]{3,2,1,0:T(8,128)(2,1)S(1)} %pad_maximum_fusion.2), channel_id=1, source_target_pairs={{0,3},{1,2},{2,1},{3,0},{4,7},{5,6},{6,5},{7,4},{8,11},{9,10},{10,... | collective-permute-start | bytes 294920 | tf_op jit(solution)/shard_map/ppermute | solution.py:557
  26.0 4.6 %copy-start = (bf16[256,256]{1,0:T(8,128)(2,1)S(1)}, bf16[256,256]{1,0:T(8,128)(2,1)}, u32[]{:S(2)}) copy-start(bf16[256,256]{1,0:T(8,128)(2,1)} %wq_ref.1) | copy-start | bytes 393220
  26.0 4.6 %copy-start.1 = (bf16[256,256]{1,0:T(8,128)(2,1)S(1)}, bf16[256,256]{1,0:T(8,128)(2,1)}, u32[]{:S(2)}) copy-start(bf16[256,256]{1,0:T(8,128)(2,1)} %wk_ref.5) | copy-start | bytes 393220
  26.0 25.1 %copy-start.2 = (bf16[256,256]{1,0:T(8,128)(2,1)S(1)}, bf16[256,256]{1,0:T(8,128)(2,1)}, u32[]{:S(2)}) copy-start(bf16[256,256]{1,0:T(8,128)(2,1)} %wv_ref.7) | copy-start | bytes 393220
  26.0 25.0 %all-to-all-start.1 = ((bf16[16,192,256]{2,1,0:T(8,128)(2,1)}), bf16[16,192,256]{2,1,0:T(8,128)(2,1)S(1)}, u32[]{:S(2)}, u32[]{:S(2)}) async-start(bf16[16,192,256]{2,1,0:T(8,128)(2,1)} %bitcast.13), calls=%async_computation.1 | async-start | bytes 3145728 | tf_op jit(solution)/shard_map/all_to_all | solution.py:548
  53.3 6.3 %copy-start.3 = (bf16[256,256]{1,0:T(8,128)(2,1)S(1)}, bf16[256,256]{1,0:T(8,128)(2,1)}, u32[]{:S(2)}) copy-start(bf16[256,256]{1,0:T(8,128)(2,1)} %wo_ref.3) | copy-start | bytes 393220
  53.3 6.3 %collective-permute-start.4 = (bf16[288,128]{1,0:T(8,128)(2,1)S(1)}, bf16[288,128]{1,0:T(8,128)(2,1)S(1)}, u32[]{:S(2)}, u32[]{:S(2)}) collective-permute-start(bf16[288,128]{1,0:T(8,128)(2,1)S(1)} %get-tuple-element.33.own_ref), channel_id=1, source_target_pairs={{0,3},{1,2},{2,1},{3,0},{4,7},{5,6},{6,5},{7,4},{8,11},{9,10},{10,... | collective-permute-start | bytes 221192 | tf_op jit(solution)/shard_map/ppermute | solution.py:557
  58.1 6.2 %collective-permute-start.3 = (bf16[288,128]{1,0:T(8,128)(2,1)S(1)}, bf16[288,128]{1,0:T(8,128)(2,1)S(1)}, u32[]{:S(2)}, u32[]{:S(2)}) collective-permute-start(bf16[288,128]{1,0:T(8,128)(2,1)S(1)} %get-tuple-element.29.own_ref), channel_id=1, source_target_pairs={{0,3},{1,2},{2,1},{3,0},{4,7},{5,6},{6,5},{7,4},{8,11},{9,10},{10,... | collective-permute-start | bytes 221192 | tf_op jit(solution)/shard_map/ppermute | solution.py:557
  96.4 5.1 %collective-permute-start.5 = (bf16[64,256]{1,0:T(8,128)(2,1)S(1)}, bf16[64,256]{1,0:T(8,128)(2,1)S(1)}, u32[]{:S(2)}, u32[]{:S(2)}) collective-permute-start(bf16[64,256]{1,0:T(8,128)(2,1)S(1)} %slice_reduce_fusion), channel_id=1, source_target_pairs={{0,2},{2,0},{1,3},{3,1},{4,6},{6,4},{5,7},{7,5},{8,10},{10,8},{9,1... | collective-permute-start | bytes 98312 | tf_op jit(solution)/shard_map/ppermute | solution.py:552
  102.4 12.4 %all-to-all-start.3 = ((bf16[16,64,256]{2,1,0:T(8,128)(2,1)}), bf16[16,64,256]{2,1,0:T(8,128)(2,1)S(1)}, u32[]{:S(2)}, u32[]{:S(2)}) async-start(bf16[16,64,256]{2,1,0:T(8,128)(2,1)} %broadcast_in_dim.22), calls=%async_computation.3 | async-start | bytes 1048576 | tf_op jit(solution)/shard_map/all_to_all | solution.py:548

commit v3 on v2

--- a/solution.py
+++ b/solution.py
@@ -86,8 +86,7 @@
     place = lax.broadcasted_iota(jnp.int32, (capacity, block), 0).astype(F32)
     lane = lax.broadcasted_iota(jnp.int32, (1, block), 1)
     count = jnp.zeros((shards, 1), F32)
-    rows = jnp.zeros((2 * shards, capacity), F32)
-    flags = jnp.zeros((capacity, shards), F32)
+    rows = jnp.zeros((3 * shards, capacity), F32)
     for user in range(users):
         for start in range(0, seq, block):
             ids = ids_ref[user : user + 1, start : start + block]
@@ -106,20 +105,18 @@
             ranked = (place == rank).astype(F32).astype(BF16)
             upper = lax.shift_right_logical(row, 6).astype(F32)
             lower = (row & 63).astype(F32)
-            parts = jnp.concatenate([hot * upper, hot * lower], axis=0).astype(BF16)
-            rows = rows + nt(parts, ranked)
-            flags = flags + nt(ranked, (hot * float(user + 1)).astype(BF16))
+            parts = jnp.concatenate([hot * upper, hot * lower, hot * float(user + 1)], axis=0)
+            rows = rows + nt(parts.astype(BF16), ranked)
     requests = jnp.concatenate(
-        [rows[:shards] * 64.0 + rows[shards:], jnp.broadcast_to(count, (shards, LINE))], axis=1
+        [rows[:shards] * 64.0 + rows[shards : 2 * shards], jnp.broadcast_to(count, (shards, LINE))],
+        axis=1,
     )
     requests_ref[...] = requests.astype(jnp.int32)
-    below = lax.broadcasted_iota(jnp.int32, (8, half), 0)
-    counts = jnp.zeros((8, half), F32)
+    lane = lax.broadcasted_iota(jnp.int32, (shards, 128 - capacity), 1)
+    rest = jnp.zeros(lane.shape, F32)
     for user in range(users):
-        counts = jnp.where(below == user, counts_ref[user].astype(F32), counts)
-    for h in range(2):
-        flags_ref[h, :capacity, :] = flags[:, h * half : (h + 1) * half]
-        flags_ref[h, capacity:, :] = counts
+        rest = jnp.where(lane == user, counts_ref[user].astype(F32), rest)
+    flags_ref[...] = jnp.concatenate([rows[2 * shards :], rest], axis=1).astype(BF16)
     _, held, width = cands_ref.shape
     square = lax.broadcasted_iota(jnp.int32, (held, held), 0)
     square = square == lax.broadcasted_iota(jnp.int32, (held, held), 1)
@@ -140,7 +137,7 @@
         functools.partial(plan_kernel, rows_dev, sizes),
         out_shape=(
             jax.ShapeDtypeStruct((2 * half, capacity + LINE), jnp.int32),
-            jax.ShapeDtypeStruct((2, capacity + 8, half), F32),
+            jax.ShapeDtypeStruct((2 * half, 128), BF16),
             jax.ShapeDtypeStruct(candidates.shape[:2] + (candidates.shape[2] + 128,), BF16),
         ),
         in_specs=[pl.BlockSpec(memory_space=pltpu.HBM)] * 5,
@@ -154,11 +151,12 @@
             pltpu.SemaphoreType.DMA((5,)),
         ],
         compiler_params=pltpu.CompilerParams(vmem_limit_bytes=VMEM_LIMIT),
+        cost_estimate=cost(2**24, 0),
         name="plan",
     )(*(pltpu.with_memory_space_constraint(x, pltpu.HBM) for x in operands))
 
 
-def gather_kernel(blocks, wanted_ref, table_hbm, out_hbm, narrow, wide, out, in_sems, out_sems):
+def gather_kernel(blocks, wanted_ref, table_hbm, out_hbm, narrow, wide, out, in_sems, sems):
     slots = out.shape[0]
     capacity = slots // blocks
     line = capacity + LINE
@@ -195,12 +193,12 @@
         return lax.fori_loop(0, steps, fetch, carry)
 
     copies = []
-    groups = out_sems.shape[0]
+    groups = sems.shape[0]
     each = blocks // joint // groups
     for g in range(groups):
         lax.fori_loop(g * each, (g + 1) * each, bucket, 0)
         part = pl.ds(g * each * joint * capacity, each * joint * capacity)
-        copies.append(pltpu.make_async_copy(out.at[part], out_hbm.at[part], out_sems.at[g]))
+        copies.append(pltpu.make_async_copy(out.at[part], out_hbm.at[part], sems.at[g]))
         copies[-1].start()
     for copy in copies:
         copy.wait()
@@ -211,7 +209,7 @@
     slots = wanted.shape[0] - blocks * LINE
     return pl.pallas_call(
         functools.partial(gather_kernel, blocks),
-        out_shape=jax.ShapeDtypeStruct((slots, width), BF16),
+        out_shape=pltpu.HBM((slots, width), BF16),
         in_specs=[
             pl.BlockSpec(memory_space=pltpu.SMEM),
             pl.BlockSpec(memory_space=pltpu.HBM),
@@ -225,8 +223,28 @@
             pltpu.SemaphoreType.DMA((4,)),
         ],
         compiler_params=pltpu.CompilerParams(vmem_limit_bytes=VMEM_LIMIT),
+        cost_estimate=cost(slots * width, 0),
         name="gather_rows",
     )(wanted, pltpu.with_memory_space_constraint(table, pltpu.HBM))
+
+
+def spread_kernel(own_ref, other_ref, out_ref):
+    part = (own_ref[...].astype(F32) + other_ref[...].astype(F32)).astype(BF16)
+    for k in range(out_ref.shape[0]):
+        out_ref[k] = part
+
+
+def spread(own, other, copies):
+    vmem = pl.BlockSpec(memory_space=pltpu.VMEM)
+    return pl.pallas_call(
+        spread_kernel,
+        out_shape=pltpu.VMEM((copies,) + own.shape, BF16),
+        in_specs=[vmem, vmem],
+        out_specs=vmem,
+        compiler_params=pltpu.CompilerParams(vmem_limit_bytes=VMEM_LIMIT),
+        cost_estimate=cost(own.size, 0),
+        name="spread",
+    )(own, other)
 
 
 def scatter_kernel(wanted_ref, returned_ref, out_ref, grads):
@@ -264,6 +282,7 @@
         out_specs=pl.BlockSpec((tile, width), lambda t: (t, 0)),
         scratch_shapes=[pltpu.VMEM((slots, width), BF16)],
         compiler_params=pltpu.CompilerParams(vmem_limit_bytes=VMEM_LIMIT),
+        cost_estimate=cost(2 * rows_dev * slots * width, 0),
         name="scatter_rows",
     )(wanted, returned)
 
@@ -319,6 +338,7 @@
         in_specs=[vmem] * 3,
         out_specs=(vmem, vmem),
         compiler_params=pltpu.CompilerParams(vmem_limit_bytes=VMEM_LIMIT),
+        cost_estimate=cost(2**24, 0),
         name="queries",
     )(cands, w_query, w_key)
 
@@ -333,7 +353,7 @@
     )
 
 
-TILE = 384
+TILE = 768
 
 
 def forward_kernel(
@@ -348,13 +368,13 @@
     user_of = lax.rem(lax.broadcasted_iota(jnp.int32, (1, cols), 1), live) // num + 1
     user_of = user_of.astype(F32)
     query_w = query_w_ref[r]
+    flags = flags_ref[r].astype(F32).T
     top = jnp.full((1, cols), LOWEST, F32)
     for t in range(tiles):
         rows = take_tile(rows_ref, r, t, per_tile, capacity)
         turned_ref[:, t * TILE : (t + 1) * TILE] = rows.T
         flag = jnp.concatenate(
-            [flags_ref[r, :capacity, o : o + 1] for o in range(t * per_tile, (t + 1) * per_tile)],
-            axis=0,
+            [flags[:capacity, o : o + 1] for o in range(t * per_tile, (t + 1) * per_tile)], axis=0
         )
         score = jnp.where(flag == user_of, nt(rows, query_w), LOWEST)
         scores[t * TILE : (t + 1) * TILE, :] = score
@@ -466,7 +486,7 @@
     index = lax.broadcasted_iota(jnp.int32, (live, 1), 0)
     limit = jnp.zeros((live, 1), F32)
     for user in range(users):
-        count = flags_ref[r, capacity + user : capacity + user + 1, 0:1]
+        count = flags_ref[r, 0:1, capacity + user : capacity + user + 1].astype(F32)
         limit = jnp.where(index >= user * num, count, limit)
     alive = place_ref[...] < limit
     grad_logit = jnp.where(alive, (jax.nn.sigmoid(logit) - label) / USERS_DEV, 0.0)
@@ -486,14 +506,14 @@
     grad_heads = by_head(grad_mixed)
     grad_w = nt((grad_heads * factor_col).astype(BF16), wv).astype(BF16)
 
-    query_w = query_w_ref[r]
+    both_w = jnp.concatenate([query_w_ref[r], grad_w], axis=0)
     rows_s = jnp.zeros((width, cols), F32)
     for t in range(tiles):
         rows = take_tile(rows_ref, r, t, per_tile, capacity)
         e = expo_ref[t * TILE : (t + 1) * TILE, :]
         grad_score = (e.astype(F32) * (nt(rows, grad_w) - inner)).astype(BF16)
         rows_s = rows_s + nn(turned_ref[:, t * TILE : (t + 1) * TILE], grad_score)
-        grad_rows = (nn(grad_score, query_w) + nn(e, grad_w)).astype(BF16)
+        grad_rows = nn(jnp.concatenate([grad_score, e], axis=1), both_w).astype(BF16)
         for k in range(per_tile):
             out_ref[t * per_tile + k, r * capacity : (r + 1) * capacity, :] = grad_rows[
                 k * capacity : (k + 1) * capacity, :
@@ -557,30 +577,36 @@
     return lax.ppermute(x, PEERS, [(i, peers - 1 - i) for i in range(peers)])
 
 
-def half_candidates(mine, users):
-    peers, low = lax.axis_size(PEERS), lax.axis_size("lo")
-    hi, lo = lax.axis_index("hi"), lax.axis_index("lo")
-    mine = mine.reshape((peers, users) + mine.shape[1:])
-
-    def for_pair(to):
+def pair_candidates(mine, users, flags):
+    peers = lax.axis_size(PEERS)
+    peer = lax.axis_index(PEERS)
+    first = lax.axis_index("hi") == 0
+    _, held, wide = mine.shape
+    mine = mine.reshape(peers, users, held, wide)
+    got = []
+    for k in range(peers):
+        to = peer ^ k
         lower = jnp.minimum(to, peers - 1 - to)
-        return jnp.stack(
+        piece = jnp.stack(
             [
                 lax.dynamic_index_in_dim(mine, lower, 0, keepdims=False),
                 lax.dynamic_index_in_dim(mine, peers - 1 - lower, 0, keepdims=False),
             ]
         )
-
-    got = [for_pair(hi * low + lo)]
-    for step in range(1, low):
-        got.append(
-            lax.ppermute(
-                for_pair(hi * low + lax.rem(lo + step, low)),
-                "lo",
-                [(i, (i + step) % low) for i in range(low)],
+        if k == peers - 1:
+            piece = jnp.concatenate(
+                [piece.reshape(-1, wide), jnp.pad(flags, ((0, 0), (0, wide - flags.shape[1])))], axis=0
             )
-        )
-    return jnp.concatenate(got, axis=2)
+        if k > 0:
+            piece = lax.ppermute(piece, PEERS, [(i, i ^ k) for i in range(peers)])
+        got.append(piece)
+    lines = 2 * users * held
+    flags = got[-1][lines:, : flags.shape[1]]
+    got[-1] = got[-1][:lines].reshape(got[0].shape)
+    cands = jnp.concatenate(
+        [jnp.where(first, got[k], got[peers - 1 - k]) for k in range(peers)], axis=2
+    )
+    return cands.reshape(2, -1, wide), flags
 
 
 def local(
@@ -601,10 +627,9 @@
         behaviour_ids, lengths, cand_counts, candidates, labels, rows_dev, sizes, capacity
     )
     wanted = exchange(requests, BY_HALF)
-    here = half_candidates(mine, users)
-    there = swap(here)
+    flags = flags.reshape(2, half, -1)
     flags_kept = jnp.where(first, flags[0], flags[1])
-    swapped = swap(jnp.where(first, flags[1], flags[0]))
+    cands, swapped = pair_candidates(mine, users, jnp.where(first, flags[1], flags[0]))
 
     wanted = wanted.reshape(2, sizes[0], sizes[1], capacity + LINE)
     lower = jnp.where(first, wanted[0], wanted[0, :, ::-1])
@@ -612,20 +637,16 @@
     wanted = jnp.stack([lower, upper], axis=2).reshape(shards, capacity + LINE)
     served = gather(wanted.reshape(-1), table, shards)
     wanted = wanted[:, :capacity]
-    served, there, swapped = lax.optimization_barrier((served, there, swapped))
+    served, cands, swapped = lax.optimization_barrier((served, cands, swapped))
     rows = exchange(served.reshape(half, 2 * capacity, width), HALF)
     flags = jnp.stack(
         [jnp.where(first, flags_kept, swapped), jnp.where(first, swapped, flags_kept)]
     )
-    cands = jnp.concatenate([jnp.where(first, here, there), jnp.where(first, there, here)], axis=2)
-    cands = cands.reshape(2, users * num, width + 128)
     query, query_w = queries(cands, w_query, w_key)
-    low, held = lax.axis_size("lo"), candidates.shape[1]
-    step = lax.broadcasted_iota(jnp.int32, (2, low, held), 1)
-    upper_half = lax.broadcasted_iota(jnp.int32, (2, low, held), 0)
-    start = jnp.where(first == (upper_half == 0), lax.axis_index("lo"), low - 1 - lax.axis_index("lo"))
-    place = upper_half * low + lax.rem(start - step + low, low)
-    place = place * held + lax.broadcasted_iota(jnp.int32, (2, low, held), 2)
+    peers, held = lax.axis_size(PEERS), candidates.shape[1]
+    peer = lax.axis_index(PEERS)
+    place = jnp.minimum(peer, peers - 1 - peer) ^ jnp.arange(peers, dtype=jnp.int32)
+    place = place[:, None] * held + jnp.arange(held, dtype=jnp.int32)[None]
     place = jnp.broadcast_to(place.astype(F32).reshape(1, num), (users, num)).reshape(users * num, 1)
 
     ahead = [forward(r, rows, flags, query_w, num, w_value) for r in range(2)]
@@ -655,8 +676,7 @@
     table_grad = scatter(wanted.reshape(1, slots), returned, rows_dev)
 
     part = jnp.sum(returned[:, 2 * capacity :, :].astype(F32), axis=0).astype(BF16)
-    part = (part.astype(F32) + swap_halves(part).astype(F32)).astype(BF16)
-    weight_grads = exchange(jnp.broadcast_to(part[None], (half,) + part.shape), HALF)
+    weight_grads = exchange(spread(part, swap_halves(part), half), HALF)
     return table_grad, weight_grads.reshape(4, width, width).astype(F32)
 
 

time: 116 us -> 114 us (0.983)
    ppermute x4 -> x2, starting transfers between devices: 6.93 us -> 3.96 us  [swap(): return lax.ppermute(x, PEERS, [(i, peers - 1 - i) for i in range(peers)])]
    ppermute x1 -> x3, starting transfers between devices: 1.84 us -> 4.58 us  [pair_candidates(): piece = lax.ppermute(piece, PEERS, [(i, i ^ k) for i in range(peers)])]
    pallas_call x1 -> x2, Pallas kernels: 7.07 us -> 7.81 us  [the longest x1 6.96 us: gather(): pl.pallas_call(functools.partial(gather_kernel, blocks), out_shape=pltpu....]
where the time goes in v3:
time: 114 us
  Pallas kernels  29.4 us (26%)
  blocking collectives  28.9 us (25%)
  waiting for transfers between devices  27.8 us (24%)
  starting transfers between devices  24.7 us (22%)
  other arithmetic  1.36 us (1%)
    all_to_all x1, blocking collectives, exchange(): return lax.all_to_all(x, axes, split_axis=0, concat_axis=0, tiled=True)  28.9 us
    all_to_all x3, waiting for transfers between devices, exchange(): return lax.all_to_all(x, axes, split_axis=0, concat_axis=0, tiled=True)  22.9 us
    all_to_all x3, starting transfers between devices, exchange(): return lax.all_to_all(x, axes, split_axis=0, concat_axis=0, tiled=True)  14.7 us
    pallas_call x1, Pallas kernels, scatter(): pl.pallas_call(scatter_kernel, grid=(rows_dev // tile,), out_shape=jax.Sh...  8.75 us
    pallas_call x1, Pallas kernels, gather(): pl.pallas_call(functools.partial(gather_kernel, blocks), out_shape=pltpu....  6.96 us
    pallas_call x2, Pallas kernels, backward(): pl.pallas_call(functools.partial(backward_kernel, r, users), out_shape=ou...  6.2 us
    ppermute x3, starting transfers between devices, pair_candidates(): piece = lax.ppermute(piece, PEERS, [(i, i ^ k) for i in range(peers)])  4.58 us
    pallas_call x2, Pallas kernels, forward(): pl.pallas_call(functools.partial(forward_kernel, r, num), out_shape=(jax....  4.12 us
  transfers between devices with their start and end apart: 9, of which 5 were waited for; matrix products, arithmetic and copies ran while one was open for 1% of the time, Pallas kernels for 19%

profile of v3, /device:TPU:0, one launch (start us, length us, event | category | flops | bytes accessed | tf_op | source)
XLA Modules:
  0.0 113.7 jit_solution(9907890999623968813)
XLA Ops:
  0.6 2.1 %plan.1 = (s32[32,104]{1,0:T(8,128)}, bf16[32,128]{1,0:T(8,128)(2,1)S(1)}, bf16[8,16,384]{2,1,0:T(8,128)(2,1)S(1)}) custom-call(s32[2]{0:T(128)} %lengths_hbm.1, s32[2]{0:T(128)} %counts_hbm.1, s32[2,1024]{1,0:T(2,128)} %ids_hbm.1, bf16[8,16,256]{2,1,0:T(8,128)(2,1)} %cands_hbm.1, f32[8,16]{1,0:T(8,128)} %labels_hbm.1), custom_call_target="tpu_custom_call" | custom-call | flops 16777216 | tf_op jit(solution)/shard_map/plan/pallas_call | solution.py:136
  2.7 7.3 %all-to-all-start = ((s32[32,1,104]{2,1,0:T(1,128)}), s32[32,1,104]{2,1,0:T(1,128)S(1)}, u32[]{:S(2)}, u32[]{:S(2)}) async-start(s32[32,1,104]{2,1,0:T(1,128)} %bitcast.1), calls=%async_computation | async-start | bytes 32768 | tf_op jit(solution)/shard_map/all_to_all | solution.py:568
  10.1 2.7 %collective-permute-start.2 = (bf16[2,2,16,384]{3,2,1,0:T(8,128)(2,1)S(1)}, bf16[2,2,16,384]{3,2,1,0:T(8,128)(2,1)S(1)}, u32[]{:S(2)}, u32[]{:S(2)}) collective-permute-start(bf16[2,2,16,384]{3,2,1,0:T(8,128)(2,1)S(1)} %pad_maximum_fusion.4), channel_id=1, source_target_pairs={{0,2},{1,3},{2,0},{3,1},{4,6},{5,7},{6,4},{7,5},{8,10},{9,11},{10,... | collective-permute-start | bytes 147464 | tf_op jit(solution)/shard_map/ppermute | solution.py:601
  12.9 1.6 %collective-permute-start.1 = (bf16[2,2,16,384]{3,2,1,0:T(8,128)(2,1)S(1)}, bf16[2,2,16,384]{3,2,1,0:T(8,128)(2,1)S(1)}, u32[]{:S(2)}, u32[]{:S(2)}) collective-permute-start(bf16[2,2,16,384]{3,2,1,0:T(8,128)(2,1)S(1)} %pad_maximum_fusion.3), channel_id=1, source_target_pairs={{0,1},{1,0},{2,3},{3,2},{4,5},{5,4},{6,7},{7,6},{8,9},{9,8},{10,11... | collective-permute-start | bytes 147464 | tf_op jit(solution)/shard_map/ppermute | solution.py:601
  14.5 0.3 collective-permute-start
  14.8 2.5 %all-to-all-done = s32[32,1,104]{2,1,0:T(1,128)S(1)} async-done(((s32[32,1,104]{2,1,0:T(1,128)}), s32[32,1,104]{2,1,0:T(1,128)S(1)}, u32[]{:S(2)}, u32[]{:S(2)}) %all-to-all-start) | async-done | bytes 13344 | tf_op jit(solution)/shard_map/all_to_all | solution.py:568
  17.4 0.1 reshape_reshape.3.wanted_ref
  17.5 7.0 %gather_rows.1 = bf16[3072,256]{1,0:T(8,128)(2,1)} custom-call(s32[3328]{0:T(1024)S(1)} %reshape_reshape.3.wanted_ref, bf16[4096,256]{1,0:T(8,128)(2,1)} %table_hbm.1), custom_call_target="tpu_custom_call" | custom-call | flops 786432 | tf_op jit(solution)/shard_map/gather_rows/pallas_call | solution.py:210
  24.5 0.0 copy-start
  24.6 3.9 %all-to-all-start.1 = ((bf16[16,192,256]{2,1,0:T(8,128)(2,1)}), bf16[16,192,256]{2,1,0:T(8,128)(2,1)S(1)}, u32[]{:S(2)}, u32[]{:S(2)}) async-start(bf16[16,192,256]{2,1,0:T(8,128)(2,1)} %bitcast.32), calls=%async_computation.1 | async-start | bytes 3145728 | tf_op jit(solution)/shard_map/all_to_all | solution.py:568
  28.5 0.1 add_convert_fusion
  28.6 0.1 convert_element_type.21
  28.7 0.1 reshape.115.place_ref
  28.8 0.4 queries.1
  29.3 20.4 %all-to-all-done.1.rows_ref = bf16[16,192,256]{2,1,0:T(8,128)(2,1)S(1)} async-done(((bf16[16,192,256]{2,1,0:T(8,128)(2,1)}), bf16[16,192,256]{2,1,0:T(8,128)(2,1)S(1)}, u32[]{:S(2)}, u32[]{:S(2)}) %all-to-all-start.1) | async-done | bytes 1572896 | tf_op jit(solution)/shard_map/all_to_all | solution.py:568
  49.7 2.1 %forward.3 = (bf16[1536,512]{1,0:T(8,128)(2,1)S(1)}, bf16[288,128]{1,0:T(8,128)(2,1)S(1)}, bf16[256,512]{1,0:T(8,128)(2,1)S(1)}, bf16[256,1536]{1,0:T(8,128)(2,1)S(1)}) custom-call(bf16[16,192,256]{2,1,0:T(8,128)(2,1)S(1)} %all-to-all-done.1.rows_ref, bf16[2,16,128]{2,1,0:T(8,128)(2,1)S(1)} %pad_maximum_fusion.5.flags_ref, ...), custom_call_target="tpu_custom_call" | custom-call | flops 805306368 | tf_op jit(solution)/shard_map/forward/pallas_call | solution.py:403
  51.8 2.1 %collective-permute-start.4 = (bf16[288,128]{1,0:T(8,128)(2,1)S(1)}, bf16[288,128]{1,0:T(8,128)(2,1)S(1)}, u32[]{:S(2)}, u32[]{:S(2)}) collective-permute-start(bf16[288,128]{1,0:T(8,128)(2,1)S(1)} %get-tuple-element.33.own_ref), channel_id=1, source_target_pairs={{0,3},{1,2},{2,1},{3,0},{4,7},{5,6},{6,5},{7,4},{8,11},{9,10},{10,... | collective-permute-start | bytes 221192 | tf_op jit(solution)/shard_map/ppermute | solution.py:577
  53.9 2.1 %forward.2 = (bf16[1536,512]{1,0:T(8,128)(2,1)S(1)}, bf16[288,128]{1,0:T(8,128)(2,1)S(1)}, bf16[256,512]{1,0:T(8,128)(2,1)S(1)}, bf16[256,1536]{1,0:T(8,128)(2,1)S(1)}) custom-call(bf16[16,192,256]{2,1,0:T(8,128)(2,1)S(1)} %all-to-all-done.1.rows_ref, bf16[2,16,128]{2,1,0:T(8,128)(2,1)S(1)} %pad_maximum_fusion.5.flags_ref, ...), custom_call_target="tpu_custom_call" | custom-call | flops 805306368 | tf_op jit(solution)/shard_map/forward/pallas_call | solution.py:403
  56.0 1.8 %collective-permute-start.3 = (bf16[288,128]{1,0:T(8,128)(2,1)S(1)}, bf16[288,128]{1,0:T(8,128)(2,1)S(1)}, u32[]{:S(2)}, u32[]{:S(2)}) collective-permute-start(bf16[288,128]{1,0:T(8,128)(2,1)S(1)} %get-tuple-element.29.own_ref), channel_id=1, source_target_pairs={{0,3},{1,2},{2,1},{3,0},{4,7},{5,6},{6,5},{7,4},{8,11},{9,10},{10,... | collective-permute-start | bytes 221192 | tf_op jit(solution)/shard_map/ppermute | solution.py:577
  57.8 0.3 collective-permute-done.4.other_ref
  58.1 3.1 %backward.2 = (bf16[16,96,256]{2,1,0:T(8,128)(2,1)S(1)}, f32[1024,256]{1,0:T(8,128)S(1)}) custom-call(bf16[16,192,256]{2,1,0:T(8,128)(2,1)S(1)} %all-to-all-done.1.rows_ref, bf16[2,16,128]{2,1,0:T(8,128)(2,1)S(1)} %pad_maximum_fusion.5.flags_ref, bf16[2,128,384]{2,1,0:T(8,128)(2,1)S(1)} %bitcast.29, f32[128,1]{1,0:T(8,128)S(1)} %reshape.115.place_ref, ...), custom_call_target="tpu_custom_call" | custom-call | flops 4831838208 | tf_op jit(solution)/shard_map/backward/pallas_call | solution.py:555
  61.2 1.0 collective-permute-done.3.other_ref
  62.2 3.1 %backward.3 = bf16[16,256,256]{2,1,0:T(8,128)(2,1)S(1)} custom-call(bf16[16,192,256]{2,1,0:T(8,128)(2,1)S(1)} %all-to-all-done.1.rows_ref, bf16[2,16,128]{2,1,0:T(8,128)(2,1)S(1)} %pad_maximum_fusion.5.flags_ref, bf16[2,128,384]{2,1,0:T(8,128)(2,1)S(1)} %bitcast.30, f32[128,1]{1,0:T(8,128)S(1)} %reshape.115.place_ref, ...), custom_call_target="tpu_custom_call" | custom-call | flops 4831838208 | tf_op jit(solution)/shard_map/backward/pallas_call | solution.py:555
  65.3 28.9 %all_to_all.24.returned_ref = bf16[16,256,256]{2,1,0:T(8,128)(2,1)S(1)} all-to-all(bf16[16,256,256]{2,1,0:T(8,128)(2,1)S(1)} %backward.3), channel_id=1, replica_groups=mesh['group'=8,'hi'=2,'lo'=2] {'group','lo'}, dimensions={0} | all-to-all | bytes 4194304 | tf_op jit(solution)/shard_map/all_to_all | solution.py:568
  94.2 0.1 slice_reduce_fusion.own_ref
  94.3 1.5 %collective-permute-start.5 = (bf16[64,256]{1,0:T(8,128)(2,1)S(1)}, bf16[64,256]{1,0:T(8,128)(2,1)S(1)}, u32[]{:S(2)}, u32[]{:S(2)}) collective-permute-start(bf16[64,256]{1,0:T(8,128)(2,1)S(1)} %slice_reduce_fusion.own_ref), channel_id=1, source_target_pairs={{0,2},{2,0},{1,3},{3,1},{4,6},{6,4},{5,7},{7,5},{8,10},{10,8},{9,1... | collective-permute-start | bytes 98312 | tf_op jit(solution)/shard_map/ppermute | solution.py:572
  95.7 3.6 %collective-permute-done.5.other_ref = bf16[64,256]{1,0:T(8,128)(2,1)S(1)} collective-permute-done((bf16[64,256]{1,0:T(8,128)(2,1)S(1)}, bf16[64,256]{1,0:T(8,128)(2,1)S(1)}, u32[]{:S(2)}, u32[]{:S(2)}) %collective-permute-start.5) | collective-permute-done | bytes 32800 | tf_op jit(solution)/shard_map/ppermute | solution.py:572
  99.4 0.8 spread.1
  100.2 3.6 %all-to-all-start.3 = ((bf16[16,64,256]{2,1,0:T(8,128)(2,1)}), bf16[16,64,256]{2,1,0:T(8,128)(2,1)S(1)}, u32[]{:S(2)}, u32[]{:S(2)}) async-start(bf16[16,64,256]{2,1,0:T(8,128)(2,1)} %spread.1), calls=%async_computation.3 | async-start | bytes 1048576 | tf_op jit(solution)/shard_map/all_to_all | solution.py:568
  103.8 0.1 reshape.107.wanted_ref
  103.9 8.7 %scatter_rows.1 = bf16[4096,256]{1,0:T(8,128)(2,1)} custom-call(s32[1,3072]{1,0:T(1,128)S(1)} %reshape.107.wanted_ref, bf16[16,256,256]{2,1,0:T(8,128)(2,1)S(1)} %all_to_all.24.returned_ref), custom_call_target="tpu_custom_call" | custom-call | flops 6442450944 | tf_op jit(solution)/shard_map/scatter_rows/pallas_call | solution.py:274
  112.6 1.1 bitcast_convert_fusion
  (31 shorter events, 0.3 us)
Async XLA Ops:
  2.7 14.6 %all-to-all-start = ((s32[32,1,104]{2,1,0:T(1,128)}), s32[32,1,104]{2,1,0:T(1,128)S(1)}, u32[]{:S(2)}, u32[]{:S(2)}) async-start(s32[32,1,104]{2,1,0:T(1,128)} %bitcast.1), calls=%async_computation | async-start | bytes 32768 | tf_op jit(solution)/shard_map/all_to_all | solution.py:568
  10.1 14.4 %collective-permute-start.2 = (bf16[2,2,16,384]{3,2,1,0:T(8,128)(2,1)S(1)}, bf16[2,2,16,384]{3,2,1,0:T(8,128)(2,1)S(1)}, u32[]{:S(2)}, u32[]{:S(2)}) collective-permute-start(bf16[2,2,16,384]{3,2,1,0:T(8,128)(2,1)S(1)} %pad_maximum_fusion.4), channel_id=1, source_target_pairs={{0,2},{1,3},{2,0},{3,1},{4,6},{5,7},{6,4},{7,5},{8,10},{9,11},{10,... | collective-permute-start | bytes 147464 | tf_op jit(solution)/shard_map/ppermute | solution.py:601
  12.9 11.6 %collective-permute-start.1 = (bf16[2,2,16,384]{3,2,1,0:T(8,128)(2,1)S(1)}, bf16[2,2,16,384]{3,2,1,0:T(8,128)(2,1)S(1)}, u32[]{:S(2)}, u32[]{:S(2)}) collective-permute-start(bf16[2,2,16,384]{3,2,1,0:T(8,128)(2,1)S(1)} %pad_maximum_fusion.3), channel_id=1, source_target_pairs={{0,1},{1,0},{2,3},{3,2},{4,5},{5,4},{6,7},{7,6},{8,9},{9,8},{10,11... | collective-permute-start | bytes 147464 | tf_op jit(solution)/shard_map/ppermute | solution.py:601
  14.5 10.0 %collective-permute-start = (bf16[80,384]{1,0:T(8,128)(2,1)S(1)}, bf16[80,384]{1,0:T(8,128)(2,1)S(1)}, u32[]{:S(2)}, u32[]{:S(2)}) collective-permute-start(bf16[80,384]{1,0:T(8,128)(2,1)S(1)} %fusion.1), channel_id=1, source_target_pairs={{0,3},{1,2},{2,1},{3,0},{4,7},{5,6},{6,5},{7,4},{8,11},{9,10},{10,... | collective-permute-start | bytes 184328 | tf_op jit(solution)/shard_map/ppermute | solution.py:601
  24.5 4.4 %copy-start = (bf16[256,256]{1,0:T(8,128)(2,1)S(1)}, bf16[256,256]{1,0:T(8,128)(2,1)}, u32[]{:S(2)}) copy-start(bf16[256,256]{1,0:T(8,128)(2,1)} %wq_ref.1) | copy-start | bytes 393220
  24.5 4.4 %copy-start.1 = (bf16[256,256]{1,0:T(8,128)(2,1)S(1)}, bf16[256,256]{1,0:T(8,128)(2,1)}, u32[]{:S(2)}) copy-start(bf16[256,256]{1,0:T(8,128)(2,1)} %wk_ref.5) | copy-start | bytes 393220
  24.6 25.1 %copy-start.2 = (bf16[256,256]{1,0:T(8,128)(2,1)S(1)}, bf16[256,256]{1,0:T(8,128)(2,1)}, u32[]{:S(2)}) copy-start(bf16[256,256]{1,0:T(8,128)(2,1)} %wv_ref.7) | copy-start | bytes 393220
  24.6 25.1 %all-to-all-start.1 = ((bf16[16,192,256]{2,1,0:T(8,128)(2,1)}), bf16[16,192,256]{2,1,0:T(8,128)(2,1)S(1)}, u32[]{:S(2)}, u32[]{:S(2)}) async-start(bf16[16,192,256]{2,1,0:T(8,128)(2,1)} %bitcast.32), calls=%async_computation.1 | async-start | bytes 3145728 | tf_op jit(solution)/shard_map/all_to_all | solution.py:568
  51.8 6.3 %copy-start.3 = (bf16[256,256]{1,0:T(8,128)(2,1)S(1)}, bf16[256,256]{1,0:T(8,128)(2,1)}, u32[]{:S(2)}) copy-start(bf16[256,256]{1,0:T(8,128)(2,1)} %wo_ref.3) | copy-start | bytes 393220
  51.8 6.3 %collective-permute-start.4 = (bf16[288,128]{1,0:T(8,128)(2,1)S(1)}, bf16[288,128]{1,0:T(8,128)(2,1)S(1)}, u32[]{:S(2)}, u32[]{:S(2)}) collective-permute-start(bf16[288,128]{1,0:T(8,128)(2,1)S(1)} %get-tuple-element.33.own_ref), channel_id=1, source_target_pairs={{0,3},{1,2},{2,1},{3,0},{4,7},{5,6},{6,5},{7,4},{8,11},{9,10},{10,... | collective-permute-start | bytes 221192 | tf_op jit(solution)/shard_map/ppermute | solution.py:577
  56.0 6.2 %collective-permute-start.3 = (bf16[288,128]{1,0:T(8,128)(2,1)S(1)}, bf16[288,128]{1,0:T(8,128)(2,1)S(1)}, u32[]{:S(2)}, u32[]{:S(2)}) collective-permute-start(bf16[288,128]{1,0:T(8,128)(2,1)S(1)} %get-tuple-element.29.own_ref), channel_id=1, source_target_pairs={{0,3},{1,2},{2,1},{3,0},{4,7},{5,6},{6,5},{7,4},{8,11},{9,10},{10,... | collective-permute-start | bytes 221192 | tf_op jit(solution)/shard_map/ppermute | solution.py:577
  94.3 5.1 %collective-permute-start.5 = (bf16[64,256]{1,0:T(8,128)(2,1)S(1)}, bf16[64,256]{1,0:T(8,128)(2,1)S(1)}, u32[]{:S(2)}, u32[]{:S(2)}) collective-permute-start(bf16[64,256]{1,0:T(8,128)(2,1)S(1)} %slice_reduce_fusion.own_ref), channel_id=1, source_target_pairs={{0,2},{2,0},{1,3},{3,1},{4,6},{6,4},{5,7},{7,5},{8,10},{10,8},{9,1... | collective-permute-start | bytes 98312 | tf_op jit(solution)/shard_map/ppermute | solution.py:572
  100.2 12.4 %all-to-all-start.3 = ((bf16[16,64,256]{2,1,0:T(8,128)(2,1)}), bf16[16,64,256]{2,1,0:T(8,128)(2,1)S(1)}, u32[]{:S(2)}, u32[]{:S(2)}) async-start(bf16[16,64,256]{2,1,0:T(8,128)(2,1)} %spread.1), calls=%async_computation.3 | async-start | bytes 1048576 | tf_op jit(solution)/shard_map/all_to_all | solution.py:568

commit v4 on v3

--- a/solution.py
+++ b/solution.py
@@ -156,12 +156,13 @@
     )(*(pltpu.with_memory_space_constraint(x, pltpu.HBM) for x in operands))
 
 
-def gather_kernel(blocks, wanted_ref, table_hbm, out_hbm, narrow, wide, out, in_sems, sems):
+def gather_kernel(blocks, wanted_ref, table_hbm, out, narrow, wide, in_sems):
     slots = out.shape[0]
     capacity = slots // blocks
     line = capacity + LINE
-    joint = 1 if capacity % 16 == 0 else math.lcm(capacity, 16) // capacity
-    step = 16 if joint == 1 else joint * capacity
+    joint = 1 if capacity % 32 == 0 else math.lcm(capacity, 16) // capacity
+    step = 32 if joint == 1 else joint * capacity
+    halves, _, lanes = wide.shape
     loads = in_sems.shape[0]
     size = narrow.shape[0] // loads
     copies = []
@@ -173,7 +174,8 @@
     for k, copy in enumerate(copies):
         copy.wait()
         part = slice(k * size, (k + 1) * size)
-        wide[part, :] = narrow[part, :].astype(F32)
+        for h in range(halves):
+            wide[h, part, :] = narrow[part, h * lanes : (h + 1) * lanes].astype(F32)
 
     def bucket(b, carry):
         first = b * joint * line
@@ -182,26 +184,18 @@
             at = c * step
             start = pl.multiple_of(b * joint * capacity + at, 16)
             for k in range(0, step, 16):
-                rows = [
-                    wide[pl.ds(wanted_ref[first + at + n + n // capacity * LINE], 1), :]
-                    for n in range(k, k + 16)
-                ]
-                out[pl.ds(start + k, 16), :] = jnp.concatenate(rows, axis=0).astype(BF16)
+                ids = [wanted_ref[first + at + n + n // capacity * LINE] for n in range(k, k + 16)]
+                for h in range(halves):
+                    rows = [wide[h, pl.ds(row, 1), :] for row in ids]
+                    out[pl.ds(start + k, 16), h * lanes : (h + 1) * lanes] = jnp.concatenate(
+                        rows, axis=0
+                    ).astype(BF16)
             return carry
 
         steps = 1 if joint > 1 else lax.div(wanted_ref[first + capacity] + step - 1, step)
         return lax.fori_loop(0, steps, fetch, carry)
 
-    copies = []
-    groups = sems.shape[0]
-    each = blocks // joint // groups
-    for g in range(groups):
-        lax.fori_loop(g * each, (g + 1) * each, bucket, 0)
-        part = pl.ds(g * each * joint * capacity, each * joint * capacity)
-        copies.append(pltpu.make_async_copy(out.at[part], out_hbm.at[part], sems.at[g]))
-        copies[-1].start()
-    for copy in copies:
-        copy.wait()
+    lax.fori_loop(0, blocks // joint, bucket, 0)
 
 
 def gather(wanted, table, blocks):
@@ -209,18 +203,16 @@
     slots = wanted.shape[0] - blocks * LINE
     return pl.pallas_call(
         functools.partial(gather_kernel, blocks),
-        out_shape=pltpu.HBM((slots, width), BF16),
+        out_shape=jax.ShapeDtypeStruct((slots, width), BF16),
         in_specs=[
             pl.BlockSpec(memory_space=pltpu.SMEM),
             pl.BlockSpec(memory_space=pltpu.HBM),
         ],
-        out_specs=pl.BlockSpec(memory_space=pltpu.HBM),
+        out_specs=pl.BlockSpec(memory_space=pltpu.VMEM),
         scratch_shapes=[
             pltpu.VMEM(table.shape, BF16),
-            pltpu.VMEM(table.shape, F32),
-            pltpu.VMEM((slots, width), BF16),
+            pltpu.VMEM((width // 128, table.shape[0], 128), F32),
             pltpu.SemaphoreType.DMA((8,)),
-            pltpu.SemaphoreType.DMA((4,)),
         ],
         compiler_params=pltpu.CompilerParams(vmem_limit_bytes=VMEM_LIMIT),
         cost_estimate=cost(slots * width, 0),
@@ -270,7 +262,7 @@
 def scatter(wanted, returned, rows_dev):
     slots = wanted.shape[1]
     width = returned.shape[-1]
-    tile = 512
+    tile = 1024
     return pl.pallas_call(
         scatter_kernel,
         grid=(rows_dev // tile,),
@@ -316,33 +308,6 @@
     return jnp.concatenate([x[h : h + 1, :] for h in range(HEADS)], axis=1)
 
 
-def query_kernel(cands_ref, wq_ref, wk_ref, query_ref, query_w_ref):
-    width = wq_ref.shape[0]
-    live = cands_ref.shape[1]
-    scale = float(width // HEADS) ** (-0.5)
-    cands = jnp.concatenate([cands_ref[r, :, :width] for r in range(2)], axis=0)
-    query = nn(cands, wq_ref[...]).astype(BF16).astype(F32) * scale
-    for r in range(2):
-        heads = by_head(query[r * live : (r + 1) * live]).astype(BF16)
-        query_ref[r] = heads
-        query_w_ref[r] = nt(heads, wk_ref[...]).astype(BF16)
-
-
-def queries(cands, w_query, w_key):
-    width = w_query.shape[0]
-    shape = jax.ShapeDtypeStruct((2, HEADS * cands.shape[1], width), BF16)
-    vmem = pl.BlockSpec(memory_space=pltpu.VMEM)
-    return pl.pallas_call(
-        query_kernel,
-        out_shape=(shape, shape),
-        in_specs=[vmem] * 3,
-        out_specs=(vmem, vmem),
-        compiler_params=pltpu.CompilerParams(vmem_limit_bytes=VMEM_LIMIT),
-        cost_estimate=cost(2**24, 0),
-        name="queries",
-    )(cands, w_query, w_key)
-
-
 def take_tile(rows_ref, r, t, per_tile, capacity):
     return jnp.concatenate(
         [
@@ -354,39 +319,61 @@
 
 
 TILE = 768
+FORWARD_TILE = 256
 
 
 def forward_kernel(
-    r, num, rows_ref, flags_ref, query_w_ref, wv_ref, expo_ref, part_ref, mean_ref, turned_ref, scores
+    r,
+    num,
+    rows_ref,
+    flags_ref,
+    cands_ref,
+    wq_ref,
+    wk_ref,
+    wv_ref,
+    expo_ref,
+    part_ref,
+    mean_ref,
+    turned_ref,
+    query_ref,
+    query_w_ref,
+    scores,
+    mine,
 ):
     blocks, both, width = rows_ref.shape
     capacity = both // 2
-    cols = query_w_ref.shape[1]
-    live = cols // HEADS
-    per_tile = TILE // capacity
-    tiles = blocks // per_tile
+    live = cands_ref.shape[1]
+    cols = HEADS * live
+    tiles = blocks * capacity // FORWARD_TILE
+    for b in range(blocks):
+        mine[b * capacity : (b + 1) * capacity, :] = rows_ref[b, r * capacity : (r + 1) * capacity, :]
     user_of = lax.rem(lax.broadcasted_iota(jnp.int32, (1, cols), 1), live) // num + 1
     user_of = user_of.astype(F32)
-    query_w = query_w_ref[r]
+    scale = float(width // HEADS) ** (-0.5)
+    query = nn(cands_ref[r, :, :width], wq_ref[...]).astype(BF16).astype(F32) * scale
+    query = by_head(query).astype(BF16)
+    query_w = nt(query, wk_ref[...]).astype(BF16)
+    query_ref[...] = query
+    query_w_ref[...] = query_w
     flags = flags_ref[r].astype(F32).T
     top = jnp.full((1, cols), LOWEST, F32)
+    flags = jnp.concatenate([flags[:capacity, o : o + 1] for o in range(blocks)], axis=0)
     for t in range(tiles):
-        rows = take_tile(rows_ref, r, t, per_tile, capacity)
-        turned_ref[:, t * TILE : (t + 1) * TILE] = rows.T
-        flag = jnp.concatenate(
-            [flags[:capacity, o : o + 1] for o in range(t * per_tile, (t + 1) * per_tile)], axis=0
-        )
-        score = jnp.where(flag == user_of, nt(rows, query_w), LOWEST)
-        scores[t * TILE : (t + 1) * TILE, :] = score
+        part = slice(t * FORWARD_TILE, (t + 1) * FORWARD_TILE)
+        rows = mine[part, :]
+        turned_ref[:, part] = rows.T
+        score = jnp.where(flags[part] == user_of, nt(rows, query_w), LOWEST)
+        scores[part, :] = score
         top = jnp.maximum(top, jnp.max(score, axis=0, keepdims=True))
     norm = jnp.zeros((1, cols), F32)
     rows_e = jnp.zeros((width, cols), F32)
     for t in range(tiles):
-        e = jnp.exp(scores[t * TILE : (t + 1) * TILE, :] - top)
+        part = slice(t * FORWARD_TILE, (t + 1) * FORWARD_TILE)
+        e = jnp.exp(scores[part, :] - top)
         norm = norm + jnp.sum(e, axis=0, keepdims=True)
         e = e.astype(BF16)
-        expo_ref[t * TILE : (t + 1) * TILE, :] = e
-        rows_e = rows_e + nn(turned_ref[:, t * TILE : (t + 1) * TILE], e)
+        expo_ref[part, :] = e
+        rows_e = rows_e + nn(turned_ref[:, part], e)
     mean = (rows_e * (1.0 / norm)).astype(BF16)
     mean_ref[...] = mean
     part_ref[:width, :] = head_blocks(wv_ref[...].T, mean, live).astype(BF16)
@@ -395,26 +382,30 @@
     part_ref[width:, :] = jnp.concatenate([x.astype(F32) for x in rest], axis=0).astype(BF16)
 
 
-def forward(r, rows, flags, query_w, num, w_value):
+def forward(r, rows, flags, cands, num, w_query, w_key, w_value):
     blocks, both, width = rows.shape
-    cols = query_w.shape[1]
+    live = cands.shape[1]
+    cols = HEADS * live
     slots = blocks * both // 2
     vmem = pl.BlockSpec(memory_space=pltpu.VMEM)
+    shapes = (
+        (slots, cols),
+        (width + 32, live),
+        (width, cols),
+        (width, slots),
+        (cols, width),
+        (cols, width),
+    )
     return pl.pallas_call(
         functools.partial(forward_kernel, r, num),
-        out_shape=(
-            jax.ShapeDtypeStruct((slots, cols), BF16),
-            jax.ShapeDtypeStruct((width + 32, cols // HEADS), BF16),
-            jax.ShapeDtypeStruct((width, cols), BF16),
-            jax.ShapeDtypeStruct((width, slots), BF16),
-        ),
-        in_specs=[vmem] * 4,
-        out_specs=(vmem,) * 4,
-        scratch_shapes=[pltpu.VMEM((slots, cols), F32)],
+        out_shape=tuple(jax.ShapeDtypeStruct(shape, BF16) for shape in shapes),
+        in_specs=[vmem] * 6,
+        out_specs=(vmem,) * len(shapes),
+        scratch_shapes=[pltpu.VMEM((slots, cols), F32), pltpu.VMEM((slots, width), BF16)],
         compiler_params=pltpu.CompilerParams(vmem_limit_bytes=VMEM_LIMIT),
         cost_estimate=cost(4 * slots * width * cols, slots * cols),
         name="forward",
-    )(rows, flags, query_w, w_value)
+    )(rows, flags, cands, w_query, w_key, w_value)
 
 
 def opened(part_ref, width):
@@ -427,20 +418,20 @@
 def backward_kernel(
     r,
     users,
+    low,
     rows_ref,
     flags_ref,
     cands_ref,
-    place_ref,
-    query_ref,
-    query_w_ref,
     wk_ref,
     wv_ref,
     wo_ref,
+    other_ref,
     expo_ref,
     own_ref,
-    other_ref,
     mean_ref,
     turned_ref,
+    query_ref,
+    query_w_ref,
     *refs,
 ):
     if r == 0:
@@ -483,12 +474,17 @@
     proj = nn(mixed_tb.T, wo)
     logit = jnp.sum(proj * cand_f, axis=1, keepdims=True) / root
     label = cands_ref[r, :, width:].astype(F32)[:, 0:1]
+    lo = lax.axis_index("lo")
+    lower = jnp.where(lax.axis_index("hi") == 0, lo, low - 1 - lo)
     index = lax.broadcasted_iota(jnp.int32, (live, 1), 0)
+    held = num // (2 * low)
+    place = lax.rem(index, num)
+    place = (lax.div(place, held) ^ lower) * held + lax.rem(place, held)
     limit = jnp.zeros((live, 1), F32)
     for user in range(users):
         count = flags_ref[r, 0:1, capacity + user : capacity + user + 1].astype(F32)
         limit = jnp.where(index >= user * num, count, limit)
-    alive = place_ref[...] < limit
+    alive = place.astype(F32) < limit
     grad_logit = jnp.where(alive, (jax.nn.sigmoid(logit) - label) / USERS_DEV, 0.0)
     grad_proj = (grad_logit * cand_f / root).astype(BF16)
     grad_mixed = nt(grad_proj, wo).astype(BF16).astype(F32)
@@ -506,7 +502,7 @@
     grad_heads = by_head(grad_mixed)
     grad_w = nt((grad_heads * factor_col).astype(BF16), wv).astype(BF16)
 
-    both_w = jnp.concatenate([query_w_ref[r], grad_w], axis=0)
+    both_w = jnp.concatenate([query_w_ref[...], grad_w], axis=0)
     rows_s = jnp.zeros((width, cols), F32)
     for t in range(tiles):
         rows = take_tile(rows_ref, r, t, per_tile, capacity)
@@ -524,7 +520,7 @@
     share = flat(part_own)
     parts = (
         nt(cands.T, grad_query_t),
-        nn(rows_s, query_ref[r]),
+        nn(rows_s, query_ref[...]),
         nn((mean_ref[...].astype(F32) * share).astype(BF16), grad_heads.astype(BF16)),
         nn(mixed_tb, grad_proj) * 0.5,
     )
@@ -542,7 +538,7 @@
             out_ref[b, both:, :] = weights[b * rows_each : (b + 1) * rows_each, :].astype(BF16)
 
 
-def backward(r, users, rows, *operands):
+def backward(r, users, low, rows, *operands):
     blocks, both, width = rows.shape
     vmem = pl.BlockSpec(memory_space=pltpu.VMEM)
     weights = jax.ShapeDtypeStruct((4 * width, width), F32)
@@ -553,7 +549,7 @@
         out_shape = jax.ShapeDtypeStruct((blocks, both + 4 * width // blocks, width), BF16)
         scratch_shapes = [pltpu.VMEM(weights.shape, F32)]
     return pl.pallas_call(
-        functools.partial(backward_kernel, r, users),
+        functools.partial(backward_kernel, r, users, low),
         out_shape=out_shape,
         in_specs=[vmem] * (1 + len(operands)),
         out_specs=(vmem, vmem) if r == 0 else vmem,
@@ -639,36 +635,28 @@
     wanted = wanted[:, :capacity]
     served, cands, swapped = lax.optimization_barrier((served, cands, swapped))
     rows = exchange(served.reshape(half, 2 * capacity, width), HALF)
+    rows, cands, swapped, flags_kept = lax.optimization_barrier((rows, cands, swapped, flags_kept))
     flags = jnp.stack(
         [jnp.where(first, flags_kept, swapped), jnp.where(first, swapped, flags_kept)]
     )
-    query, query_w = queries(cands, w_query, w_key)
-    peers, held = lax.axis_size(PEERS), candidates.shape[1]
-    peer = lax.axis_index(PEERS)
-    place = jnp.minimum(peer, peers - 1 - peer) ^ jnp.arange(peers, dtype=jnp.int32)
-    place = place[:, None] * held + jnp.arange(held, dtype=jnp.int32)[None]
-    place = jnp.broadcast_to(place.astype(F32).reshape(1, num), (users, num)).reshape(users * num, 1)
-
-    ahead = [forward(r, rows, flags, query_w, num, w_value) for r in range(2)]
+    ahead = [forward(r, rows, flags, cands, num, w_query, w_key, w_value) for r in range(2)]
     back = []
-    for r, (expo, own, mean, turned) in enumerate(ahead):
+    for r, (expo, own, *kept) in enumerate(ahead):
+        other = swap(own)
         back = backward(
             r,
             users,
+            sizes[1],
             rows,
             flags,
             cands,
-            place,
-            query,
-            query_w,
             w_key,
             w_value,
             w_out,
+            other,
             expo,
             own,
-            swap(own),
-            mean,
-            turned,
+            *kept,
             *back,
         )
     outgoing = back

time: 114 us -> 111 us (0.974)
  blocking collectives: 28.9 us -> 51.1 us
  waiting for transfers between devices: 27.8 us -> 8.75 us
  starting transfers between devices: 24.7 us -> 21 us
  Pallas kernels: 29.4 us -> 27.2 us
    all_to_all x1 -> x2, blocking collectives: 28.9 us -> 51.1 us  [exchange(): return lax.all_to_all(x, axes, split_axis=0, concat_axis=0, tiled=True)]
    all_to_all x3 -> x2, waiting for transfers between devices: 22.9 us -> 3.04 us  [exchange(): return lax.all_to_all(x, axes, split_axis=0, concat_axis=0, tiled=True)]
    all_to_all x3 -> x2, starting transfers between devices: 14.7 us -> 10.9 us  [exchange(): return lax.all_to_all(x, axes, split_axis=0, concat_axis=0, tiled=True)]
    pallas_call x6 -> x5, Pallas kernels: 17.7 us -> 16.2 us  [the longest x2 6.23 us: backward(): pl.pallas_call(functools.partial(backward_kernel, r, users, low), out_sha...]
  transfers between devices with their start and end apart: 9 -> 8, of which waited for: 5 -> 5; matrix products, arithmetic and copies ran while one was open for 1% -> 0% of each run, Pallas kernels for 19% -> 17%
where the time goes in v4:
time: 111 us
  blocking collectives  51.1 us (46%)
  Pallas kernels  27.2 us (25%)
  starting transfers between devices  21 us (19%)
  waiting for transfers between devices  8.75 us (8%)
  other arithmetic  1.29 us (1%)
    all_to_all x2, blocking collectives, exchange(): return lax.all_to_all(x, axes, split_axis=0, concat_axis=0, tiled=True)  51.1 us
    all_to_all x2, starting transfers between devices, exchange(): return lax.all_to_all(x, axes, split_axis=0, concat_axis=0, tiled=True)  10.9 us
    pallas_call x1, Pallas kernels, scatter(): pl.pallas_call(scatter_kernel, grid=(rows_dev // tile,), out_shape=jax.Sh...  8.11 us
    pallas_call x2, Pallas kernels, backward(): pl.pallas_call(functools.partial(backward_kernel, r, users, low), out_sha...  6.23 us
    pallas_call x1, Pallas kernels, gather(): pl.pallas_call(functools.partial(gather_kernel, blocks), out_shape=jax.Sh...  5.09 us
    pallas_call x2, Pallas kernels, forward(): pl.pallas_call(functools.partial(forward_kernel, r, num), out_shape=tuple...  4.84 us
    ppermute x3, starting transfers between devices, pair_candidates(): piece = lax.ppermute(piece, PEERS, [(i, i ^ k) for i in range(peers)])  4.58 us
    ppermute x2, starting transfers between devices, swap(): return lax.ppermute(x, PEERS, [(i, peers - 1 - i) for i in range(peers)])  3.95 us
  transfers between devices with their start and end apart: 8, of which 5 were waited for; matrix products, arithmetic and copies ran while one was open for 0% of the time, Pallas kernels for 17%

profile of v4, /device:TPU:0, one launch (start us, length us, event | category | flops | bytes accessed | tf_op | source)
XLA Modules:
  0.0 110.6 jit_solution(12470386210381035057)
XLA Ops:
  0.6 2.1 %plan.1 = (s32[32,104]{1,0:T(8,128)}, bf16[32,128]{1,0:T(8,128)(2,1)S(1)}, bf16[8,16,384]{2,1,0:T(8,128)(2,1)S(1)}) custom-call(s32[2]{0:T(128)} %lengths_hbm.1, s32[2]{0:T(128)} %counts_hbm.1, s32[2,1024]{1,0:T(2,128)} %ids_hbm.1, bf16[8,16,256]{2,1,0:T(8,128)(2,1)} %cands_hbm.1, f32[8,16]{1,0:T(8,128)} %labels_hbm.1), custom_call_target="tpu_custom_call" | custom-call | flops 16777216 | tf_op jit(solution)/shard_map/plan/pallas_call | solution.py:136
  2.7 7.3 %all-to-all-start = ((s32[32,1,104]{2,1,0:T(1,128)}), s32[32,1,104]{2,1,0:T(1,128)S(1)}, u32[]{:S(2)}, u32[]{:S(2)}) async-start(s32[32,1,104]{2,1,0:T(1,128)} %bitcast.1), calls=%async_computation | async-start | bytes 32768 | tf_op jit(solution)/shard_map/all_to_all | solution.py:564
  10.1 2.7 %collective-permute-start.2 = (bf16[2,2,16,384]{3,2,1,0:T(8,128)(2,1)S(1)}, bf16[2,2,16,384]{3,2,1,0:T(8,128)(2,1)S(1)}, u32[]{:S(2)}, u32[]{:S(2)}) collective-permute-start(bf16[2,2,16,384]{3,2,1,0:T(8,128)(2,1)S(1)} %pad_maximum_fusion.4), channel_id=1, source_target_pairs={{0,2},{1,3},{2,0},{3,1},{4,6},{5,7},{6,4},{7,5},{8,10},{9,11},{10,... | collective-permute-start | bytes 147464 | tf_op jit(solution)/shard_map/ppermute | solution.py:597
  12.9 1.6 %collective-permute-start.1 = (bf16[2,2,16,384]{3,2,1,0:T(8,128)(2,1)S(1)}, bf16[2,2,16,384]{3,2,1,0:T(8,128)(2,1)S(1)}, u32[]{:S(2)}, u32[]{:S(2)}) collective-permute-start(bf16[2,2,16,384]{3,2,1,0:T(8,128)(2,1)S(1)} %pad_maximum_fusion.3), channel_id=1, source_target_pairs={{0,1},{1,0},{2,3},{3,2},{4,5},{5,4},{6,7},{7,6},{8,9},{9,8},{10,11... | collective-permute-start | bytes 147464 | tf_op jit(solution)/shard_map/ppermute | solution.py:597
  14.5 0.3 collective-permute-start
  14.8 2.5 %all-to-all-done = s32[32,1,104]{2,1,0:T(1,128)S(1)} async-done(((s32[32,1,104]{2,1,0:T(1,128)}), s32[32,1,104]{2,1,0:T(1,128)S(1)}, u32[]{:S(2)}, u32[]{:S(2)}) %all-to-all-start) | async-done | bytes 13344 | tf_op jit(solution)/shard_map/all_to_all | solution.py:564
  17.4 0.1 reshape_reshape.3.wanted_ref
  17.5 5.1 %gather_rows.1 = bf16[3072,256]{1,0:T(8,128)(2,1)S(1)} custom-call(s32[3328]{0:T(1024)S(1)} %reshape_reshape.3.wanted_ref, bf16[4096,256]{1,0:T(8,128)(2,1)} %table_hbm.1), custom_call_target="tpu_custom_call" | custom-call | flops 786432 | tf_op jit(solution)/shard_map/gather_rows/pallas_call | solution.py:204
  22.6 0.0 copy-start
  22.6 0.0 copy-start.1
  22.6 0.0 copy-start.2
  22.6 0.0 collective-permute-done.1
  22.7 0.0 collective-permute-done
  22.8 22.7 %all_to_all.24.rows_ref = bf16[16,192,256]{2,1,0:T(8,128)(2,1)S(1)} all-to-all(bf16[16,192,256]{2,1,0:T(8,128)(2,1)S(1)} %bitcast.28), channel_id=1, replica_groups=mesh['group'=8,'hi'=2,'lo'=2] {'group','lo'}, dimensions={0} | all-to-all | bytes 3145728 | tf_op jit(solution)/shard_map/all_to_all | solution.py:564
  45.5 2.4 %forward.3 = (bf16[1536,512]{1,0:T(8,128)(2,1)S(1)}, bf16[288,128]{1,0:T(8,128)(2,1)S(1)}, bf16[256,512]{1,0:T(8,128)(2,1)S(1)}, bf16[256,1536]{1,0:T(8,128)(2,1...) custom-call(bf16[16,192,256]{2,1,0:T(8,128)(2,1)S(1)} %all_to_all.24.rows_ref, ...), custom_call_target="tpu_custom_call" | custom-call | flops 805306368 | tf_op jit(solution)/shard_map/forward/pallas_call | solution.py:399
  47.9 3.1 %collective-permute-start.4 = (bf16[288,128]{1,0:T(8,128)(2,1)S(1)}, bf16[288,128]{1,0:T(8,128)(2,1)S(1)}, u32[]{:S(2)}, u32[]{:S(2)}) collective-permute-start(bf16[288,128]{1,0:T(8,128)(2,1)S(1)} %get-tuple-element.42.own_ref), channel_id=1, source_target_pairs={{0,3},{1,2},{2,1},{3,0},{4,7},{5,6},{6,5},{7,4},{8,11},{9,10},{10,... | collective-permute-start | bytes 221192 | tf_op jit(solution)/shard_map/ppermute | solution.py:573
  51.0 2.4 %forward.2 = (bf16[1536,512]{1,0:T(8,128)(2,1)S(1)}, bf16[288,128]{1,0:T(8,128)(2,1)S(1)}, bf16[256,512]{1,0:T(8,128)(2,1)S(1)}, bf16[256,1536]{1,0:T(8,128)(2,1...) custom-call(bf16[16,192,256]{2,1,0:T(8,128)(2,1)S(1)} %all_to_all.24.rows_ref, ...), custom_call_target="tpu_custom_call" | custom-call | flops 805306368 | tf_op jit(solution)/shard_map/forward/pallas_call | solution.py:399
  53.4 0.8 collective-permute-start.3
  54.3 0.2 collective-permute-done.4.other_ref
  54.5 3.1 %backward.2 = (bf16[16,96,256]{2,1,0:T(8,128)(2,1)S(1)}, f32[1024,256]{1,0:T(8,128)S(1)}) custom-call(bf16[16,192,256]{2,1,0:T(8,128)(2,1)S(1)} %all_to_all.24.rows_ref, bf16[2,16,128]{2,1,0:T(8,128)(2,1)S(1)} %pad_maximum_fusion.5.flags_ref, bf16[2,128,384]{2,1,0:T(8,128)(2,1)S(1)} %bitcast.32, bf16[256,256]{1,0:T(8,128)(2,1)S(1)} %copy-done.1, ...), custom_call_target="tpu_custom_call" | custom-call | flops 4831838208 | tf_op jit(solution)/shard_map/backward/pallas_call | solution.py:551
  57.6 2.0 %collective-permute-done.3.other_ref = bf16[288,128]{1,0:T(8,128)(2,1)S(1)} collective-permute-done((bf16[288,128]{1,0:T(8,128)(2,1)S(1)}, bf16[288,128]{1,0:T(8,128)(2,1)S(1)}, u32[]{:S(2)}, u32[]{:S(2)}) %collective-permute-start.3) | collective-permute-done | bytes 73760 | tf_op jit(solution)/shard_map/ppermute | solution.py:573
  59.6 3.1 %backward.3 = bf16[16,256,256]{2,1,0:T(8,128)(2,1)S(1)} custom-call(bf16[16,192,256]{2,1,0:T(8,128)(2,1)S(1)} %all_to_all.24.rows_ref, bf16[2,16,128]{2,1,0:T(8,128)(2,1)S(1)} %pad_maximum_fusion.5.flags_ref, bf16[2,128,384]{2,1,0:T(8,128)(2,1)S(1)} %bitcast.33, bf16[256,256]{1,0:T(8,128)(2,1)S(1)} %copy-done.1, bf16[256,256]{1,0:T(8,128)(2,1)S(1)} %copy-done.2, ...), custom_call_target="tpu_custom_call" | custom-call | flops 4831838208 | tf_op jit(solution)/shard_map/backward/pallas_call | solution.py:551
  62.8 28.4 %all_to_all.25.returned_ref = bf16[16,256,256]{2,1,0:T(8,128)(2,1)S(1)} all-to-all(bf16[16,256,256]{2,1,0:T(8,128)(2,1)S(1)} %backward.3), channel_id=1, replica_groups=mesh['group'=8,'hi'=2,'lo'=2] {'group','lo'}, dimensions={0} | all-to-all | bytes 4194304 | tf_op jit(solution)/shard_map/all_to_all | solution.py:564
  91.2 0.1 slice_reduce_fusion.own_ref
  91.3 1.6 %collective-permute-start.5 = (bf16[64,256]{1,0:T(8,128)(2,1)S(1)}, bf16[64,256]{1,0:T(8,128)(2,1)S(1)}, u32[]{:S(2)}, u32[]{:S(2)}) collective-permute-start(bf16[64,256]{1,0:T(8,128)(2,1)S(1)} %slice_reduce_fusion.own_ref), channel_id=1, source_target_pairs={{0,2},{2,0},{1,3},{3,1},{4,6},{6,4},{5,7},{7,5},{8,10},{10,8},{9,1... | collective-permute-start | bytes 98312 | tf_op jit(solution)/shard_map/ppermute | solution.py:568
  92.9 3.5 %collective-permute-done.5.other_ref = bf16[64,256]{1,0:T(8,128)(2,1)S(1)} collective-permute-done((bf16[64,256]{1,0:T(8,128)(2,1)S(1)}, bf16[64,256]{1,0:T(8,128)(2,1)S(1)}, u32[]{:S(2)}, u32[]{:S(2)}) %collective-permute-start.5) | collective-permute-done | bytes 32800 | tf_op jit(solution)/shard_map/ppermute | solution.py:568
  96.4 0.8 spread.1
  97.2 3.6 %all-to-all-start.3 = ((bf16[16,64,256]{2,1,0:T(8,128)(2,1)}), bf16[16,64,256]{2,1,0:T(8,128)(2,1)S(1)}, u32[]{:S(2)}, u32[]{:S(2)}) async-start(bf16[16,64,256]{2,1,0:T(8,128)(2,1)} %spread.1), calls=%async_computation.3 | async-start | bytes 1048576 | tf_op jit(solution)/shard_map/all_to_all | solution.py:564
  100.8 0.1 reshape.81.wanted_ref
  100.9 8.1 %scatter_rows.1 = bf16[4096,256]{1,0:T(8,128)(2,1)} custom-call(s32[1,3072]{1,0:T(1,128)S(1)} %reshape.81.wanted_ref, bf16[16,256,256]{2,1,0:T(8,128)(2,1)S(1)} %all_to_all.25.returned_ref), custom_call_target="tpu_custom_call" | custom-call | flops 6442450944 | tf_op jit(solution)/shard_map/scatter_rows/pallas_call | solution.py:266
  109.0 0.5 all-to-all-done.3
  109.5 1.1 bitcast_convert_fusion
  (24 shorter events, 0.3 us)
Async XLA Ops:
  2.7 14.6 %all-to-all-start = ((s32[32,1,104]{2,1,0:T(1,128)}), s32[32,1,104]{2,1,0:T(1,128)S(1)}, u32[]{:S(2)}, u32[]{:S(2)}) async-start(s32[32,1,104]{2,1,0:T(1,128)} %bitcast.1), calls=%async_computation | async-start | bytes 32768 | tf_op jit(solution)/shard_map/all_to_all | solution.py:564
  10.1 12.5 %collective-permute-start.2 = (bf16[2,2,16,384]{3,2,1,0:T(8,128)(2,1)S(1)}, bf16[2,2,16,384]{3,2,1,0:T(8,128)(2,1)S(1)}, u32[]{:S(2)}, u32[]{:S(2)}) collective-permute-start(bf16[2,2,16,384]{3,2,1,0:T(8,128)(2,1)S(1)} %pad_maximum_fusion.4), channel_id=1, source_target_pairs={{0,2},{1,3},{2,0},{3,1},{4,6},{5,7},{6,4},{7,5},{8,10},{9,11},{10,... | collective-permute-start | bytes 147464 | tf_op jit(solution)/shard_map/ppermute | solution.py:597
  12.9 9.8 %collective-permute-start.1 = (bf16[2,2,16,384]{3,2,1,0:T(8,128)(2,1)S(1)}, bf16[2,2,16,384]{3,2,1,0:T(8,128)(2,1)S(1)}, u32[]{:S(2)}, u32[]{:S(2)}) collective-permute-start(bf16[2,2,16,384]{3,2,1,0:T(8,128)(2,1)S(1)} %pad_maximum_fusion.3), channel_id=1, source_target_pairs={{0,1},{1,0},{2,3},{3,2},{4,5},{5,4},{6,7},{7,6},{8,9},{9,8},{10,11... | collective-permute-start | bytes 147464 | tf_op jit(solution)/shard_map/ppermute | solution.py:597
  14.5 8.2 %collective-permute-start = (bf16[80,384]{1,0:T(8,128)(2,1)S(1)}, bf16[80,384]{1,0:T(8,128)(2,1)S(1)}, u32[]{:S(2)}, u32[]{:S(2)}) collective-permute-start(bf16[80,384]{1,0:T(8,128)(2,1)S(1)} %fusion.1), channel_id=1, source_target_pairs={{0,3},{1,2},{2,1},{3,0},{4,7},{5,6},{6,5},{7,4},{8,11},{9,10},{10,... | collective-permute-start | bytes 184328 | tf_op jit(solution)/shard_map/ppermute | solution.py:597
  22.6 22.8 %copy-start = (bf16[256,256]{1,0:T(8,128)(2,1)S(1)}, bf16[256,256]{1,0:T(8,128)(2,1)}, u32[]{:S(2)}) copy-start(bf16[256,256]{1,0:T(8,128)(2,1)} %wq_ref.3) | copy-start | bytes 393220
  22.6 22.8 %copy-start.1 = (bf16[256,256]{1,0:T(8,128)(2,1)S(1)}, bf16[256,256]{1,0:T(8,128)(2,1)}, u32[]{:S(2)}) copy-start(bf16[256,256]{1,0:T(8,128)(2,1)} %wk_ref.7) | copy-start | bytes 393220
  22.6 22.8 %copy-start.2 = (bf16[256,256]{1,0:T(8,128)(2,1)S(1)}, bf16[256,256]{1,0:T(8,128)(2,1)}, u32[]{:S(2)}) copy-start(bf16[256,256]{1,0:T(8,128)(2,1)} %wv_ref.7) | copy-start | bytes 393220
  47.9 6.6 %copy-start.3 = (bf16[256,256]{1,0:T(8,128)(2,1)S(1)}, bf16[256,256]{1,0:T(8,128)(2,1)}, u32[]{:S(2)}) copy-start(bf16[256,256]{1,0:T(8,128)(2,1)} %wo_ref.3) | copy-start | bytes 393220
  47.9 6.6 %collective-permute-start.4 = (bf16[288,128]{1,0:T(8,128)(2,1)S(1)}, bf16[288,128]{1,0:T(8,128)(2,1)S(1)}, u32[]{:S(2)}, u32[]{:S(2)}) collective-permute-start(bf16[288,128]{1,0:T(8,128)(2,1)S(1)} %get-tuple-element.42.own_ref), channel_id=1, source_target_pairs={{0,3},{1,2},{2,1},{3,0},{4,7},{5,6},{6,5},{7,4},{8,11},{9,10},{10,... | collective-permute-start | bytes 221192 | tf_op jit(solution)/shard_map/ppermute | solution.py:573
  53.4 6.2 %collective-permute-start.3 = (bf16[288,128]{1,0:T(8,128)(2,1)S(1)}, bf16[288,128]{1,0:T(8,128)(2,1)S(1)}, u32[]{:S(2)}, u32[]{:S(2)}) collective-permute-start(bf16[288,128]{1,0:T(8,128)(2,1)S(1)} %get-tuple-element.36.own_ref), channel_id=1, source_target_pairs={{0,3},{1,2},{2,1},{3,0},{4,7},{5,6},{6,5},{7,4},{8,11},{9,10},{10,... | collective-permute-start | bytes 221192 | tf_op jit(solution)/shard_map/ppermute | solution.py:573
  91.3 5.1 %collective-permute-start.5 = (bf16[64,256]{1,0:T(8,128)(2,1)S(1)}, bf16[64,256]{1,0:T(8,128)(2,1)S(1)}, u32[]{:S(2)}, u32[]{:S(2)}) collective-permute-start(bf16[64,256]{1,0:T(8,128)(2,1)S(1)} %slice_reduce_fusion.own_ref), channel_id=1, source_target_pairs={{0,2},{2,0},{1,3},{3,1},{4,6},{6,4},{5,7},{7,5},{8,10},{10,8},{9,1... | collective-permute-start | bytes 98312 | tf_op jit(solution)/shard_map/ppermute | solution.py:568
  97.2 12.3 %all-to-all-start.3 = ((bf16[16,64,256]{2,1,0:T(8,128)(2,1)}), bf16[16,64,256]{2,1,0:T(8,128)(2,1)S(1)}, u32[]{:S(2)}, u32[]{:S(2)}) async-start(bf16[16,64,256]{2,1,0:T(8,128)(2,1)} %spread.1), calls=%async_computation.3 | async-start | bytes 1048576 | tf_op jit(solution)/shard_map/all_to_all | solution.py:564

commit v5 on v4

--- a/solution.py
+++ b/solution.py
@@ -293,11 +293,11 @@
     )
 
 
-def pieces(x):
-    a = x.astype(BF16)
-    x = x - a.astype(F32)
-    b = x.astype(BF16)
-    return [a, b, (x - b.astype(F32)).astype(BF16)]
+def head_sums(x):
+    size = x.shape[0] // HEADS
+    return jnp.concatenate(
+        [jnp.sum(x[h * size : (h + 1) * size], axis=0, keepdims=True) for h in range(HEADS)], axis=0
+    )
 
 
 def stacked(x, live):
@@ -331,12 +331,15 @@
     wq_ref,
     wk_ref,
     wv_ref,
+    wo_ref,
     expo_ref,
     part_ref,
     mean_ref,
     turned_ref,
     query_ref,
     query_w_ref,
+    mixed_ref,
+    turned_out_ref,
     scores,
     mine,
 ):
@@ -376,43 +379,42 @@
         rows_e = rows_e + nn(turned_ref[:, part], e)
     mean = (rows_e * (1.0 / norm)).astype(BF16)
     mean_ref[...] = mean
-    part_ref[:width, :] = head_blocks(wv_ref[...].T, mean, live).astype(BF16)
-    rest = pieces(stacked(top, live)) + pieces(stacked(norm, live))
-    rest.append(jnp.zeros((8, live), BF16))
-    part_ref[width:, :] = jnp.concatenate([x.astype(F32) for x in rest], axis=0).astype(BF16)
-
-
-def forward(r, rows, flags, cands, num, w_query, w_key, w_value):
+    mixed = head_blocks(wv_ref[...].T, mean, live)
+    mixed_ref[...] = mixed.astype(BF16)
+    out = nt(wo_ref[...], cands_ref[r, :, :width])
+    turned_out_ref[...] = out
+    part_ref[...] = jnp.concatenate(
+        [head_sums(mixed * out), stacked(top, live), stacked(norm, live), jnp.zeros((4, live), F32)],
+        axis=0,
+    )
+
+
+def forward(r, rows, flags, cands, num, *weights):
     blocks, both, width = rows.shape
     live = cands.shape[1]
     cols = HEADS * live
     slots = blocks * both // 2
     vmem = pl.BlockSpec(memory_space=pltpu.VMEM)
     shapes = (
-        (slots, cols),
-        (width + 32, live),
-        (width, cols),
-        (width, slots),
-        (cols, width),
-        (cols, width),
+        ((slots, cols), BF16),
+        ((16, live), F32),
+        ((width, cols), BF16),
+        ((width, slots), BF16),
+        ((cols, width), BF16),
+        ((cols, width), BF16),
+        ((width, live), BF16),
+        ((width, live), F32),
     )
     return pl.pallas_call(
         functools.partial(forward_kernel, r, num),
-        out_shape=tuple(jax.ShapeDtypeStruct(shape, BF16) for shape in shapes),
-        in_specs=[vmem] * 6,
+        out_shape=tuple(jax.ShapeDtypeStruct(*shape) for shape in shapes),
+        in_specs=[vmem] * (3 + len(weights)),
         out_specs=(vmem,) * len(shapes),
         scratch_shapes=[pltpu.VMEM((slots, cols), F32), pltpu.VMEM((slots, width), BF16)],
         compiler_params=pltpu.CompilerParams(vmem_limit_bytes=VMEM_LIMIT),
         cost_estimate=cost(4 * slots * width * cols, slots * cols),
         name="forward",
-    )(rows, flags, cands, w_query, w_key, w_value)
-
-
-def opened(part_ref, width):
-    rest = part_ref[width:, :].astype(F32)
-    top = rest[0:4] + rest[4:8] + rest[8:12]
-    norm = rest[12:16] + rest[16:20] + rest[20:24]
-    return part_ref[:width, :].astype(F32), top, norm
+    )(rows, flags, cands, *weights)
 
 
 def backward_kernel(
@@ -424,7 +426,6 @@
     cands_ref,
     wk_ref,
     wv_ref,
-    wo_ref,
     other_ref,
     expo_ref,
     own_ref,
@@ -432,6 +433,8 @@
     turned_ref,
     query_ref,
     query_w_ref,
+    mixed_ref,
+    turned_out_ref,
     *refs,
 ):
     if r == 0:
@@ -448,59 +451,39 @@
     root = float(width) ** 0.5
     per_tile = TILE // capacity
     tiles = blocks // per_tile
-    wv, wo = wv_ref[...], wo_ref[...]
-
-    mixed_own, top_own, norm_own = opened(own_ref, width)
-    mixed_other, top_other, norm_other = opened(other_ref, width)
+
+    top_own, top_other = own_ref[4:8, :], other_ref[4:8, :]
     top = jnp.maximum(top_own, top_other)
     factor = jnp.exp(top_own - top)
-    part_own = norm_own * factor
-    part_other = norm_other * jnp.exp(top_other - top)
+    part_own = own_ref[8:12, :] * factor
+    part_other = other_ref[8:12, :] * jnp.exp(top_other - top)
     inv = 1.0 / (part_own + part_other)
     factor = factor * inv
     part_own = part_own * inv
     part_other = part_other * inv
-    mixed_t = jnp.concatenate(
-        [
-            mixed_own[h * head_size : (h + 1) * head_size] * part_own[h : h + 1]
-            + mixed_other[h * head_size : (h + 1) * head_size] * part_other[h : h + 1]
-            for h in range(HEADS)
-        ],
-        axis=0,
-    )
-    mixed_tb = mixed_t.astype(BF16)
+    dots = own_ref[0:4, :] * part_own + other_ref[0:4, :] * part_other
+    logit = jnp.sum(dots, axis=0, keepdims=True) / root
+
     cands = cands_ref[r, :, :width]
-    cand_f = cands.astype(F32)
-    proj = nn(mixed_tb.T, wo)
-    logit = jnp.sum(proj * cand_f, axis=1, keepdims=True) / root
-    label = cands_ref[r, :, width:].astype(F32)[:, 0:1]
+    label = cands_ref[r, :, width:].astype(F32).T[0:1, :]
     lo = lax.axis_index("lo")
     lower = jnp.where(lax.axis_index("hi") == 0, lo, low - 1 - lo)
-    index = lax.broadcasted_iota(jnp.int32, (live, 1), 0)
+    index = lax.broadcasted_iota(jnp.int32, (1, live), 1)
     held = num // (2 * low)
     place = lax.rem(index, num)
     place = (lax.div(place, held) ^ lower) * held + lax.rem(place, held)
-    limit = jnp.zeros((live, 1), F32)
+    limit = jnp.zeros((1, live), F32)
     for user in range(users):
         count = flags_ref[r, 0:1, capacity + user : capacity + user + 1].astype(F32)
         limit = jnp.where(index >= user * num, count, limit)
     alive = place.astype(F32) < limit
     grad_logit = jnp.where(alive, (jax.nn.sigmoid(logit) - label) / USERS_DEV, 0.0)
-    grad_proj = (grad_logit * cand_f / root).astype(BF16)
-    grad_mixed = nt(grad_proj, wo).astype(BF16).astype(F32)
-    joint = grad_mixed.T * mixed_t
-    inner = jnp.concatenate(
-        [
-            jnp.sum(joint[h * head_size : (h + 1) * head_size, :], axis=0, keepdims=True)
-            for h in range(HEADS)
-        ],
-        axis=0,
-    )
-    inner = flat(inner * factor)
+    grad_mixed = (turned_out_ref[...] * (grad_logit / root)).T.astype(BF16).astype(F32)
+    inner = flat(dots * (grad_logit / root) * factor)
     factor = flat(factor)
     factor_col = jnp.broadcast_to(factor, (128, cols)).T[:, :1]
     grad_heads = by_head(grad_mixed)
-    grad_w = nt((grad_heads * factor_col).astype(BF16), wv).astype(BF16)
+    grad_w = nt((grad_heads * factor_col).astype(BF16), wv_ref[...]).astype(BF16)
 
     both_w = jnp.concatenate([query_w_ref[...], grad_w], axis=0)
     rows_s = jnp.zeros((width, cols), F32)
@@ -517,12 +500,20 @@
 
     rows_s = rows_s.astype(BF16)
     grad_query_t = (head_blocks(wk_ref[...].T, rows_s, live) * scale).astype(BF16)
-    share = flat(part_own)
+    grad_col = jnp.broadcast_to(grad_logit, (128, live)).T[:, :1]
+    grad_proj = (grad_col * cands.astype(F32) / root).astype(BF16)
+    mixed = jnp.concatenate(
+        [
+            mixed_ref[h * head_size : (h + 1) * head_size, :].astype(F32) * part_own[h : h + 1]
+            for h in range(HEADS)
+        ],
+        axis=0,
+    )
     parts = (
         nt(cands.T, grad_query_t),
         nn(rows_s, query_ref[...]),
-        nn((mean_ref[...].astype(F32) * share).astype(BF16), grad_heads.astype(BF16)),
-        nn(mixed_tb, grad_proj) * 0.5,
+        nn((mean_ref[...].astype(F32) * flat(part_own)).astype(BF16), grad_heads.astype(BF16)),
+        nn(mixed.astype(BF16), grad_proj),
     )
     for k, part in enumerate(parts):
         if r == 0:
@@ -639,7 +630,9 @@
     flags = jnp.stack(
         [jnp.where(first, flags_kept, swapped), jnp.where(first, swapped, flags_kept)]
     )
-    ahead = [forward(r, rows, flags, cands, num, w_query, w_key, w_value) for r in range(2)]
+    ahead = [
+        forward(r, rows, flags, cands, num, w_query, w_key, w_value, w_out) for r in range(2)
+    ]
     back = []
     for r, (expo, own, *kept) in enumerate(ahead):
         other = swap(own)
@@ -652,7 +645,6 @@
             cands,
             w_key,
             w_value,
-            w_out,
             other,
             expo,
             own,

time: 111 us -> 110 us (level)
  transfers between devices with their start and end apart: 8 -> 8, of which waited for: 5 -> 4; matrix products, arithmetic and copies ran while one was open for 0% -> 0% of each run, Pallas kernels for 17% -> 17%
where the time goes in v5:
time: 110 us
  blocking collectives  51.1 us (46%)
  Pallas kernels  26.6 us (24%)
  starting transfers between devices  21.3 us (19%)
  waiting for transfers between devices  7.97 us (7%)
  other arithmetic  1.29 us (1%)
    all_to_all x2, blocking collectives, exchange(): return lax.all_to_all(x, axes, split_axis=0, concat_axis=0, tiled=True)  51.1 us
    all_to_all x2, starting transfers between devices, exchange(): return lax.all_to_all(x, axes, split_axis=0, concat_axis=0, tiled=True)  10.9 us
    pallas_call x1, Pallas kernels, scatter(): pl.pallas_call(scatter_kernel, grid=(rows_dev // tile,), out_shape=jax.Sh...  8.12 us
    pallas_call x1, Pallas kernels, gather(): pl.pallas_call(functools.partial(gather_kernel, blocks), out_shape=jax.Sh...  5.38 us
    pallas_call x2, Pallas kernels, backward(): pl.pallas_call(functools.partial(backward_kernel, r, users, low), out_sha...  5.31 us
    pallas_call x2, Pallas kernels, forward(): pl.pallas_call(functools.partial(forward_kernel, r, num), out_shape=tuple...  4.89 us
    ppermute x3, starting transfers between devices, pair_candidates(): piece = lax.ppermute(piece, PEERS, [(i, i ^ k) for i in range(peers)])  4.58 us
    ppermute x2, starting transfers between devices, swap(): return lax.ppermute(x, PEERS, [(i, peers - 1 - i) for i in range(peers)])  3.98 us
  transfers between devices with their start and end apart: 8, of which 4 were waited for; matrix products, arithmetic and copies ran while one was open for 0% of the time, Pallas kernels for 17%

profile of v5, /device:TPU:0, one launch (start us, length us, event | category | flops | bytes accessed | tf_op | source)
XLA Modules:
  0.0 109.5 jit_solution(5539424112649608583)
XLA Ops:
  0.6 2.1 %plan.1 = (s32[32,104]{1,0:T(8,128)}, bf16[32,128]{1,0:T(8,128)(2,1)S(1)}, bf16[8,16,384]{2,1,0:T(8,128)(2,1)S(1)}) custom-call(s32[2]{0:T(128)} %lengths_hbm.1, s32[2]{0:T(128)} %counts_hbm.1, s32[2,1024]{1,0:T(2,128)} %ids_hbm.1, bf16[8,16,256]{2,1,0:T(8,128)(2,1)} %cands_hbm.1, f32[8,16]{1,0:T(8,128)} %labels_hbm.1), custom_call_target="tpu_custom_call" | custom-call | flops 16777216 | tf_op jit(solution)/shard_map/plan/pallas_call | solution.py:136
  2.7 7.3 %all-to-all-start = ((s32[32,1,104]{2,1,0:T(1,128)}), s32[32,1,104]{2,1,0:T(1,128)S(1)}, u32[]{:S(2)}, u32[]{:S(2)}) async-start(s32[32,1,104]{2,1,0:T(1,128)} %bitcast.1), calls=%async_computation | async-start | bytes 32768 | tf_op jit(solution)/shard_map/all_to_all | solution.py:555
  10.1 2.7 %collective-permute-start.2 = (bf16[2,2,16,384]{3,2,1,0:T(8,128)(2,1)S(1)}, bf16[2,2,16,384]{3,2,1,0:T(8,128)(2,1)S(1)}, u32[]{:S(2)}, u32[]{:S(2)}) collective-permute-start(bf16[2,2,16,384]{3,2,1,0:T(8,128)(2,1)S(1)} %pad_maximum_fusion.4), channel_id=1, source_target_pairs={{0,2},{1,3},{2,0},{3,1},{4,6},{5,7},{6,4},{7,5},{8,10},{9,11},{10,... | collective-permute-start | bytes 147464 | tf_op jit(solution)/shard_map/ppermute | solution.py:588
  12.9 1.6 %collective-permute-start.1 = (bf16[2,2,16,384]{3,2,1,0:T(8,128)(2,1)S(1)}, bf16[2,2,16,384]{3,2,1,0:T(8,128)(2,1)S(1)}, u32[]{:S(2)}, u32[]{:S(2)}) collective-permute-start(bf16[2,2,16,384]{3,2,1,0:T(8,128)(2,1)S(1)} %pad_maximum_fusion.3), channel_id=1, source_target_pairs={{0,1},{1,0},{2,3},{3,2},{4,5},{5,4},{6,7},{7,6},{8,9},{9,8},{10,11... | collective-permute-start | bytes 147464 | tf_op jit(solution)/shard_map/ppermute | solution.py:588
  14.5 0.3 collective-permute-start
  14.8 2.5 %all-to-all-done = s32[32,1,104]{2,1,0:T(1,128)S(1)} async-done(((s32[32,1,104]{2,1,0:T(1,128)}), s32[32,1,104]{2,1,0:T(1,128)S(1)}, u32[]{:S(2)}, u32[]{:S(2)}) %all-to-all-start) | async-done | bytes 13344 | tf_op jit(solution)/shard_map/all_to_all | solution.py:555
  17.4 0.1 reshape_reshape.3.wanted_ref
  17.5 5.4 %gather_rows.1 = bf16[3072,256]{1,0:T(8,128)(2,1)S(1)} custom-call(s32[3328]{0:T(1024)S(1)} %reshape_reshape.3.wanted_ref, bf16[4096,256]{1,0:T(8,128)(2,1)} %table_hbm.1), custom_call_target="tpu_custom_call" | custom-call | flops 786432 | tf_op jit(solution)/shard_map/gather_rows/pallas_call | solution.py:204
  22.9 0.0 copy-start
  22.9 0.0 copy-start.1
  22.9 0.0 copy-start.2
  22.9 0.0 copy-start.3
  23.0 0.0 collective-permute-done
  23.1 22.7 %all_to_all.24.rows_ref = bf16[16,192,256]{2,1,0:T(8,128)(2,1)S(1)} all-to-all(bf16[16,192,256]{2,1,0:T(8,128)(2,1)S(1)} %bitcast.28), channel_id=1, replica_groups=mesh['group'=8,'hi'=2,'lo'=2] {'group','lo'}, dimensions={0} | all-to-all | bytes 3145728 | tf_op jit(solution)/shard_map/all_to_all | solution.py:555
  45.8 2.4 %forward.3 = (bf16[1536,512]{1,0:T(8,128)(2,1)S(1)}, f32[16,128]{1,0:T(8,128)S(1)}, bf16[256,512]{1,0:T(8,128)(2,1)S(1)}, bf16[256,1536]{1,0:T(8,128)(2,1)S(1)},...) custom-call(bf16[16,192,256]{2,1,0:T(8,128)(2,1)S(1)} %all_to_all.24, ...), custom_call_target="tpu_custom_call" | custom-call | flops 805306368 | tf_op jit(solution)/shard_map/forward/pallas_call | solution.py:408
  48.2 2.9 %collective-permute-start.4 = (f32[16,128]{1,0:T(8,128)S(1)}, f32[16,128]{1,0:T(8,128)S(1)}, u32[]{:S(2)}, u32[]{:S(2)}) collective-permute-start(f32[16,128]{1,0:T(8,128)S(1)} %get-tuple-element.48.own_ref), channel_id=1, source_target_pairs={{0,3},{1,2},{2,1},{3,0},{4,7},{5,6},{6,5},{7,4},{8,11},{9,10},{10,... | collective-permute-start | bytes 24584 | tf_op jit(solution)/shard_map/ppermute | solution.py:564
  51.1 2.4 %forward.2 = (bf16[1536,512]{1,0:T(8,128)(2,1)S(1)}, f32[16,128]{1,0:T(8,128)S(1)}, bf16[256,512]{1,0:T(8,128)(2,1)S(1)}, bf16[256,1536]{1,0:T(8,128)(2,1)S(1)},...) custom-call(bf16[16,192,256]{2,1,0:T(8,128)(2,1)S(1)} %all_to_all.24, ...), custom_call_target="tpu_custom_call" | custom-call | flops 805306368 | tf_op jit(solution)/shard_map/forward/pallas_call | solution.py:408
  53.5 1.1 %collective-permute-start.3 = (f32[16,128]{1,0:T(8,128)S(1)}, f32[16,128]{1,0:T(8,128)S(1)}, u32[]{:S(2)}, u32[]{:S(2)}) collective-permute-start(f32[16,128]{1,0:T(8,128)S(1)} %get-tuple-element.40.own_ref), channel_id=1, source_target_pairs={{0,3},{1,2},{2,1},{3,0},{4,7},{5,6},{6,5},{7,4},{8,11},{9,10},{10,... | collective-permute-start | bytes 24584 | tf_op jit(solution)/shard_map/ppermute | solution.py:564
  54.6 0.0 collective-permute-done.4.other_ref
  54.6 2.7 %backward.2 = (bf16[16,96,256]{2,1,0:T(8,128)(2,1)S(1)}, f32[1024,256]{1,0:T(8,128)S(1)}) custom-call(bf16[16,192,256]{2,1,0:T(8,128)(2,1)S(1)} %all_to_all.24.rows_ref, bf16[2,16,128]{2,1,0:T(8,128)(2,1)S(1)} %pad_maximum_fusion.5.flags_ref, bf16[2,128,384]{2,1,0:T(8,128)(2,1)S(1)} %bitcast.32, bf16[256,256]{1,0:T(8,128)(2,1)S(1)} %copy-done.2, ...), custom_call_target="tpu_custom_call" | custom-call | flops 4831838208 | tf_op jit(solution)/shard_map/backward/pallas_call | solution.py:542
  57.3 1.7 %collective-permute-done.3.other_ref = f32[16,128]{1,0:T(8,128)S(1)} collective-permute-done((f32[16,128]{1,0:T(8,128)S(1)}, f32[16,128]{1,0:T(8,128)S(1)}, u32[]{:S(2)}, u32[]{:S(2)}) %collective-permute-start.3) | collective-permute-done | bytes 8224 | tf_op jit(solution)/shard_map/ppermute | solution.py:564
  59.0 2.7 %backward.3 = bf16[16,256,256]{2,1,0:T(8,128)(2,1)S(1)} custom-call(bf16[16,192,256]{2,1,0:T(8,128)(2,1)S(1)} %all_to_all.24.rows_ref, bf16[2,16,128]{2,1,0:T(8,128)(2,1)S(1)} %pad_maximum_fusion.5.flags_ref, bf16[2,128,384]{2,1,0:T(8,128)(2,1)S(1)} %bitcast.33, bf16[256,256]{1,0:T(8,128)(2,1)S(1)} %copy-done.2, bf16[256,256]{1,0:T(8,128)(2,1)S(1)} %copy-done.3, ...), custom_call_target="tpu_custom_call" | custom-call | flops 4831838208 | tf_op jit(solution)/shard_map/backward/pallas_call | solution.py:542
  61.7 28.5 %all_to_all.25.returned_ref = bf16[16,256,256]{2,1,0:T(8,128)(2,1)S(1)} all-to-all(bf16[16,256,256]{2,1,0:T(8,128)(2,1)S(1)} %backward.3), channel_id=1, replica_groups=mesh['group'=8,'hi'=2,'lo'=2] {'group','lo'}, dimensions={0} | all-to-all | bytes 4194304 | tf_op jit(solution)/shard_map/all_to_all | solution.py:555
  90.1 0.1 slice_reduce_fusion.own_ref
  90.2 1.9 %collective-permute-start.5 = (bf16[64,256]{1,0:T(8,128)(2,1)S(1)}, bf16[64,256]{1,0:T(8,128)(2,1)S(1)}, u32[]{:S(2)}, u32[]{:S(2)}) collective-permute-start(bf16[64,256]{1,0:T(8,128)(2,1)S(1)} %slice_reduce_fusion.own_ref), channel_id=1, source_target_pairs={{0,2},{2,0},{1,3},{3,1},{4,6},{6,4},{5,7},{7,5},{8,10},{10,8},{9,1... | collective-permute-start | bytes 98312 | tf_op jit(solution)/shard_map/ppermute | solution.py:559
  92.1 3.2 %collective-permute-done.5.other_ref = bf16[64,256]{1,0:T(8,128)(2,1)S(1)} collective-permute-done((bf16[64,256]{1,0:T(8,128)(2,1)S(1)}, bf16[64,256]{1,0:T(8,128)(2,1)S(1)}, u32[]{:S(2)}, u32[]{:S(2)}) %collective-permute-start.5) | collective-permute-done | bytes 32800 | tf_op jit(solution)/shard_map/ppermute | solution.py:559
  95.3 0.8 spread.1
  96.2 3.6 %all-to-all-start.3 = ((bf16[16,64,256]{2,1,0:T(8,128)(2,1)}), bf16[16,64,256]{2,1,0:T(8,128)(2,1)S(1)}, u32[]{:S(2)}, u32[]{:S(2)}) async-start(bf16[16,64,256]{2,1,0:T(8,128)(2,1)} %spread.1), calls=%async_computation.3 | async-start | bytes 1048576 | tf_op jit(solution)/shard_map/all_to_all | solution.py:555
  99.7 0.1 reshape.81.wanted_ref
  99.8 8.1 %scatter_rows.1 = bf16[4096,256]{1,0:T(8,128)(2,1)} custom-call(s32[1,3072]{1,0:T(1,128)S(1)} %reshape.81.wanted_ref, bf16[16,256,256]{2,1,0:T(8,128)(2,1)S(1)} %all_to_all.25.returned_ref), custom_call_target="tpu_custom_call" | custom-call | flops 6442450944 | tf_op jit(solution)/shard_map/scatter_rows/pallas_call | solution.py:266
  107.9 0.5 all-to-all-done.3
  108.5 1.1 bitcast_convert_fusion
  (24 shorter events, 0.3 us)
Async XLA Ops:
  2.7 14.6 %all-to-all-start = ((s32[32,1,104]{2,1,0:T(1,128)}), s32[32,1,104]{2,1,0:T(1,128)S(1)}, u32[]{:S(2)}, u32[]{:S(2)}) async-start(s32[32,1,104]{2,1,0:T(1,128)} %bitcast.1), calls=%async_computation | async-start | bytes 32768 | tf_op jit(solution)/shard_map/all_to_all | solution.py:555
  10.1 12.8 %collective-permute-start.2 = (bf16[2,2,16,384]{3,2,1,0:T(8,128)(2,1)S(1)}, bf16[2,2,16,384]{3,2,1,0:T(8,128)(2,1)S(1)}, u32[]{:S(2)}, u32[]{:S(2)}) collective-permute-start(bf16[2,2,16,384]{3,2,1,0:T(8,128)(2,1)S(1)} %pad_maximum_fusion.4), channel_id=1, source_target_pairs={{0,2},{1,3},{2,0},{3,1},{4,6},{5,7},{6,4},{7,5},{8,10},{9,11},{10,... | collective-permute-start | bytes 147464 | tf_op jit(solution)/shard_map/ppermute | solution.py:588
  12.9 10.1 %collective-permute-start.1 = (bf16[2,2,16,384]{3,2,1,0:T(8,128)(2,1)S(1)}, bf16[2,2,16,384]{3,2,1,0:T(8,128)(2,1)S(1)}, u32[]{:S(2)}, u32[]{:S(2)}) collective-permute-start(bf16[2,2,16,384]{3,2,1,0:T(8,128)(2,1)S(1)} %pad_maximum_fusion.3), channel_id=1, source_target_pairs={{0,1},{1,0},{2,3},{3,2},{4,5},{5,4},{6,7},{7,6},{8,9},{9,8},{10,11... | collective-permute-start | bytes 147464 | tf_op jit(solution)/shard_map/ppermute | solution.py:588
  14.5 8.5 %collective-permute-start = (bf16[80,384]{1,0:T(8,128)(2,1)S(1)}, bf16[80,384]{1,0:T(8,128)(2,1)S(1)}, u32[]{:S(2)}, u32[]{:S(2)}) collective-permute-start(bf16[80,384]{1,0:T(8,128)(2,1)S(1)} %fusion.1), channel_id=1, source_target_pairs={{0,3},{1,2},{2,1},{3,0},{4,7},{5,6},{6,5},{7,4},{8,11},{9,10},{10,... | collective-permute-start | bytes 184328 | tf_op jit(solution)/shard_map/ppermute | solution.py:588
  22.9 22.9 %copy-start = (bf16[256,256]{1,0:T(8,128)(2,1)S(1)}, bf16[256,256]{1,0:T(8,128)(2,1)}, u32[]{:S(2)}) copy-start(bf16[256,256]{1,0:T(8,128)(2,1)} %wq_ref.3) | copy-start | bytes 393220
  22.9 22.9 %copy-start.1 = (bf16[256,256]{1,0:T(8,128)(2,1)S(1)}, bf16[256,256]{1,0:T(8,128)(2,1)}, u32[]{:S(2)}) copy-start(bf16[256,256]{1,0:T(8,128)(2,1)} %wo_ref.3) | copy-start | bytes 393220
  22.9 22.9 %copy-start.2 = (bf16[256,256]{1,0:T(8,128)(2,1)S(1)}, bf16[256,256]{1,0:T(8,128)(2,1)}, u32[]{:S(2)}) copy-start(bf16[256,256]{1,0:T(8,128)(2,1)} %wk_ref.7) | copy-start | bytes 393220
  22.9 22.9 %copy-start.3 = (bf16[256,256]{1,0:T(8,128)(2,1)S(1)}, bf16[256,256]{1,0:T(8,128)(2,1)}, u32[]{:S(2)}) copy-start(bf16[256,256]{1,0:T(8,128)(2,1)} %wv_ref.7) | copy-start | bytes 393220
  48.2 6.4 %collective-permute-start.4 = (f32[16,128]{1,0:T(8,128)S(1)}, f32[16,128]{1,0:T(8,128)S(1)}, u32[]{:S(2)}, u32[]{:S(2)}) collective-permute-start(f32[16,128]{1,0:T(8,128)S(1)} %get-tuple-element.48.own_ref), channel_id=1, source_target_pairs={{0,3},{1,2},{2,1},{3,0},{4,7},{5,6},{6,5},{7,4},{8,11},{9,10},{10,... | collective-permute-start | bytes 24584 | tf_op jit(solution)/shard_map/ppermute | solution.py:564
  53.5 5.5 %collective-permute-start.3 = (f32[16,128]{1,0:T(8,128)S(1)}, f32[16,128]{1,0:T(8,128)S(1)}, u32[]{:S(2)}, u32[]{:S(2)}) collective-permute-start(f32[16,128]{1,0:T(8,128)S(1)} %get-tuple-element.40.own_ref), channel_id=1, source_target_pairs={{0,3},{1,2},{2,1},{3,0},{4,7},{5,6},{6,5},{7,4},{8,11},{9,10},{10,... | collective-permute-start | bytes 24584 | tf_op jit(solution)/shard_map/ppermute | solution.py:564
  90.2 5.1 %collective-permute-start.5 = (bf16[64,256]{1,0:T(8,128)(2,1)S(1)}, bf16[64,256]{1,0:T(8,128)(2,1)S(1)}, u32[]{:S(2)}, u32[]{:S(2)}) collective-permute-start(bf16[64,256]{1,0:T(8,128)(2,1)S(1)} %slice_reduce_fusion.own_ref), channel_id=1, source_target_pairs={{0,2},{2,0},{1,3},{3,1},{4,6},{6,4},{5,7},{7,5},{8,10},{10,8},{9,1... | collective-permute-start | bytes 98312 | tf_op jit(solution)/shard_map/ppermute | solution.py:559
  96.2 12.3 %all-to-all-start.3 = ((bf16[16,64,256]{2,1,0:T(8,128)(2,1)}), bf16[16,64,256]{2,1,0:T(8,128)(2,1)S(1)}, u32[]{:S(2)}, u32[]{:S(2)}) async-start(bf16[16,64,256]{2,1,0:T(8,128)(2,1)} %spread.1), calls=%async_computation.3 | async-start | bytes 1048576 | tf_op jit(solution)/shard_map/all_to_all | solution.py:555

commit v6 on v0

v6 whole, which is shorter than its diff:
```python
import functools
import math

import jax
import jax.numpy as jnp
from jax import lax
from jax.experimental import pallas as pl
from jax.experimental.pallas import tpu as pltpu
from jax.sharding import Mesh
from jax.sharding import PartitionSpec as P

HEADS = 4
USERS_DEV = 2
PEERS = ("hi", "lo")
ALL = ("ga", "core") + PEERS
COLUMN = ("ga",) + PEERS
BY_CORE = ("core",) + COLUMN
HALF = ("ga", "core", "lo")
BF16 = jnp.bfloat16
F32 = jnp.float32
VMEM_LIMIT = 16 * 1024 * 1024
LOWEST = -1e30
LINE = 8
TILE = 768
SENDS = 4


def nt(a, b):
    return lax.dot_general(a, b, (((1,), (1,)), ((), ())), preferred_element_type=F32)


def nn(a, b):
    return jnp.dot(a, b, preferred_element_type=F32)


def cost(flops, transcendentals):
    return pl.CostEstimate(flops=flops, bytes_accessed=0, transcendentals=transcendentals)


def log2(n):
    return n.bit_length() - 1


def plan_kernel(
    rows_dev, peers, lengths_hbm, ids_hbm, requests_ref, lengths_ref, ids_ref, sems
):
    copies = [
        pltpu.make_async_copy(source, target, sems.at[k])
        for k, (source, target) in enumerate(((lengths_hbm, lengths_ref), (ids_hbm, ids_ref)))
    ]
    for copy in copies:
        copy.start()
    for copy in copies:
        copy.wait()
    users, seq = ids_ref.shape
    shards = requests_ref.shape[0]
    capacity = requests_ref.shape[1] - LINE
    block = 256
    before = (
        lax.broadcasted_iota(jnp.int32, (block, block), 0)
        < lax.broadcasted_iota(jnp.int32, (block, block), 1)
    ).astype(BF16)
    device = lax.broadcasted_iota(jnp.int32, (shards, block), 0)
    place = lax.broadcasted_iota(jnp.int32, (capacity, block), 0).astype(F32)
    lane = lax.broadcasted_iota(jnp.int32, (1, block), 1)
    count = jnp.zeros((shards, 1), F32)
    rows = jnp.zeros((3 * shards, capacity), F32)
    for user in range(users):
        for start in range(0, seq, block):
            ids = ids_ref[user : user + 1, start : start + block]
            owner = lax.shift_right_logical(ids, log2(rows_dev))
            row = ids & (rows_dev - 1)
            group = lax.shift_right_logical(owner, log2(peers))
            owner = (
                (group & 1) * (shards // 2)
                + lax.shift_right_logical(group, 1) * peers
                + (owner & (peers - 1))
            )
            live = lane + start < lengths_ref[user]
            owner = jnp.where(live, owner, shards)
            hot = (device == owner).astype(F32)
            hot_b = hot.astype(BF16)
            earlier = nn(hot_b, before) + count
            count = count + jnp.sum(hot, axis=1, keepdims=True)
            rank = jnp.sum(hot * earlier, axis=0, keepdims=True)
            ranked = (place == rank).astype(F32).astype(BF16)
            upper = lax.shift_right_logical(row, 6).astype(F32)
            lower = (row & 63).astype(F32)
            parts = jnp.concatenate([hot * upper, hot * lower, hot * float(user + 1)], axis=0)
            rows = rows + nt(parts.astype(BF16), ranked)
    row = rows[:shards] * 64.0 + rows[shards : 2 * shards]
    requests = jnp.concatenate(
        [row * 4.0 + rows[2 * shards :], jnp.broadcast_to(count, (shards, LINE))], axis=1
    )
    requests_ref[...] = requests.astype(jnp.int32)


def plan(behaviour_ids, lengths, rows_dev, shards, peers, capacity):
    operands = (lengths, behaviour_ids)
    return pl.pallas_call(
        functools.partial(plan_kernel, rows_dev, peers),
        out_shape=jax.ShapeDtypeStruct((shards, capacity + LINE), jnp.int32),
        in_specs=[pl.BlockSpec(memory_space=pltpu.HBM)] * 2,
        out_specs=pl.BlockSpec(memory_space=pltpu.VMEM),
        scratch_shapes=[
            pltpu.SMEM(lengths.shape, jnp.int32),
            pltpu.VMEM(behaviour_ids.shape, jnp.int32),
            pltpu.SemaphoreType.DMA((2,)),
        ],
        compiler_params=pltpu.CompilerParams(vmem_limit_bytes=VMEM_LIMIT),
        cost_estimate=cost(2**24, 0),
        name="plan",
    )(*(pltpu.with_memory_space_constraint(x, pltpu.HBM) for x in operands))


def gather_kernel(blocks, wanted_ref, table_hbm, *refs):
    keep, *sends, narrow, wide, in_sems = refs
    slots = 2 * keep.shape[0]
    capacity = slots // blocks
    line = capacity + LINE
    joint = 1 if capacity % 32 == 0 else math.lcm(capacity, 16) // capacity
    step = 32 if joint == 1 else joint * capacity
    halves, _, lanes = wide.shape
    loads = in_sems.shape[0]
    size = narrow.shape[0] // loads
    copies = []
    for k in range(loads):
        part = pl.ds(k * size, size)
        copies.append(pltpu.make_async_copy(table_hbm.at[part], narrow.at[part], in_sems.at[k]))
        copies[-1].start()
    for out in (keep, *sends):
        out[...] = jnp.zeros(out.shape, BF16)
    for k, copy in enumerate(copies):
        copy.wait()
        part = slice(k * size, (k + 1) * size)
        for h in range(halves):
            wide[h, part, :] = narrow[part, h * lanes : (h + 1) * lanes].astype(F32)

    def bucket(out, skip, b, carry):
        first = (skip + b) * joint * line

        def fetch(c, carry):
            at = c * step
            start = pl.multiple_of(b * joint * capacity + at, 16)
            for k in range(0, step, 16):
                ids = [wanted_ref[first + at + n + n // capacity * LINE] for n in range(k, k + 16)]
                ids = [lax.shift_right_logical(row, 2) for row in ids]
                for h in range(halves):
                    rows = [wide[h, pl.ds(row, 1), :] for row in ids]
                    out[pl.ds(start + k, 16), h * lanes : (h + 1) * lanes] = jnp.concatenate(
                        rows, axis=0
                    ).astype(BF16)
            return carry

        steps = 1 if joint > 1 else lax.div(wanted_ref[first + capacity] + step - 1, step)
        return lax.fori_loop(0, steps, fetch, carry)

    each = blocks // joint // 2
    some = each // len(sends)
    for k, send in enumerate(sends):
        lax.fori_loop(0, some, functools.partial(bucket, send, each + k * some), 0)
    lax.fori_loop(0, each, functools.partial(bucket, keep, 0), 0)


def gather(wanted, table, blocks):
    width = table.shape[1]
    slots = wanted.shape[0] - blocks * LINE
    half = jax.ShapeDtypeStruct((slots // 2, width), BF16)
    part = jax.ShapeDtypeStruct((slots // 2 // SENDS, width), BF16)
    vmem = pl.BlockSpec(memory_space=pltpu.VMEM)
    return pl.pallas_call(
        functools.partial(gather_kernel, blocks),
        out_shape=(half,) + (part,) * SENDS,
        in_specs=[
            pl.BlockSpec(memory_space=pltpu.SMEM),
            pl.BlockSpec(memory_space=pltpu.HBM),
        ],
        out_specs=(vmem,) * (1 + SENDS),
        scratch_shapes=[
            pltpu.VMEM(table.shape, BF16),
            pltpu.VMEM((width // 128, table.shape[0], 128), F32),
            pltpu.SemaphoreType.DMA((8,)),
        ],
        compiler_params=pltpu.CompilerParams(vmem_limit_bytes=VMEM_LIMIT),
        cost_estimate=cost(6 * 10**9, 0),
        name="gather_rows",
    )(wanted, pltpu.with_memory_space_constraint(table, pltpu.HBM))


def spread_kernel(own_ref, other_ref, out_ref):
    part = (own_ref[...].astype(F32) + other_ref[...].astype(F32)).astype(BF16)
    for k in range(out_ref.shape[0]):
        out_ref[k] = part


def spread(own, other, copies):
    vmem = pl.BlockSpec(memory_space=pltpu.VMEM)
    return pl.pallas_call(
        spread_kernel,
        out_shape=pltpu.VMEM((copies,) + own.shape, BF16),
        in_specs=[vmem, vmem],
        out_specs=vmem,
        compiler_params=pltpu.CompilerParams(vmem_limit_bytes=VMEM_LIMIT),
        cost_estimate=cost(own.size, 0),
        name="spread",
    )(own, other)


def scatter_kernel(wanted_ref, keep_ref, back_ref, out_ref):
    tile = out_ref.shape[0]
    block = 256
    row = lax.broadcasted_iota(jnp.int32, (tile, block), 0) + pl.program_id(0) * tile
    total = jnp.zeros(out_ref.shape, F32)
    for k, grads in enumerate((keep_ref, back_ref)):
        slots = grads.shape[0]
        for start in range(0, slots, block):
            at = k * slots + start
            hot = (row == wanted_ref[:, at : at + block]).astype(F32).astype(BF16)
            total = total + nn(hot, grads[start : start + block, :])
    out_ref[...] = total.astype(BF16)


def scatter(wanted, keep, back, rows_dev):
    slots, width = keep.shape
    tile = 1024
    return pl.pallas_call(
        scatter_kernel,
        grid=(rows_dev // tile,),
        out_shape=jax.ShapeDtypeStruct((rows_dev, width), BF16),
        in_specs=[
            pl.BlockSpec((1, 2 * slots), lambda t: (0, 0)),
            pl.BlockSpec((slots, width), lambda t: (0, 0)),
            pl.BlockSpec((slots, width), lambda t: (0, 0)),
        ],
        out_specs=pl.BlockSpec((tile, width), lambda t: (t, 0)),
        compiler_params=pltpu.CompilerParams(vmem_limit_bytes=VMEM_LIMIT),
        cost_estimate=cost(4 * rows_dev * slots * width, 0),
        name="scatter_rows",
    )(wanted, keep, back)


def by_head(x):
    head_size = x.shape[1] // HEADS
    head = lax.broadcasted_iota(jnp.int32, x.shape, 1) // head_size
    return jnp.concatenate([jnp.where(head == h, x, 0.0) for h in range(HEADS)], axis=0)


def head_sums(x):
    size = x.shape[0] // HEADS
    return jnp.concatenate(
        [jnp.sum(x[h * size : (h + 1) * size], axis=0, keepdims=True) for h in range(HEADS)], axis=0
    )


def stacked(x, live):
    return jnp.concatenate([x[:, h * live : (h + 1) * live] for h in range(HEADS)], axis=0)


def flat(x):
    return jnp.concatenate([x[h : h + 1, :] for h in range(HEADS)], axis=1)


def diagonal(x, live):
    size = x.shape[0] // HEADS
    return jnp.concatenate(
        [x[h * size : (h + 1) * size, h * live : (h + 1) * live] for h in range(HEADS)], axis=0
    )


def tn(a, b):
    return lax.dot_general(a, b, (((0,), (0,)), ((), ())), preferred_element_type=F32)


def prepare_kernel(low, *refs):
    *sources, wq_ref, wo_ref, all_ref, query_ref, out_ref, wide = refs
    groups = len(sources)
    peers, group_users, held, width = sources[0].shape
    users = group_users // peers
    num = peers * held
    scale = float(width // HEADS) ** (-0.5)
    ga = lax.axis_index("ga")
    peer = lax.axis_index("hi") * low + lax.axis_index("lo")
    for n, source in enumerate(sources):
        to = (ga ^ n) * peers
        for k in range(peers):
            first = pl.multiple_of((peer ^ k) * held, held)
            for owner in range(peers):
                for user in range(users):
                    wide[to + owner, pl.ds(first + user * num, held), :] = source[
                        k, owner * users + user
                    ].astype(F32)
    for r in range(groups * peers):
        cands = wide[r].astype(BF16)
        all_ref[r] = cands
        query_ref[r] = (nn(cands, wq_ref[...]).astype(BF16).astype(F32) * scale).astype(BF16)
        out_ref[r] = nt(cands, wo_ref[...]).astype(BF16)


def prepare(sources, low, w_query, w_out):
    groups = len(sources)
    peers, group_users, held, width = sources[0].shape
    live = group_users * held
    shape = (groups * peers, live, width)
    out = jax.ShapeDtypeStruct(shape, BF16)
    vmem = pl.BlockSpec(memory_space=pltpu.VMEM)
    return pl.pallas_call(
        functools.partial(prepare_kernel, low),
        out_shape=(out,) * 3,
        in_specs=[vmem] * (groups + 2),
        out_specs=(vmem,) * 3,
        scratch_shapes=[pltpu.VMEM(shape, F32)],
        compiler_params=pltpu.CompilerParams(vmem_limit_bytes=VMEM_LIMIT),
        cost_estimate=cost(4 * groups * peers * live * width * width, 0),
        name="prepare",
    )(*sources, w_query, w_out)


def forward_kernel(
    peers,
    low,
    keep_ref,
    lists_ref,
    other_lists_ref,
    query_ref,
    out_ref,
    labels_ref,
    wk_ref,
    wv_ref,
    *refs,
):
    *others, expo_ref, dots_ref, part_ref, rows_ref, keys_ref, values_ref = refs
    sources, both, width = rows_ref.shape
    capacity = both // 2
    live = query_ref.shape[1]
    cols = HEADS * live
    some = sources // len(others)
    group_users, held = labels_ref.shape
    users = group_users // peers
    num = peers * held
    ga = lax.axis_index("ga")
    peer = lax.axis_index("hi") * low + lax.axis_index("lo")
    here = lax.div(lax.rem(lax.broadcasted_iota(jnp.int32, (1, live), 1), num), held) == peer
    user_of = lax.rem(lax.broadcasted_iota(jnp.int32, (1, cols), 1), live) // num + 1
    user_of = user_of.astype(F32)
    flags = [
        (ref[:, :capacity] & 3).astype(F32).T if capacity % 128 == 0 else
        jnp.concatenate(
            [(ref[:, :capacity] & 3).astype(F32), jnp.zeros((sources, 128 - capacity), F32)], axis=1
        ).T
        for ref in (lists_ref, other_lists_ref)
    ]
    for r in range(sources):
        rows_ref[r, :capacity, :] = keep_ref[r]
        rows_ref[r, capacity:, :] = others[r // some][r % some]
    per_tile = TILE // both
    for t in range(sources // per_tile):
        part = slice(t * per_tile, (t + 1) * per_tile)
        rows = rows_ref[part].reshape(TILE, width)
        keys_ref[part] = nn(rows, wk_ref[...]).astype(BF16).reshape(per_tile, both, width)
        values_ref[part] = nn(rows, wv_ref[...]).astype(BF16).reshape(per_tile, both, width)
    for r in range(sources):
        query = by_head(query_ref[r].astype(F32)).astype(BF16)
        out = by_head(out_ref[r].astype(F32)).astype(BF16)
        flag = jnp.concatenate([f[:capacity, r : r + 1] for f in flags], axis=0)
        score = jnp.where(flag == user_of, nt(keys_ref[r], query), LOWEST)
        top = jnp.max(score, axis=0, keepdims=True)
        e = jnp.exp(score - top)
        norm = jnp.sum(e, axis=0, keepdims=True)
        dots = nt(values_ref[r], out)
        mixed = jnp.sum(e * dots, axis=0, keepdims=True) / norm
        expo_ref[r] = e.astype(BF16)
        dots_ref[r] = dots.astype(BF16)
        label = jnp.concatenate(
            [
                labels_ref[r % peers * users + user : r % peers * users + user + 1, :]
                for user in range(users)
                for _ in range(peers)
            ],
            axis=1,
        )
        label = jnp.where(here & (ga == r // peers), label, 0.0)
        part_ref[r] = jnp.concatenate(
            [stacked(x, live) for x in (mixed, top, norm)] + [jnp.broadcast_to(label, (4, live))], axis=0
        )


def forward(keep, other, lists, other_lists, query, out, labels, peers, w_key, w_value):
    sources, capacity, width = keep.shape
    live = query.shape[1]
    cols = HEADS * live
    both = 2 * capacity
    vmem = pl.BlockSpec(memory_space=pltpu.VMEM)
    shapes = (
        ((sources, both, cols), BF16),
        ((sources, both, cols), BF16),
        ((sources, 16, live), F32),
        ((sources, both, width), BF16),
        ((sources, both, width), BF16),
        ((sources, both, width), BF16),
    )
    return pl.pallas_call(
        functools.partial(forward_kernel, peers, peers // 2),
        out_shape=tuple(jax.ShapeDtypeStruct(*shape) for shape in shapes),
        in_specs=[vmem] * (8 + len(other)),
        out_specs=(vmem,) * len(shapes),
        compiler_params=pltpu.CompilerParams(vmem_limit_bytes=VMEM_LIMIT),
        cost_estimate=cost(8 * sources * both * width * cols, sources * both * cols),
        name="forward",
    )(keep, lists, other_lists, query, out, labels, w_key, w_value, *other)


def combine_kernel(users, root, counts_ref, parts_ref, out_ref):
    sources, _, live = parts_ref.shape
    num = live // users
    top = parts_ref[0, 4:8, :]
    for k in range(1, sources):
        top = jnp.maximum(top, parts_ref[k, 4:8, :])
    norm = jnp.zeros((HEADS, live), F32)
    dots = jnp.zeros((HEADS, live), F32)
    label = jnp.zeros((1, live), F32)
    for k in range(sources):
        label = label + parts_ref[k, 12:13, :]
        share = parts_ref[k, 8:12, :] * jnp.exp(parts_ref[k, 4:8, :] - top)
        norm = norm + share
        dots = dots + share * parts_ref[k, 0:4, :]
    inv = 1.0 / norm
    dots = dots * inv
    logit = jnp.sum(dots, axis=0, keepdims=True) / root
    index = lax.broadcasted_iota(jnp.int32, (1, live), 1)
    alive = index < 0
    for user in range(users):
        alive = alive | ((index >= user * num) & (index < user * num + counts_ref[user]))
    grad = jnp.where(alive, (jax.nn.sigmoid(logit) - label) / USERS_DEV, 0.0) / root
    result = jnp.concatenate([top, inv, dots, jnp.broadcast_to(grad, (HEADS, live))], axis=0)
    for k in range(sources):
        out_ref[k] = result


def combine(parts, cand_counts, root):
    vmem = pl.BlockSpec(memory_space=pltpu.VMEM)
    return pl.pallas_call(
        functools.partial(combine_kernel, cand_counts.shape[0], root),
        out_shape=jax.ShapeDtypeStruct(parts.shape, F32),
        in_specs=[pl.BlockSpec(memory_space=pltpu.SMEM), vmem],
        out_specs=vmem,
        compiler_params=pltpu.CompilerParams(vmem_limit_bytes=VMEM_LIMIT),
        cost_estimate=cost(64 * parts.size, parts.size),
        name="combine",
    )(cand_counts, parts)


def backward_kernel(
    total_ref,
    part_ref,
    expo_ref,
    dots_ref,
    rows_ref,
    keys_ref,
    values_ref,
    cands_ref,
    query_ref,
    out_ref,
    wk_ref,
    wv_ref,
    keep_ref,
    other_ref,
    weights_ref,
    grads,
    grad_query,
    grad_out,
    weights,
):
    sources, both, width = rows_ref.shape
    capacity = both // 2
    live = query_ref.shape[1]
    scale = float(width // HEADS) ** (-0.5)
    for r in range(sources):
        query = by_head(query_ref[r].astype(F32)).astype(BF16)
        out = by_head(out_ref[r].astype(F32)).astype(BF16)
        factor = jnp.exp(part_ref[r, 4:8, :] - total_ref[r, 0:4, :]) * total_ref[r, 4:8, :]
        factor = factor * total_ref[r, 12:16, :]
        inner = flat(total_ref[r, 8:12, :])
        probs = expo_ref[r].astype(F32) * flat(factor)
        score = (probs * (dots_ref[r].astype(F32) - inner)).astype(BF16)
        probs = probs.astype(BF16)
        grads[r * both : (r + 1) * both, :width] = nn(score, query).astype(BF16)
        grads[r * both : (r + 1) * both, width:] = nn(probs, out).astype(BF16)
        mine = slice(r * live, (r + 1) * live)
        grad_query[:, mine] = (diagonal(tn(keys_ref[r], score), live) * scale).astype(BF16)
        grad_out[:, mine] = diagonal(tn(values_ref[r], probs), live).astype(BF16)
    per_tile = TILE // both
    back = jnp.concatenate([wk_ref[...].T, wv_ref[...].T], axis=0)
    by_rows = jnp.zeros((width, 2 * width), F32)
    for t in range(sources // per_tile):
        part = grads[t * TILE : (t + 1) * TILE, :]
        rows = rows_ref[t * per_tile : (t + 1) * per_tile].reshape(TILE, width)
        by_rows = by_rows + nn(rows.T, part)
        result = nn(part, back).astype(BF16)
        for k in range(per_tile):
            at = k * both
            keep_ref[t * per_tile + k] = result[at : at + capacity]
            other_ref[t * per_tile + k] = result[at + capacity : at + both]
    cands = cands_ref[...].reshape(sources * live, width)
    weights[:width, :] = nn(grad_query[...], cands).T
    weights[width : 2 * width, :] = by_rows[:, :width]
    weights[2 * width : 3 * width, :] = by_rows[:, width:]
    weights[3 * width :, :] = nn(grad_out[...], cands)
    each = 4 * width // sources
    for k in range(sources):
        weights_ref[k] = weights[k * each : (k + 1) * each, :].astype(BF16)


def backward(total, part, expo, dots, rows, keys, values, cands, query, out, w_key, w_value):
    sources, both, width = rows.shape
    live = query.shape[1]
    vmem = pl.BlockSpec(memory_space=pltpu.VMEM)
    half = jax.ShapeDtypeStruct((sources, both // 2, width), BF16)
    weights = jax.ShapeDtypeStruct((sources, 4 * width // sources, width), BF16)
    return pl.pallas_call(
        backward_kernel,
        out_shape=(half, half, weights),
        in_specs=[vmem] * 12,
        out_specs=(vmem,) * 3,
        scratch_shapes=[
            pltpu.VMEM((sources * both, 2 * width), BF16),
            pltpu.VMEM((width, sources * live), BF16),
            pltpu.VMEM((width, sources * live), BF16),
            pltpu.VMEM((4 * width, width), F32),
        ],
        compiler_params=pltpu.CompilerParams(vmem_limit_bytes=VMEM_LIMIT),
        cost_estimate=cost(16 * sources * both * width * HEADS * live, sources * both * live),
        name="backward",
    )(total, part, expo, dots, rows, keys, values, cands, query, out, w_key, w_value)


def exchange(x, axes):
    return lax.all_to_all(x, axes, split_axis=0, concat_axis=0, tiled=True)


def swap_cores(x):
    return lax.ppermute(x, "core", [(0, 1), (1, 0)])


def swap_halves(x):
    return lax.ppermute(x, "hi", [(0, 1), (1, 0)])


def gather_column(mine):
    peers, groups = lax.axis_size(PEERS), lax.axis_size("ga")
    line = jnp.stack(
        [mine]
        + [lax.ppermute(mine, PEERS, [(i, i ^ k) for i in range(peers)]) for k in range(1, peers)]
    )
    return [line] + [
        lax.ppermute(line, "ga", [(i, i ^ k) for i in range(groups)]) for k in range(1, groups)
    ]


def local(
    table, behaviour_ids, lengths, candidates, labels, cand_counts, w_query, w_key, w_value, w_out
):
    shards, peers = lax.axis_size(ALL), lax.axis_size(PEERS)
    sources = shards // 2
    first = lax.axis_index("core") == 0
    users, seq = behaviour_ids.shape
    rows_dev, width = table.shape
    total = users * seq
    capacity = total // shards + total // (2 * shards)
    held = candidates.shape[1]
    num = held * peers

    requests = plan(behaviour_ids, lengths, rows_dev, shards, peers, capacity)
    wanted = exchange(requests, BY_CORE).reshape(2, sources, capacity + LINE)
    wanted = jnp.where(first, wanted, wanted[::-1])

    column = gather_column(candidates)

    keep, *sends = gather(wanted.reshape(-1), table, shards)
    other = [swap_cores(send).reshape(-1, capacity, width) for send in sends]
    other_lists = swap_cores(wanted[1])
    keep = keep.reshape(sources, capacity, width)

    all_cands, query, out = prepare(column, lax.axis_size("lo"), w_query, w_out)
    keep, other, own_lists, other_lists = lax.optimization_barrier(
        (keep, other, wanted[0], other_lists)
    )
    expo, dots, part, rows, keys, values = forward(
        keep, other, own_lists, other_lists, query, out, labels, peers, w_key, w_value
    )
    summed = combine(exchange(part, COLUMN), cand_counts, float(width) ** 0.5)
    summed = exchange(summed, COLUMN)
    grad_keep, grad_other, weights = backward(
        summed, part, expo, dots, rows, keys, values, all_cands, query, out, w_key, w_value
    )
    back = swap_cores(grad_other)
    slots = sources * capacity
    place = lax.shift_right_logical(wanted[:, :, :capacity], 2).reshape(1, 2 * slots)
    table_grad = scatter(place, grad_keep.reshape(slots, width), back.reshape(slots, width), rows_dev)

    part = jnp.sum(exchange(weights, HALF).astype(F32), axis=0).astype(BF16)
    weight_grads = exchange(spread(part, swap_halves(part), sources), HALF)
    return table_grad, weight_grads.reshape(4, width, width).astype(F32)


def solution(mesh):
    groups, peers = mesh.shape["group"], mesh.shape["peer"]
    mesh = Mesh(mesh.devices.reshape(groups // 2, 2, 2, peers // 2), ALL)
    in_specs = (
        P(ALL, None),
        P(ALL, None),
        P(ALL),
        P(("ga", "core"), PEERS, None),
        P(("ga", "core"), PEERS),
        P(ALL),
        P(),
        P(),
        P(),
        P(),
    )
    out_specs = (P(ALL, None), P())
    return jax.shard_map(local, mesh=mesh, in_specs=in_specs, out_specs=out_specs, check_vma=False)
```

time: 377 us -> 105 us (0.28)
  waiting for transfers between devices: 172 us -> 27 us
  local copies, waits for them, and re-layouts: 79.8 us -> 0.21 us
  other arithmetic: 53.3 us -> 1.18 us
  matrix products: 33.4 us -> 0 us
  Pallas kernels: 0 us -> 29.5 us
  blocking collectives: 0 us -> 21.2 us
  between operations: 14.4 us -> 0.84 us
    psum x1 -> x0, waiting for transfers between devices: 135 us -> none  [local(): lax.psum(jnp.stack([grad_wq, grad_wk, grad_wv, grad_wo]), ('group', 'peer'))]
    gather x6 -> x0, local copies, waits for them, and re-layouts: 46.3 us -> none  [the longest x1 13 us: local(): served = table[wanted.reshape(-1)].reshape(shards, capacity, width)]
    dot_general x16 -> x0, matrix products: 30 us -> none  [the longest x1 7.07 us: local(): jnp.einsum('uhcl,uchd->ulhd', grad_scores, q_heads, preferred_element_typ...]
    pallas_call x0 -> x8, Pallas kernels: none -> 29.5 us  [the longest x1 8 us: scatter(): pl.pallas_call(scatter_kernel, grid=(rows_dev // tile,), out_shape=jax.Sh...]
    scatter x3 -> x0, local copies, waits for them, and re-layouts: 27.3 us -> none  [the longest x1 11 us: local(): outgoing = jnp.zeros((shards * capacity, width), jnp.bfloat16).at[positio...]
    all_to_all x5 -> x3, waiting for transfers between devices: 36.6 us -> 11.8 us  [exchange(): return lax.all_to_all(x, axes, split_axis=0, concat_axis=0, tiled=True)]
    all_to_all x0 -> x2, blocking collectives: none -> 21.2 us  [exchange(): return lax.all_to_all(x, axes, split_axis=0, concat_axis=0, tiled=True)]
    scatter-add x1 -> x0, other arithmetic: 19.6 us -> none  [local(): table_sum = jnp.zeros((table.shape[0], width), jnp.float32).at[wanted.res...]
  transfers between devices with their start and end apart: 6 -> 16, of which waited for: 4 -> 8; matrix products, arithmetic and copies ran while one was open for 10% -> 0% of each run, Pallas kernels for 0% -> 14%
where the time goes in v6:
time: 105 us
  Pallas kernels  29.5 us (28%)
  waiting for transfers between devices  27 us (26%)
  starting transfers between devices  24.5 us (23%)
  blocking collectives  21.2 us (20%)
  other arithmetic  1.18 us (1%)
    all_to_all x2, blocking collectives, exchange(): return lax.all_to_all(x, axes, split_axis=0, concat_axis=0, tiled=True)  21.2 us
    all_to_all x3, starting transfers between devices, exchange(): return lax.all_to_all(x, axes, split_axis=0, concat_axis=0, tiled=True)  14.5 us
    all_to_all x3, waiting for transfers between devices, exchange(): return lax.all_to_all(x, axes, split_axis=0, concat_axis=0, tiled=True)  11.8 us
    ppermute x3, waiting for transfers between devices, gather_column(): lax.ppermute(line, 'ga', [(i, i ^ k) for i in range(groups)])  9.57 us
    pallas_call x1, Pallas kernels, scatter(): pl.pallas_call(scatter_kernel, grid=(rows_dev // tile,), out_shape=jax.Sh...  8 us
    pallas_call x1, Pallas kernels, backward(): pl.pallas_call(backward_kernel, out_shape=(half, half, weights), in_specs...  7.28 us
    pallas_call x1, Pallas kernels, gather(): pl.pallas_call(functools.partial(gather_kernel, blocks), out_shape=(half,...  5.39 us
    ppermute x1, waiting for transfers between devices, swap_halves(): return lax.ppermute(x, 'hi', [(0, 1), (1, 0)])  4.38 us
  transfers between devices with their start and end apart: 16, of which 8 were waited for; matrix products, arithmetic and copies ran while one was open for 0% of the time, Pallas kernels for 14%

profile of v6, /device:TPU:0, one launch (start us, length us, event | category | flops | bytes accessed | tf_op | source)
XLA Modules:
  0.0 104.5 jit_solution(2686384346858488428)
XLA Ops:
  0.6 1.9 %plan.1 = s32[32,104]{1,0:T(8,128)} custom-call(s32[2]{0:T(128)} %lengths_hbm.1, s32[2,1024]{1,0:T(2,128)} %ids_hbm.1), custom_call_target="tpu_custom_call" | custom-call | flops 16777216 | tf_op jit(solution)/shard_map/plan/pallas_call | solution.py:100
  2.5 7.3 %all-to-all-start = ((s32[32,1,104]{2,1,0:T(1,128)}), s32[32,1,104]{2,1,0:T(1,128)S(1)}, u32[]{:S(2)}, u32[]{:S(2)}) async-start(s32[32,1,104]{2,1,0:T(1,128)} %bitcast.1), calls=%async_computation | async-start | bytes 32768 | tf_op jit(solution)/shard_map/all_to_all | solution.py:537
  9.8 1.8 %collective-permute-start.5 = (bf16[8,16,256]{2,1,0:T(8,128)(2,1)}, bf16[8,16,256]{2,1,0:T(8,128)(2,1)S(1)}, u32[]{:S(2)}, u32[]{:S(2)}) collective-permute-start(bf16[8,16,256]{2,1,0:T(8,128)(2,1)} %param.13), channel_id=1, source_target_pairs={{0,1},{1,0},{2,3},{3,2},{4,5},{5,4},{6,7},{7,6},{8,9},{9,8},{10,11... | collective-permute-start | bytes 196616 | tf_op jit(solution)/shard_map/ppermute | solution.py:552
  11.7 2.4 %collective-permute-start.7 = (bf16[8,16,256]{2,1,0:T(8,128)(2,1)}, bf16[8,16,256]{2,1,0:T(8,128)(2,1)S(1)}, u32[]{:S(2)}, u32[]{:S(2)}) collective-permute-start(bf16[8,16,256]{2,1,0:T(8,128)(2,1)} %param.13), channel_id=1, source_target_pairs={{0,3},{1,2},{2,1},{3,0},{4,7},{5,6},{6,5},{7,4},{8,11},{9,10},{10,... | collective-permute-start | bytes 196616 | tf_op jit(solution)/shard_map/ppermute | solution.py:552
  14.1 2.9 %all-to-all-done = s32[32,1,104]{2,1,0:T(1,128)S(1)} async-done(((s32[32,1,104]{2,1,0:T(1,128)}), s32[32,1,104]{2,1,0:T(1,128)S(1)}, u32[]{:S(2)}, u32[]{:S(2)}) %all-to-all-start) | async-done | bytes 13344 | tf_op jit(solution)/shard_map/all_to_all | solution.py:537
  17.1 5.4 %gather_rows.1 = (bf16[1536,256]{1,0:T(8,128)(2,1)S(1)}, bf16[384,256]{1,0:T(8,128)(2,1)S(1)}, bf16[384,256]{1,0:T(8,128)(2,1)S(1)}, bf16[384,256]{1,0:T(8,128)(2,1)S(1)}, bf16[384,256]{1,0:T(8,128)(2,1)S(1)}) custom-call(s32[3328]{0:T(1024)S(1)} %reshape.42.wanted_ref, bf16[4096,256]{1,0:T(8,128)(2,1)} %table_hbm.1), custom_call_target="tpu_custom_call" | custom-call | flops 6000000000 | tf_op jit(solution)/shard_map/gather_rows/pallas_call | solution.py:171
  22.6 0.5 collective-permute-start.1
  23.2 0.9 collective-permute-start.10
  24.1 1.5 %collective-permute-start.9 = (bf16[4,8,16,256]{3,2,1,0:T(8,128)(2,1)S(1)}, bf16[4,8,16,256]{3,2,1,0:T(8,128)(2,1)S(1)}, u32[]{:S(2)}, u32[]{:S(2)}) collective-permute-start(bf16[4,8,16,256]{3,2,1,0:T(8,128)(2,1)S(1)} %pad_maximum_fusion.refs_0_), channel_id=1, source_target_pairs={{0,16},{8,24},{16,0},{24,8},{1,17},{9,25},{17,1},{25,9},{2,18},{10... | collective-permute-start | bytes 786440 | tf_op jit(solution)/shard_map/ppermute | solution.py:555
  25.6 1.2 %collective-permute-start.8 = (bf16[4,8,16,256]{3,2,1,0:T(8,128)(2,1)S(1)}, bf16[4,8,16,256]{3,2,1,0:T(8,128)(2,1)S(1)}, u32[]{:S(2)}, u32[]{:S(2)}) collective-permute-start(bf16[4,8,16,256]{3,2,1,0:T(8,128)(2,1)S(1)} %pad_maximum_fusion.refs_0_), channel_id=1, source_target_pairs={{0,8},{8,0},{16,24},{24,16},{1,9},{9,1},{17,25},{25,17},{2,10},{10... | collective-permute-start | bytes 786440 | tf_op jit(solution)/shard_map/ppermute | solution.py:555
  26.8 0.5 collective-permute-start.3
  27.3 0.9 collective-permute-done.2
  28.2 0.3 collective-permute-done.3
  28.5 4.8 %collective-permute-done.10.refs_3_ = bf16[4,8,16,256]{3,2,1,0:T(8,128)(2,1)S(1)} collective-permute-done((bf16[4,8,16,256]{3,2,1,0:T(8,128)(2,1)S(1)}, bf16[4,8,16,256]{3,2,1,0:T(8,128)(2,1)S(1)}, u32[]{:S(2)}, u32[]{:S(2)}) %collective-permute-start.10) | collective-permute-done | bytes 262176 | tf_op jit(solution)/shard_map/ppermute | solution.py:555
  33.3 4.7 %collective-permute-done.9.refs_2_ = bf16[4,8,16,256]{3,2,1,0:T(8,128)(2,1)S(1)} collective-permute-done((bf16[4,8,16,256]{3,2,1,0:T(8,128)(2,1)S(1)}, bf16[4,8,16,256]{3,2,1,0:T(8,128)(2,1)S(1)}, u32[]{:S(2)}, u32[]{:S(2)}) %collective-permute-start.9) | collective-permute-done | bytes 262176 | tf_op jit(solution)/shard_map/ppermute | solution.py:555
  38.1 1.3 %prepare.1 = (bf16[16,128,256]{2,1,0:T(8,128)(2,1)S(1)}, bf16[16,128,256]{2,1,0:T(8,128)(2,1)S(1)}, bf16[16,128,256]{2,1,0:T(8,128)(2,1)S(1)}) custom-call(bf16[4,8,16,256]{3,2,1,0:T(8,128)(2,1)S(1)} %pad_maximum_fusion.refs_0_, bf16[4,8,16,256]{3,2,1,0:T(8,128)(2,1)S(1)} %collective-permute-done.8.refs_1_, ...), custom_call_target="tpu_custom_call" | custom-call | flops 536870912 | tf_op jit(solution)/shard_map/prepare/pallas_call | solution.py:306
  39.5 4.2 %forward.1 = (bf16[16,192,512]{2,1,0:T(8,128)(2,1)S(1)}, bf16[16,192,512]{2,1,0:T(8,128)(2,1)S(1)}, f32[16,16,128]{2,1,0:T(8,128)S(1)}, bf16[16,192,256]{2,1,0:T...) custom-call(bf16[16,96,256]{2,1,0:T(8,128)(2,1)S(1)} %bitcast.28, ...), custom_call_target="tpu_custom_call" | custom-call | flops 3221225472 | tf_op jit(solution)/shard_map/forward/pallas_call | solution.py:401
  43.7 10.9 %all_to_all.29.parts_ref = f32[16,16,128]{2,1,0:T(8,128)S(1)} all-to-all(f32[16,16,128]{2,1,0:T(8,128)S(1)} %get-tuple-element.40.part_ref), channel_id=1, replica_groups=mesh['ga'=4,'core'=2,'hi'=2,'lo'=2] {'ga','hi','lo'}, dimensions={0} | all-to-all | bytes 262144 | tf_op jit(solution)/shard_map/all_to_all | solution.py:537
  54.5 0.6 combine.1
  55.2 10.4 %all_to_all.30.total_ref = f32[16,16,128]{2,1,0:T(8,128)S(1)} all-to-all(f32[16,16,128]{2,1,0:T(8,128)S(1)} %combine.1), channel_id=1, replica_groups=mesh['ga'=4,'core'=2,'hi'=2,'lo'=2] {'ga','hi','lo'}, dimensions={0} | all-to-all | bytes 262144 | tf_op jit(solution)/shard_map/all_to_all | solution.py:537
  65.5 7.3 %backward.1 = (bf16[16,96,256]{2,1,0:T(8,128)(2,1)S(1)}, bf16[16,96,256]{2,1,0:T(8,128)(2,1)S(1)}, bf16[16,64,256]{2,1,0:T(8,128)(2,1)}) custom-call(f32[16,16,128]{2,1,0:T(8,128)S(1)} %all_to_all.30.total_ref, f32[16,16,128]{2,1,0:T(8,128)S(1)} %get-tuple-element.40.part_ref, bf16[16,192,512]{2,1,0:T(8,128)(2,1)S(1)} %get-tuple-element.41.expo_ref, ...), custom_call_target="tpu_custom_call" | custom-call | flops 6442450944 | tf_op jit(solution)/shard_map/backward/pallas_call | solution.py:519
  72.8 3.6 %all-to-all-start.3 = ((bf16[16,64,256]{2,1,0:T(8,128)(2,1)}), bf16[16,64,256]{2,1,0:T(8,128)(2,1)S(1)}, u32[]{:S(2)}, u32[]{:S(2)}) async-start(bf16[16,64,256]{2,1,0:T(8,128)(2,1)} %get-tuple-element.49), calls=%async_computation.3 | async-start | bytes 1048576 | tf_op jit(solution)/shard_map/all_to_all | solution.py:537
  76.4 0.3 collective-permute-start.11
  76.7 8.3 %all-to-all-done.3 = bf16[16,64,256]{2,1,0:T(8,128)(2,1)S(1)} async-done(((bf16[16,64,256]{2,1,0:T(8,128)(2,1)}), bf16[16,64,256]{2,1,0:T(8,128)(2,1)S(1)}, u32[]{:S(2)}, u32[]{:S(2)}) %all-to-all-start.3) | async-done | bytes 524320 | tf_op jit(solution)/shard_map/all_to_all | solution.py:537
  85.1 0.8 collective-permute-start.12
  85.9 4.4 %collective-permute-done.12.other_ref = bf16[64,256]{1,0:T(8,128)(2,1)S(1)} collective-permute-done((bf16[64,256]{1,0:T(8,128)(2,1)S(1)}, bf16[64,256]{1,0:T(8,128)(2,1)S(1)}, u32[]{:S(2)}, u32[]{:S(2)}) %collective-permute-start.12) | collective-permute-done | bytes 32800 | tf_op jit(solution)/shard_map/ppermute | solution.py:545
  90.2 0.8 spread.1
  91.1 3.6 %all-to-all-start.4 = ((bf16[16,64,256]{2,1,0:T(8,128)(2,1)}), bf16[16,64,256]{2,1,0:T(8,128)(2,1)S(1)}, u32[]{:S(2)}, u32[]{:S(2)}) async-start(bf16[16,64,256]{2,1,0:T(8,128)(2,1)} %spread.1), calls=%async_computation.4 | async-start | bytes 1048576 | tf_op jit(solution)/shard_map/all_to_all | solution.py:537
  94.7 0.1 reshape.41.wanted_ref
  94.8 8.0 %scatter_rows.1 = bf16[4096,256]{1,0:T(8,128)(2,1)} custom-call(s32[1,3072]{1,0:T(1,128)S(1)} %reshape.41.wanted_ref, bf16[1536,256]{1,0:T(8,128)(2,1)S(1)} %bitcast.29, bf16[1536,256]{1,0:T(8,128)(2,1)S(1)} %bitcast.23), custom_call_target="tpu_custom_call" | custom-call | flops 6442450944 | tf_op jit(solution)/shard_map/scatter_rows/pallas_call | solution.py:226
  102.8 0.6 all-to-all-done.4
  103.5 1.1 %bitcast_convert_fusion = f32[4,256,256]{2,1,0:T(8,128)} fusion(bf16[4,256,256]{2,1,0:T(8,128)(2,1)S(1)} %bitcast.30), kind=kLoop, calls=%fused_computation | loop fusion | flops 262144 | bytes 1572864 | tf_op jit(solution)/shard_map/convert_element_type | solution.py:602
  (32 shorter events, 0.5 us)
Async XLA Ops:
  2.5 14.4 %all-to-all-start = ((s32[32,1,104]{2,1,0:T(1,128)}), s32[32,1,104]{2,1,0:T(1,128)S(1)}, u32[]{:S(2)}, u32[]{:S(2)}) async-start(s32[32,1,104]{2,1,0:T(1,128)} %bitcast.1), calls=%async_computation | async-start | bytes 32768 | tf_op jit(solution)/shard_map/all_to_all | solution.py:537
  9.8 13.3 %collective-permute-start.5 = (bf16[8,16,256]{2,1,0:T(8,128)(2,1)}, bf16[8,16,256]{2,1,0:T(8,128)(2,1)S(1)}, u32[]{:S(2)}, u32[]{:S(2)}) collective-permute-start(bf16[8,16,256]{2,1,0:T(8,128)(2,1)} %param.13), channel_id=1, source_target_pairs={{0,1},{1,0},{2,3},{3,2},{4,5},{5,4},{6,7},{7,6},{8,9},{9,8},{10,11... | collective-permute-start | bytes 196616 | tf_op jit(solution)/shard_map/ppermute | solution.py:552
  11.7 11.5 %collective-permute-start.7 = (bf16[8,16,256]{2,1,0:T(8,128)(2,1)}, bf16[8,16,256]{2,1,0:T(8,128)(2,1)S(1)}, u32[]{:S(2)}, u32[]{:S(2)}) collective-permute-start(bf16[8,16,256]{2,1,0:T(8,128)(2,1)} %param.13), channel_id=1, source_target_pairs={{0,3},{1,2},{2,1},{3,0},{4,7},{5,6},{6,5},{7,4},{8,11},{9,10},{10,... | collective-permute-start | bytes 196616 | tf_op jit(solution)/shard_map/ppermute | solution.py:552
  14.0 9.1 %collective-permute-start.6 = (bf16[8,16,256]{2,1,0:T(8,128)(2,1)}, bf16[8,16,256]{2,1,0:T(8,128)(2,1)S(1)}, u32[]{:S(2)}, u32[]{:S(2)}) collective-permute-start(bf16[8,16,256]{2,1,0:T(8,128)(2,1)} %param.13), channel_id=1, source_target_pairs={{0,2},{1,3},{2,0},{3,1},{4,6},{5,7},{6,4},{7,5},{8,10},{9,11},{10,... | collective-permute-start | bytes 196616 | tf_op jit(solution)/shard_map/ppermute | solution.py:552
  17.0 6.1 %copy-start.6 = (bf16[8,16,256]{2,1,0:T(8,128)(2,1)S(1)}, bf16[8,16,256]{2,1,0:T(8,128)(2,1)}, u32[]{:S(2)}) copy-start(bf16[8,16,256]{2,1,0:T(8,128)(2,1)} %param.13) | copy-start | bytes 196612
  17.0 21.0 %copy-start.1 = (bf16[256,256]{1,0:T(8,128)(2,1)S(1)}, bf16[256,256]{1,0:T(8,128)(2,1)}, u32[]{:S(2)}) copy-start(bf16[256,256]{1,0:T(8,128)(2,1)} %refs_4_.1) | copy-start | bytes 393220
  17.1 21.0 %copy-start.2 = (bf16[256,256]{1,0:T(8,128)(2,1)S(1)}, bf16[256,256]{1,0:T(8,128)(2,1)}, u32[]{:S(2)}) copy-start(bf16[256,256]{1,0:T(8,128)(2,1)} %refs_5_.1) | copy-start | bytes 393220
  22.5 16.9 %copy-start.3 = (bf16[256,256]{1,0:T(8,128)(2,1)S(1)}, bf16[256,256]{1,0:T(8,128)(2,1)}, u32[]{:S(2)}) copy-start(bf16[256,256]{1,0:T(8,128)(2,1)} %wk_ref.3) | copy-start | bytes 393220
  22.5 16.9 %copy-start.4 = (bf16[256,256]{1,0:T(8,128)(2,1)S(1)}, bf16[256,256]{1,0:T(8,128)(2,1)}, u32[]{:S(2)}) copy-start(bf16[256,256]{1,0:T(8,128)(2,1)} %wv_ref.3) | copy-start | bytes 393220
  22.5 16.9 %copy-start.5 = (f32[8,16]{1,0:T(8,128)S(1)}, f32[8,16]{1,0:T(8,128)}, u32[]{:S(2)}) copy-start(f32[8,16]{1,0:T(8,128)} %labels_ref.1) | copy-start | bytes 1540
  22.5 4.3 %collective-permute-start = (bf16[384,256]{1,0:T(8,128)(2,1)S(1)}, bf16[384,256]{1,0:T(8,128)(2,1)S(1)}, u32[]{:S(2)}, u32[]{:S(2)}) collective-permute-start(bf16[384,256]{1,0:T(8,128)(2,1)S(1)} %get-tuple-element.27), channel_id=1, source_target_pairs={{0,4},{4,0},{1,5},{5,1},{2,6},{6,2},{3,7},{7,3},{8,12},{12,8},{9,1... | collective-permute-start | bytes 589832 | tf_op jit(solution)/shard_map/ppermute | solution.py:541
  22.6 4.2 %collective-permute-start.1 = (bf16[384,256]{1,0:T(8,128)(2,1)S(1)}, bf16[384,256]{1,0:T(8,128)(2,1)S(1)}, u32[]{:S(2)}, u32[]{:S(2)}) collective-permute-start(bf16[384,256]{1,0:T(8,128)(2,1)S(1)} %get-tuple-element.28), channel_id=1, source_target_pairs={{0,4},{4,0},{1,5},{5,1},{2,6},{6,2},{3,7},{7,3},{8,12},{12,8},{9,1... | collective-permute-start | bytes 589832 | tf_op jit(solution)/shard_map/ppermute | solution.py:541
  23.1 2.5 %collective-permute-start.4 = (s32[16,104]{1,0:T(8,128)S(1)}, s32[16,104]{1,0:T(8,128)S(1)}, u32[]{:S(2)}, u32[]{:S(2)}) collective-permute-start(s32[16,104]{1,0:T(8,128)S(1)} %get-tuple-element.50), channel_id=1, source_target_pairs={{0,4},{4,0},{1,5},{5,1},{2,6},{6,2},{3,7},{7,3},{8,12},{12,8},{9,1... | collective-permute-start | bytes 19976 | tf_op jit(solution)/shard_map/ppermute | solution.py:541
  23.2 10.1 %collective-permute-start.10 = (bf16[4,8,16,256]{3,2,1,0:T(8,128)(2,1)S(1)}, bf16[4,8,16,256]{3,2,1,0:T(8,128)(2,1)S(1)}, u32[]{:S(2)}, u32[]{:S(2)}) collective-permute-start(bf16[4,8,16,256]{3,2,1,0:T(8,128)(2,1)S(1)} %pad_maximum_fusion.refs_0_), channel_id=1, source_target_pairs={{0,24},{8,16},{16,8},{24,0},{1,25},{9,17},{17,9},{25,1},{2,26},{10... | collective-permute-start | bytes 786440 | tf_op jit(solution)/shard_map/ppermute | solution.py:555
  24.1 14.0 %collective-permute-start.9 = (bf16[4,8,16,256]{3,2,1,0:T(8,128)(2,1)S(1)}, bf16[4,8,16,256]{3,2,1,0:T(8,128)(2,1)S(1)}, u32[]{:S(2)}, u32[]{:S(2)}) collective-permute-start(bf16[4,8,16,256]{3,2,1,0:T(8,128)(2,1)S(1)} %pad_maximum_fusion.refs_0_), channel_id=1, source_target_pairs={{0,16},{8,24},{16,0},{24,8},{1,17},{9,25},{17,1},{25,9},{2,18},{10... | collective-permute-start | bytes 786440 | tf_op jit(solution)/shard_map/ppermute | solution.py:555
  25.6 12.5 %collective-permute-start.8 = (bf16[4,8,16,256]{3,2,1,0:T(8,128)(2,1)S(1)}, bf16[4,8,16,256]{3,2,1,0:T(8,128)(2,1)S(1)}, u32[]{:S(2)}, u32[]{:S(2)}) collective-permute-start(bf16[4,8,16,256]{3,2,1,0:T(8,128)(2,1)S(1)} %pad_maximum_fusion.refs_0_), channel_id=1, source_target_pairs={{0,8},{8,0},{16,24},{24,16},{1,9},{9,1},{17,25},{25,17},{2,10},{10... | collective-permute-start | bytes 786440 | tf_op jit(solution)/shard_map/ppermute | solution.py:555
  26.8 1.4 %collective-permute-start.2 = (bf16[384,256]{1,0:T(8,128)(2,1)S(1)}, bf16[384,256]{1,0:T(8,128)(2,1)S(1)}, u32[]{:S(2)}, u32[]{:S(2)}) collective-permute-start(bf16[384,256]{1,0:T(8,128)(2,1)S(1)} %get-tuple-element.29), channel_id=1, source_target_pairs={{0,4},{4,0},{1,5},{5,1},{2,6},{6,2},{3,7},{7,3},{8,12},{12,8},{9,1... | collective-permute-start | bytes 589832 | tf_op jit(solution)/shard_map/ppermute | solution.py:541
  26.8 1.7 %collective-permute-start.3 = (bf16[384,256]{1,0:T(8,128)(2,1)S(1)}, bf16[384,256]{1,0:T(8,128)(2,1)S(1)}, u32[]{:S(2)}, u32[]{:S(2)}) collective-permute-start(bf16[384,256]{1,0:T(8,128)(2,1)S(1)} %get-tuple-element.30), channel_id=1, source_target_pairs={{0,4},{4,0},{1,5},{5,1},{2,6},{6,2},{3,7},{7,3},{8,12},{12,8},{9,1... | collective-permute-start | bytes 589832 | tf_op jit(solution)/shard_map/ppermute | solution.py:541
  39.4 15.1 %copy-start = (s32[2]{0:T(128)S(1)}, s32[2]{0:T(128)}, u32[]{:S(2)}) copy-start(s32[2]{0:T(128)} %counts_ref.1) | copy-start | bytes 28
  72.8 12.2 %all-to-all-start.3 = ((bf16[16,64,256]{2,1,0:T(8,128)(2,1)}), bf16[16,64,256]{2,1,0:T(8,128)(2,1)S(1)}, u32[]{:S(2)}, u32[]{:S(2)}) async-start(bf16[16,64,256]{2,1,0:T(8,128)(2,1)} %get-tuple-element.49), calls=%async_computation.3 | async-start | bytes 1048576 | tf_op jit(solution)/shard_map/all_to_all | solution.py:537
  76.4 18.4 %collective-permute-start.11 = (bf16[16,96,256]{2,1,0:T(8,128)(2,1)S(1)}, bf16[16,96,256]{2,1,0:T(8,128)(2,1)S(1)}, u32[]{:S(2)}, u32[]{:S(2)}) collective-permute-start(bf16[16,96,256]{2,1,0:T(8,128)(2,1)S(1)} %get-tuple-element.48), channel_id=1, source_target_pairs={{0,4},{4,0},{1,5},{5,1},{2,6},{6,2},{3,7},{7,3},{8,12},{12,8},{9,1... | collective-permute-start | bytes 2359304 | tf_op jit(solution)/shard_map/ppermute | solution.py:541
  85.1 5.2 %collective-permute-start.12 = (bf16[64,256]{1,0:T(8,128)(2,1)S(1)}, bf16[64,256]{1,0:T(8,128)(2,1)S(1)}, u32[]{:S(2)}, u32[]{:S(2)}) collective-permute-start(bf16[64,256]{1,0:T(8,128)(2,1)S(1)} %reduce_sum.12.own_ref), channel_id=1, source_target_pairs={{0,2},{2,0},{1,3},{3,1},{4,6},{6,4},{5,7},{7,5},{8,10},{10,8},{9,1... | collective-permute-start | bytes 98312 | tf_op jit(solution)/shard_map/ppermute | solution.py:545
  91.1 12.4 %all-to-all-start.4 = ((bf16[16,64,256]{2,1,0:T(8,128)(2,1)}), bf16[16,64,256]{2,1,0:T(8,128)(2,1)S(1)}, u32[]{:S(2)}, u32[]{:S(2)}) async-start(bf16[16,64,256]{2,1,0:T(8,128)(2,1)} %spread.1), calls=%async_computation.4 | async-start | bytes 1048576 | tf_op jit(solution)/shard_map/all_to_all | solution.py:537

commit v7 on v6

--- a/solution.py
+++ b/solution.py
@@ -22,7 +22,7 @@
 LOWEST = -1e30
 LINE = 8
 TILE = 768
-SENDS = 4
+SENDS = 2
 
 
 def nt(a, b):
@@ -92,7 +92,8 @@
     requests = jnp.concatenate(
         [row * 4.0 + rows[2 * shards :], jnp.broadcast_to(count, (shards, LINE))], axis=1
     )
-    requests_ref[...] = requests.astype(jnp.int32)
+    other = jnp.concatenate([requests[shards // 2 :], requests[: shards // 2]], axis=0)
+    requests_ref[...] = requests.astype(jnp.int32) + other.astype(jnp.int32) * 65536
 
 
 def plan(behaviour_ids, lengths, rows_dev, shards, peers, capacity):
@@ -545,12 +546,16 @@
     return lax.ppermute(x, "hi", [(0, 1), (1, 0)])
 
 
-def gather_column(mine):
-    peers, groups = lax.axis_size(PEERS), lax.axis_size("ga")
-    line = jnp.stack(
+def gather_line(mine):
+    peers = lax.axis_size(PEERS)
+    return jnp.stack(
         [mine]
         + [lax.ppermute(mine, PEERS, [(i, i ^ k) for i in range(peers)]) for k in range(1, peers)]
     )
+
+
+def gather_column(line):
+    groups = lax.axis_size("ga")
     return [line] + [
         lax.ppermute(line, "ga", [(i, i ^ k) for i in range(groups)]) for k in range(1, groups)
     ]
@@ -572,12 +577,15 @@
     requests = plan(behaviour_ids, lengths, rows_dev, shards, peers, capacity)
     wanted = exchange(requests, BY_CORE).reshape(2, sources, capacity + LINE)
     wanted = jnp.where(first, wanted, wanted[::-1])
-
-    column = gather_column(candidates)
+    other_lists = lax.shift_right_logical(wanted[0], 16)
+    wanted = wanted & 65535
+
+    line = gather_line(candidates)
+    wanted, line = lax.optimization_barrier((wanted, line))
+    column = gather_column(line)
 
     keep, *sends = gather(wanted.reshape(-1), table, shards)
     other = [swap_cores(send).reshape(-1, capacity, width) for send in sends]
-    other_lists = swap_cores(wanted[1])
     keep = keep.reshape(sources, capacity, width)
 
     all_cands, query, out = prepare(column, lax.axis_size("lo"), w_query, w_out)
@@ -592,12 +600,14 @@
     grad_keep, grad_other, weights = backward(
         summed, part, expo, dots, rows, keys, values, all_cands, query, out, w_key, w_value
     )
+    shares = exchange(weights, HALF)
+    shares, grad_other = lax.optimization_barrier((shares, grad_other))
     back = swap_cores(grad_other)
     slots = sources * capacity
     place = lax.shift_right_logical(wanted[:, :, :capacity], 2).reshape(1, 2 * slots)
     table_grad = scatter(place, grad_keep.reshape(slots, width), back.reshape(slots, width), rows_dev)
 
-    part = jnp.sum(exchange(weights, HALF).astype(F32), axis=0).astype(BF16)
+    part = jnp.sum(shares.astype(F32), axis=0).astype(BF16)
     weight_grads = exchange(spread(part, swap_halves(part), sources), HALF)
     return table_grad, weight_grads.reshape(4, width, width).astype(F32)
 

time: 105 us -> 103 us (0.981)
  blocking collectives: 21.2 us -> 33.3 us
  waiting for transfers between devices: 27 us -> 16.9 us
  starting transfers between devices: 24.5 us -> 20.5 us
    all_to_all x2 -> x3, blocking collectives: 21.2 us -> 33.3 us  [exchange(): return lax.all_to_all(x, axes, split_axis=0, concat_axis=0, tiled=True)]
    all_to_all x3 -> x2, waiting for transfers between devices: 11.8 us -> 3.38 us  [exchange(): return lax.all_to_all(x, axes, split_axis=0, concat_axis=0, tiled=True)]
    ppermute x3, waiting for transfers between devices: 9.57 us -> 5.01 us  [gather_column(): lax.ppermute(line, 'ga', [(i, i ^ k) for i in range(groups)])]
    ppermute x3, waiting for transfers between devices: 0.01 us -> 3.83 us  [gather_line(): lax.ppermute(mine, PEERS, [(i, i ^ k) for i in range(peers)])]
    all_to_all x3 -> x2, starting transfers between devices: 14.5 us -> 10.9 us  [exchange(): return lax.all_to_all(x, axes, split_axis=0, concat_axis=0, tiled=True)]
    ppermute x6 -> x3, waiting for transfers between devices: 1.22 us -> 0.01 us  [swap_cores(): return lax.ppermute(x, 'core', [(0, 1), (1, 0)])]
  transfers between devices with their start and end apart: 16 -> 12, of which waited for: 8 -> 8; matrix products, arithmetic and copies ran while one was open for 0% -> 0% of each run, Pallas kernels for 14% -> 15%
where the time goes in v7:
time: 103 us
  blocking collectives  33.3 us (32%)
  Pallas kernels  28.9 us (28%)
  starting transfers between devices  20.5 us (20%)
  waiting for transfers between devices  16.9 us (16%)
  other arithmetic  2.02 us (2%)
    all_to_all x3, blocking collectives, exchange(): return lax.all_to_all(x, axes, split_axis=0, concat_axis=0, tiled=True)  33.3 us
    all_to_all x2, starting transfers between devices, exchange(): return lax.all_to_all(x, axes, split_axis=0, concat_axis=0, tiled=True)  10.9 us
    pallas_call x1, Pallas kernels, scatter(): pl.pallas_call(scatter_kernel, grid=(rows_dev // tile,), out_shape=jax.Sh...  7.99 us
    pallas_call x1, Pallas kernels, backward(): pl.pallas_call(backward_kernel, out_shape=(half, half, weights), in_specs...  6.38 us
    pallas_call x1, Pallas kernels, gather(): pl.pallas_call(functools.partial(gather_kernel, blocks), out_shape=(half,...  5.66 us
    ppermute x3, waiting for transfers between devices, gather_column(): lax.ppermute(line, 'ga', [(i, i ^ k) for i in range(groups)])  5.01 us
    ppermute x1, waiting for transfers between devices, swap_halves(): return lax.ppermute(x, 'hi', [(0, 1), (1, 0)])  4.69 us
    ppermute x3, starting transfers between devices, gather_line(): lax.ppermute(mine, PEERS, [(i, i ^ k) for i in range(peers)])  4.25 us
  transfers between devices with their start and end apart: 12, of which 8 were waited for; matrix products, arithmetic and copies ran while one was open for 0% of the time, Pallas kernels for 15%

profile of v7, /device:TPU:0, one launch (start us, length us, event | category | flops | bytes accessed | tf_op | source)
XLA Modules:
  0.0 102.6 jit_solution(2627144349587515877)
XLA Ops:
  0.6 1.9 %plan.1 = s32[32,104]{1,0:T(8,128)} custom-call(s32[2]{0:T(128)} %lengths_hbm.1, s32[2,1024]{1,0:T(2,128)} %ids_hbm.1), custom_call_target="tpu_custom_call" | custom-call | flops 16777216 | tf_op jit(solution)/shard_map/plan/pallas_call | solution.py:101
  2.5 7.3 %all-to-all-start = ((s32[32,1,104]{2,1,0:T(1,128)}), s32[32,1,104]{2,1,0:T(1,128)S(1)}, u32[]{:S(2)}, u32[]{:S(2)}) async-start(s32[32,1,104]{2,1,0:T(1,128)} %bitcast.1), calls=%async_computation | async-start | bytes 32768 | tf_op jit(solution)/shard_map/all_to_all | solution.py:538
  9.8 1.8 %collective-permute-start = (bf16[8,16,256]{2,1,0:T(8,128)(2,1)}, bf16[8,16,256]{2,1,0:T(8,128)(2,1)S(1)}, u32[]{:S(2)}, u32[]{:S(2)}) collective-permute-start(bf16[8,16,256]{2,1,0:T(8,128)(2,1)} %param.13), channel_id=1, source_target_pairs={{0,1},{1,0},{2,3},{3,2},{4,5},{5,4},{6,7},{7,6},{8,9},{9,8},{10,11... | collective-permute-start | bytes 196616 | tf_op jit(solution)/shard_map/ppermute | solution.py:553
  11.7 2.4 %collective-permute-start.2 = (bf16[8,16,256]{2,1,0:T(8,128)(2,1)}, bf16[8,16,256]{2,1,0:T(8,128)(2,1)S(1)}, u32[]{:S(2)}, u32[]{:S(2)}) collective-permute-start(bf16[8,16,256]{2,1,0:T(8,128)(2,1)} %param.13), channel_id=1, source_target_pairs={{0,3},{1,2},{2,1},{3,0},{4,7},{5,6},{6,5},{7,4},{8,11},{9,10},{10,... | collective-permute-start | bytes 196616 | tf_op jit(solution)/shard_map/ppermute | solution.py:553
  14.1 2.9 %all-to-all-done = s32[32,1,104]{2,1,0:T(1,128)S(1)} async-done(((s32[32,1,104]{2,1,0:T(1,128)}), s32[32,1,104]{2,1,0:T(1,128)S(1)}, u32[]{:S(2)}, u32[]{:S(2)}) %all-to-all-start) | async-done | bytes 13344 | tf_op jit(solution)/shard_map/all_to_all | solution.py:538
  16.9 1.6 %collective-permute-done.2 = bf16[8,16,256]{2,1,0:T(8,128)(2,1)S(1)} collective-permute-done((bf16[8,16,256]{2,1,0:T(8,128)(2,1)}, bf16[8,16,256]{2,1,0:T(8,128)(2,1)S(1)}, u32[]{:S(2)}, u32[]{:S(2)}) %collective-permute-start.2) | collective-permute-done | bytes 65568 | tf_op jit(solution)/shard_map/ppermute | solution.py:553
  18.6 2.2 %collective-permute-done.1 = bf16[8,16,256]{2,1,0:T(8,128)(2,1)S(1)} collective-permute-done((bf16[8,16,256]{2,1,0:T(8,128)(2,1)}, bf16[8,16,256]{2,1,0:T(8,128)(2,1)S(1)}, u32[]{:S(2)}, u32[]{:S(2)}) %collective-permute-start.1) | collective-permute-done | bytes 65568 | tf_op jit(solution)/shard_map/ppermute | solution.py:553
  20.8 0.9 pad_maximum_fusion.refs_0_
  21.7 2.5 %collective-permute-start.7 = (bf16[4,8,16,256]{3,2,1,0:T(8,128)(2,1)S(1)}, bf16[4,8,16,256]{3,2,1,0:T(8,128)(2,1)S(1)}, u32[]{:S(2)}, u32[]{:S(2)}) collective-permute-start(bf16[4,8,16,256]{3,2,1,0:T(8,128)(2,1)S(1)} %pad_maximum_fusion.refs_0_), channel_id=1, source_target_pairs={{0,24},{8,16},{16,8},{24,0},{1,25},{9,17},{17,9},{25,1},{2,26},{10... | collective-permute-start | bytes 786440 | tf_op jit(solution)/shard_map/ppermute | solution.py:560
  24.1 0.5 collective-permute-start.6
  24.7 0.5 collective-permute-start.5
  25.4 5.7 %gather_rows.1 = (bf16[1536,256]{1,0:T(8,128)(2,1)S(1)}, bf16[768,256]{1,0:T(8,128)(2,1)S(1)}, bf16[768,256]{1,0:T(8,128)(2,1)S(1)}) custom-call(s32[3328]{0:T(1024)S(1)} %reshape.38.wanted_ref, bf16[4096,256]{1,0:T(8,128)(2,1)} %table_hbm.1), custom_call_target="tpu_custom_call" | custom-call | flops 6000000000 | tf_op jit(solution)/shard_map/gather_rows/pallas_call | solution.py:172
  31.1 0.5 collective-permute-start.4
  31.6 0.2 collective-permute-done.7.refs_3_
  31.8 4.7 %collective-permute-done.6.refs_2_ = bf16[4,8,16,256]{3,2,1,0:T(8,128)(2,1)S(1)} collective-permute-done((bf16[4,8,16,256]{3,2,1,0:T(8,128)(2,1)S(1)}, bf16[4,8,16,256]{3,2,1,0:T(8,128)(2,1)S(1)}, u32[]{:S(2)}, u32[]{:S(2)}) %collective-permute-start.6) | collective-permute-done | bytes 262176 | tf_op jit(solution)/shard_map/ppermute | solution.py:560
  36.5 0.1 collective-permute-done.5.refs_1_
  36.6 1.3 %prepare.1 = (bf16[16,128,256]{2,1,0:T(8,128)(2,1)S(1)}, bf16[16,128,256]{2,1,0:T(8,128)(2,1)S(1)}, bf16[16,128,256]{2,1,0:T(8,128)(2,1)S(1)}) custom-call(bf16[4,8,16,256]{3,2,1,0:T(8,128)(2,1)S(1)} %pad_maximum_fusion.refs_0_, bf16[4,8,16,256]{3,2,1,0:T(8,128)(2,1)S(1)} %collective-permute-done.5.refs_1_, ...), custom_call_target="tpu_custom_call" | custom-call | flops 536870912 | tf_op jit(solution)/shard_map/prepare/pallas_call | solution.py:307
  38.0 4.2 %forward.1 = (bf16[16,192,512]{2,1,0:T(8,128)(2,1)S(1)}, bf16[16,192,512]{2,1,0:T(8,128)(2,1)S(1)}, f32[16,16,128]{2,1,0:T(8,128)S(1)}, bf16[16,192,256]{2,1,0:T...) custom-call(bf16[16,96,256]{2,1,0:T(8,128)(2,1)S(1)} %bitcast.24, ...), custom_call_target="tpu_custom_call" | custom-call | flops 3221225472 | tf_op jit(solution)/shard_map/forward/pallas_call | solution.py:402
  42.2 11.6 %all_to_all.29.parts_ref = f32[16,16,128]{2,1,0:T(8,128)S(1)} all-to-all(f32[16,16,128]{2,1,0:T(8,128)S(1)} %get-tuple-element.38.part_ref), channel_id=1, replica_groups=mesh['ga'=4,'core'=2,'hi'=2,'lo'=2] {'ga','hi','lo'}, dimensions={0} | all-to-all | bytes 262144 | tf_op jit(solution)/shard_map/all_to_all | solution.py:538
  53.9 0.6 combine.1
  54.5 10.4 %all_to_all.30.total_ref = f32[16,16,128]{2,1,0:T(8,128)S(1)} all-to-all(f32[16,16,128]{2,1,0:T(8,128)S(1)} %combine.1), channel_id=1, replica_groups=mesh['ga'=4,'core'=2,'hi'=2,'lo'=2] {'ga','hi','lo'}, dimensions={0} | all-to-all | bytes 262144 | tf_op jit(solution)/shard_map/all_to_all | solution.py:538
  64.8 6.4 %backward.1 = (bf16[16,96,256]{2,1,0:T(8,128)(2,1)S(1)}, bf16[16,96,256]{2,1,0:T(8,128)(2,1)S(1)}, bf16[16,64,256]{2,1,0:T(8,128)(2,1)S(1)}) custom-call(f32[16,16,128]{2,1,0:T(8,128)S(1)} %all_to_all.30.total_ref, f32[16,16,128]{2,1,0:T(8,128)S(1)} %get-tuple-element.38.part_ref, bf16[16,192,512]{2,1,0:T(8,128)(2,1)S(1)} %get-tuple-element.39.expo_ref, ...), custom_call_target="tpu_custom_call" | custom-call | flops 6442450944 | tf_op jit(solution)/shard_map/backward/pallas_call | solution.py:520
  71.2 11.3 %all_to_all.31 = bf16[16,64,256]{2,1,0:T(8,128)(2,1)S(1)} all-to-all(bf16[16,64,256]{2,1,0:T(8,128)(2,1)S(1)} %get-tuple-element.46), channel_id=1, replica_groups=mesh['ga'=4,'core'=2,'hi'=2,'lo'=2] {'ga','core','lo'}, dimensions={0} | all-to-all | bytes 1048576 | tf_op jit(solution)/shard_map/all_to_all | solution.py:538
  82.5 0.4 collective-permute-start.8
  83.0 0.9 collective-permute-start.9
  83.8 4.7 %collective-permute-done.9.other_ref = bf16[64,256]{1,0:T(8,128)(2,1)S(1)} collective-permute-done((bf16[64,256]{1,0:T(8,128)(2,1)S(1)}, bf16[64,256]{1,0:T(8,128)(2,1)S(1)}, u32[]{:S(2)}, u32[]{:S(2)}) %collective-permute-start.9) | collective-permute-done | bytes 32800 | tf_op jit(solution)/shard_map/ppermute | solution.py:546
  88.5 0.8 spread.1
  89.4 3.6 %all-to-all-start.4 = ((bf16[16,64,256]{2,1,0:T(8,128)(2,1)}), bf16[16,64,256]{2,1,0:T(8,128)(2,1)S(1)}, u32[]{:S(2)}, u32[]{:S(2)}) async-start(bf16[16,64,256]{2,1,0:T(8,128)(2,1)} %spread.1), calls=%async_computation.4 | async-start | bytes 1048576 | tf_op jit(solution)/shard_map/all_to_all | solution.py:538
  93.0 0.1 reshape.37.wanted_ref
  93.1 8.0 %scatter_rows.1 = bf16[4096,256]{1,0:T(8,128)(2,1)} custom-call(s32[1,3072]{1,0:T(1,128)S(1)} %reshape.37.wanted_ref, bf16[1536,256]{1,0:T(8,128)(2,1)S(1)} %bitcast.25, bf16[1536,256]{1,0:T(8,128)(2,1)S(1)} %bitcast.21), custom_call_target="tpu_custom_call" | custom-call | flops 6442450944 | tf_op jit(solution)/shard_map/scatter_rows/pallas_call | solution.py:227
  101.0 0.5 all-to-all-done.4
  101.6 1.1 %bitcast_convert_fusion = f32[4,256,256]{2,1,0:T(8,128)} fusion(bf16[4,256,256]{2,1,0:T(8,128)(2,1)S(1)} %bitcast.26), kind=kLoop, calls=%fused_computation | loop fusion | flops 262144 | bytes 1572864 | tf_op jit(solution)/shard_map/convert_element_type | solution.py:612
  (24 shorter events, 0.3 us)
Async XLA Ops:
  2.5 14.4 %all-to-all-start = ((s32[32,1,104]{2,1,0:T(1,128)}), s32[32,1,104]{2,1,0:T(1,128)S(1)}, u32[]{:S(2)}, u32[]{:S(2)}) async-start(s32[32,1,104]{2,1,0:T(1,128)} %bitcast.1), calls=%async_computation | async-start | bytes 32768 | tf_op jit(solution)/shard_map/all_to_all | solution.py:538
  9.8 7.1 %collective-permute-start = (bf16[8,16,256]{2,1,0:T(8,128)(2,1)}, bf16[8,16,256]{2,1,0:T(8,128)(2,1)S(1)}, u32[]{:S(2)}, u32[]{:S(2)}) collective-permute-start(bf16[8,16,256]{2,1,0:T(8,128)(2,1)} %param.13), channel_id=1, source_target_pairs={{0,1},{1,0},{2,3},{3,2},{4,5},{5,4},{6,7},{7,6},{8,9},{9,8},{10,11... | collective-permute-start | bytes 196616 | tf_op jit(solution)/shard_map/ppermute | solution.py:553
  11.7 6.9 %collective-permute-start.2 = (bf16[8,16,256]{2,1,0:T(8,128)(2,1)}, bf16[8,16,256]{2,1,0:T(8,128)(2,1)S(1)}, u32[]{:S(2)}, u32[]{:S(2)}) collective-permute-start(bf16[8,16,256]{2,1,0:T(8,128)(2,1)} %param.13), channel_id=1, source_target_pairs={{0,3},{1,2},{2,1},{3,0},{4,7},{5,6},{6,5},{7,4},{8,11},{9,10},{10,... | collective-permute-start | bytes 196616 | tf_op jit(solution)/shard_map/ppermute | solution.py:553
  14.0 6.7 %collective-permute-start.1 = (bf16[8,16,256]{2,1,0:T(8,128)(2,1)}, bf16[8,16,256]{2,1,0:T(8,128)(2,1)S(1)}, u32[]{:S(2)}, u32[]{:S(2)}) collective-permute-start(bf16[8,16,256]{2,1,0:T(8,128)(2,1)} %param.13), channel_id=1, source_target_pairs={{0,2},{1,3},{2,0},{3,1},{4,6},{5,7},{6,4},{7,5},{8,10},{9,11},{10,... | collective-permute-start | bytes 196616 | tf_op jit(solution)/shard_map/ppermute | solution.py:553
  21.7 10.2 %collective-permute-start.7 = (bf16[4,8,16,256]{3,2,1,0:T(8,128)(2,1)S(1)}, bf16[4,8,16,256]{3,2,1,0:T(8,128)(2,1)S(1)}, u32[]{:S(2)}, u32[]{:S(2)}) collective-permute-start(bf16[4,8,16,256]{3,2,1,0:T(8,128)(2,1)S(1)} %pad_maximum_fusion.refs_0_), channel_id=1, source_target_pairs={{0,24},{8,16},{16,8},{24,0},{1,25},{9,17},{17,9},{25,1},{2,26},{10... | collective-permute-start | bytes 786440 | tf_op jit(solution)/shard_map/ppermute | solution.py:560
  24.1 12.4 %collective-permute-start.6 = (bf16[4,8,16,256]{3,2,1,0:T(8,128)(2,1)S(1)}, bf16[4,8,16,256]{3,2,1,0:T(8,128)(2,1)S(1)}, u32[]{:S(2)}, u32[]{:S(2)}) collective-permute-start(bf16[4,8,16,256]{3,2,1,0:T(8,128)(2,1)S(1)} %pad_maximum_fusion.refs_0_), channel_id=1, source_target_pairs={{0,16},{8,24},{16,0},{24,8},{1,17},{9,25},{17,1},{25,9},{2,18},{10... | collective-permute-start | bytes 786440 | tf_op jit(solution)/shard_map/ppermute | solution.py:560
  24.7 12.0 %collective-permute-start.5 = (bf16[4,8,16,256]{3,2,1,0:T(8,128)(2,1)S(1)}, bf16[4,8,16,256]{3,2,1,0:T(8,128)(2,1)S(1)}, u32[]{:S(2)}, u32[]{:S(2)}) collective-permute-start(bf16[4,8,16,256]{3,2,1,0:T(8,128)(2,1)S(1)} %pad_maximum_fusion.refs_0_), channel_id=1, source_target_pairs={{0,8},{8,0},{16,24},{24,16},{1,9},{9,1},{17,25},{25,17},{2,10},{10... | collective-permute-start | bytes 786440 | tf_op jit(solution)/shard_map/ppermute | solution.py:560
  25.3 11.3 %copy-start.1 = (bf16[256,256]{1,0:T(8,128)(2,1)S(1)}, bf16[256,256]{1,0:T(8,128)(2,1)}, u32[]{:S(2)}) copy-start(bf16[256,256]{1,0:T(8,128)(2,1)} %refs_4_.1) | copy-start | bytes 393220
  25.3 11.3 %copy-start.2 = (bf16[256,256]{1,0:T(8,128)(2,1)S(1)}, bf16[256,256]{1,0:T(8,128)(2,1)}, u32[]{:S(2)}) copy-start(bf16[256,256]{1,0:T(8,128)(2,1)} %refs_5_.1) | copy-start | bytes 393220
  25.3 12.6 %copy-start.3 = (bf16[256,256]{1,0:T(8,128)(2,1)S(1)}, bf16[256,256]{1,0:T(8,128)(2,1)}, u32[]{:S(2)}) copy-start(bf16[256,256]{1,0:T(8,128)(2,1)} %wk_ref.3) | copy-start | bytes 393220
  25.3 12.6 %copy-start.4 = (bf16[256,256]{1,0:T(8,128)(2,1)S(1)}, bf16[256,256]{1,0:T(8,128)(2,1)}, u32[]{:S(2)}) copy-start(bf16[256,256]{1,0:T(8,128)(2,1)} %wv_ref.3) | copy-start | bytes 393220
  25.3 12.6 %copy-start.5 = (f32[8,16]{1,0:T(8,128)S(1)}, f32[8,16]{1,0:T(8,128)}, u32[]{:S(2)}) copy-start(f32[8,16]{1,0:T(8,128)} %labels_ref.1) | copy-start | bytes 1540
  31.0 6.9 %collective-permute-start.3 = (bf16[768,256]{1,0:T(8,128)(2,1)S(1)}, bf16[768,256]{1,0:T(8,128)(2,1)S(1)}, u32[]{:S(2)}, u32[]{:S(2)}) collective-permute-start(bf16[768,256]{1,0:T(8,128)(2,1)S(1)} %get-tuple-element.28), channel_id=1, source_target_pairs={{0,4},{4,0},{1,5},{5,1},{2,6},{6,2},{3,7},{7,3},{8,12},{12,8},{9,1... | collective-permute-start | bytes 1179656 | tf_op jit(solution)/shard_map/ppermute | solution.py:542
  31.1 6.8 %collective-permute-start.4 = (bf16[768,256]{1,0:T(8,128)(2,1)S(1)}, bf16[768,256]{1,0:T(8,128)(2,1)S(1)}, u32[]{:S(2)}, u32[]{:S(2)}) collective-permute-start(bf16[768,256]{1,0:T(8,128)(2,1)S(1)} %get-tuple-element.29), channel_id=1, source_target_pairs={{0,4},{4,0},{1,5},{5,1},{2,6},{6,2},{3,7},{7,3},{8,12},{12,8},{9,1... | collective-permute-start | bytes 1179656 | tf_op jit(solution)/shard_map/ppermute | solution.py:542
  38.0 15.9 %copy-start = (s32[2]{0:T(128)S(1)}, s32[2]{0:T(128)}, u32[]{:S(2)}) copy-start(s32[2]{0:T(128)} %counts_ref.1) | copy-start | bytes 28
  82.5 10.6 %collective-permute-start.8 = (bf16[16,96,256]{2,1,0:T(8,128)(2,1)S(1)}, bf16[16,96,256]{2,1,0:T(8,128)(2,1)S(1)}, u32[]{:S(2)}, u32[]{:S(2)}) collective-permute-start(bf16[16,96,256]{2,1,0:T(8,128)(2,1)S(1)} %get-tuple-element.48), channel_id=1, source_target_pairs={{0,4},{4,0},{1,5},{5,1},{2,6},{6,2},{3,7},{7,3},{8,12},{12,8},{9,1... | collective-permute-start | bytes 2359304 | tf_op jit(solution)/shard_map/ppermute | solution.py:542
  83.0 5.5 %collective-permute-start.9 = (bf16[64,256]{1,0:T(8,128)(2,1)S(1)}, bf16[64,256]{1,0:T(8,128)(2,1)S(1)}, u32[]{:S(2)}, u32[]{:S(2)}) collective-permute-start(bf16[64,256]{1,0:T(8,128)(2,1)S(1)} %reduce_sum.12.own_ref), channel_id=1, source_target_pairs={{0,2},{2,0},{1,3},{3,1},{4,6},{6,4},{5,7},{7,5},{8,10},{10,8},{9,1... | collective-permute-start | bytes 98312 | tf_op jit(solution)/shard_map/ppermute | solution.py:546
  89.4 12.2 %all-to-all-start.4 = ((bf16[16,64,256]{2,1,0:T(8,128)(2,1)}), bf16[16,64,256]{2,1,0:T(8,128)(2,1)S(1)}, u32[]{:S(2)}, u32[]{:S(2)}) async-start(bf16[16,64,256]{2,1,0:T(8,128)(2,1)} %spread.1), calls=%async_computation.4 | async-start | bytes 1048576 | tf_op jit(solution)/shard_map/all_to_all | solution.py:538

commit v8 on v7

--- a/solution.py
+++ b/solution.py
@@ -546,9 +546,28 @@
     return lax.ppermute(x, "hi", [(0, 1), (1, 0)])
 
 
+def together_kernel(*refs):
+    *pieces, out_ref = refs
+    for k, piece in enumerate(pieces):
+        out_ref[k] = piece[...]
+
+
+def together(pieces):
+    vmem = pl.BlockSpec(memory_space=pltpu.VMEM)
+    return pl.pallas_call(
+        together_kernel,
+        out_shape=jax.ShapeDtypeStruct((len(pieces),) + pieces[0].shape, pieces[0].dtype),
+        in_specs=[vmem] * len(pieces),
+        out_specs=vmem,
+        compiler_params=pltpu.CompilerParams(vmem_limit_bytes=VMEM_LIMIT),
+        cost_estimate=cost(pieces[0].size, 0),
+        name="together",
+    )(*pieces)
+
+
 def gather_line(mine):
     peers = lax.axis_size(PEERS)
-    return jnp.stack(
+    return together(
         [mine]
         + [lax.ppermute(mine, PEERS, [(i, i ^ k) for i in range(peers)]) for k in range(1, peers)]
     )

time: 103 us -> 103 us (level)
  waiting for transfers between devices: 16.9 us -> 14.9 us
  blocking collectives: 33.3 us -> 34.8 us
    all_to_all x3, blocking collectives: 33.3 us -> 34.8 us  [exchange(): return lax.all_to_all(x, axes, split_axis=0, concat_axis=0, tiled=True)]
    ppermute x3, waiting for transfers between devices: 5.01 us -> 3.64 us  [gather_column(): lax.ppermute(line, 'ga', [(i, i ^ k) for i in range(groups)])]
where the time goes in v8:
time: 103 us; the launch traced here: 102 us
  blocking collectives  34.8 us (34%)
  Pallas kernels  28.7 us (28%)
  starting transfers between devices  20.7 us (20%)
  waiting for transfers between devices  14.9 us (14%)
  other arithmetic  1.15 us (1%)
  local copies, waits for them, and re-layouts  1.04 us (1%)
    all_to_all x3, blocking collectives, exchange(): return lax.all_to_all(x, axes, split_axis=0, concat_axis=0, tiled=True)  34.8 us
    all_to_all x2, starting transfers between devices, exchange(): return lax.all_to_all(x, axes, split_axis=0, concat_axis=0, tiled=True)  10.9 us
    pallas_call x1, Pallas kernels, scatter(): pl.pallas_call(scatter_kernel, grid=(rows_dev // tile,), out_shape=jax.Sh...  7.99 us
    pallas_call x1, Pallas kernels, backward(): pl.pallas_call(backward_kernel, out_shape=(half, half, weights), in_specs...  6.38 us
    pallas_call x1, Pallas kernels, gather(): pl.pallas_call(functools.partial(gather_kernel, blocks), out_shape=(half,...  5.48 us
    ppermute x1, waiting for transfers between devices, swap_halves(): return lax.ppermute(x, 'hi', [(0, 1), (1, 0)])  4.69 us
    ppermute x3, starting transfers between devices, gather_line(): lax.ppermute(mine, PEERS, [(i, i ^ k) for i in range(peers)])  4.45 us
    pallas_call x1, Pallas kernels, forward(): pl.pallas_call(functools.partial(forward_kernel, peers, peers // 2), out_...  4.2 us
  transfers between devices with their start and end apart: 12, of which 8 were waited for; matrix products, arithmetic and copies ran while one was open for 0% of the time, Pallas kernels for 15%

profile of v8, /device:TPU:0, one launch (start us, length us, event | category | flops | bytes accessed | tf_op | source)
XLA Modules:
  0.0 102.1 jit_solution(6883798860907496579)
XLA Ops:
  0.6 1.9 %plan.1 = s32[32,104]{1,0:T(8,128)} custom-call(s32[2]{0:T(128)} %lengths_hbm.1, s32[2,1024]{1,0:T(2,128)} %ids_hbm.1), custom_call_target="tpu_custom_call" | custom-call | flops 16777216 | tf_op jit(solution)/shard_map/plan/pallas_call | solution.py:101
  2.5 7.3 %all-to-all-start = ((s32[32,1,104]{2,1,0:T(1,128)}), s32[32,1,104]{2,1,0:T(1,128)S(1)}, u32[]{:S(2)}, u32[]{:S(2)}) async-start(s32[32,1,104]{2,1,0:T(1,128)} %bitcast.1), calls=%async_computation | async-start | bytes 32768 | tf_op jit(solution)/shard_map/all_to_all | solution.py:538
  9.8 2.7 %collective-permute-start.1 = (bf16[8,16,256]{2,1,0:T(8,128)(2,1)}, bf16[8,16,256]{2,1,0:T(8,128)(2,1)S(1)}, u32[]{:S(2)}, u32[]{:S(2)}) collective-permute-start(bf16[8,16,256]{2,1,0:T(8,128)(2,1)} %refs_0_.1), channel_id=1, source_target_pairs={{0,2},{1,3},{2,0},{3,1},{4,6},{5,7},{6,4},{7,5},{8,10},{9,11},{10,... | collective-permute-start | bytes 196616 | tf_op jit(solution)/shard_map/ppermute | solution.py:572
  12.6 1.5 %collective-permute-start = (bf16[8,16,256]{2,1,0:T(8,128)(2,1)}, bf16[8,16,256]{2,1,0:T(8,128)(2,1)S(1)}, u32[]{:S(2)}, u32[]{:S(2)}) collective-permute-start(bf16[8,16,256]{2,1,0:T(8,128)(2,1)} %refs_0_.1), channel_id=1, source_target_pairs={{0,1},{1,0},{2,3},{3,2},{4,5},{5,4},{6,7},{7,6},{8,9},{9,8},{10,11... | collective-permute-start | bytes 196616 | tf_op jit(solution)/shard_map/ppermute | solution.py:572
  14.1 0.2 collective-permute-start.2
  14.3 2.7 %all-to-all-done = s32[32,1,104]{2,1,0:T(1,128)S(1)} async-done(((s32[32,1,104]{2,1,0:T(1,128)}), s32[32,1,104]{2,1,0:T(1,128)S(1)}, u32[]{:S(2)}, u32[]{:S(2)}) %all-to-all-start) | async-done | bytes 13344 | tf_op jit(solution)/shard_map/all_to_all | solution.py:538
  16.9 0.3 collective-permute-done.refs_1_
  17.2 3.1 %collective-permute-done.2.refs_3_ = bf16[8,16,256]{2,1,0:T(8,128)(2,1)S(1)} collective-permute-done((bf16[8,16,256]{2,1,0:T(8,128)(2,1)}, bf16[8,16,256]{2,1,0:T(8,128)(2,1)S(1)}, u32[]{:S(2)}, u32[]{:S(2)}) %collective-permute-start.2) | collective-permute-done | bytes 65568 | tf_op jit(solution)/shard_map/ppermute | solution.py:572
  20.4 0.8 copy-done
  21.2 2.5 %collective-permute-start.7 = (bf16[4,8,16,256]{3,2,1,0:T(8,128)(2,1)S(1)}, bf16[4,8,16,256]{3,2,1,0:T(8,128)(2,1)S(1)}, u32[]{:S(2)}, u32[]{:S(2)}) collective-permute-start(bf16[4,8,16,256]{3,2,1,0:T(8,128)(2,1)S(1)} %together.1.refs_0_), channel_id=1, source_target_pairs={{0,24},{8,16},{16,8},{24,0},{1,25},{9,17},{17,9},{25,1},{2,26},{10... | collective-permute-start | bytes 786440 | tf_op jit(solution)/shard_map/ppermute | solution.py:579
  23.7 0.5 collective-permute-start.6
  24.2 0.5 collective-permute-start.5
  24.9 5.5 %gather_rows.1 = (bf16[1536,256]{1,0:T(8,128)(2,1)S(1)}, bf16[768,256]{1,0:T(8,128)(2,1)S(1)}, bf16[768,256]{1,0:T(8,128)(2,1)S(1)}) custom-call(s32[3328]{0:T(1024)S(1)} %reshape.38.wanted_ref, bf16[4096,256]{1,0:T(8,128)(2,1)} %table_hbm.1), custom_call_target="tpu_custom_call" | custom-call | flops 6000000000 | tf_op jit(solution)/shard_map/gather_rows/pallas_call | solution.py:172
  30.5 0.5 collective-permute-start.4
  31.0 0.5 collective-permute-done.7.refs_3_
  31.5 3.1 %collective-permute-done.6.refs_2_ = bf16[4,8,16,256]{3,2,1,0:T(8,128)(2,1)S(1)} collective-permute-done((bf16[4,8,16,256]{3,2,1,0:T(8,128)(2,1)S(1)}, bf16[4,8,16,256]{3,2,1,0:T(8,128)(2,1)S(1)}, u32[]{:S(2)}, u32[]{:S(2)}) %collective-permute-start.6) | collective-permute-done | bytes 262176 | tf_op jit(solution)/shard_map/ppermute | solution.py:579
  34.6 1.3 %prepare.1 = (bf16[16,128,256]{2,1,0:T(8,128)(2,1)S(1)}, bf16[16,128,256]{2,1,0:T(8,128)(2,1)S(1)}, bf16[16,128,256]{2,1,0:T(8,128)(2,1)S(1)}) custom-call(bf16[4,8,16,256]{3,2,1,0:T(8,128)(2,1)S(1)} %together.1.refs_0_, bf16[4,8,16,256]{3,2,1,0:T(8,128)(2,1)S(1)} %collective-permute-done.5.refs_1_, ...), custom_call_target="tpu_custom_call" | custom-call | flops 536870912 | tf_op jit(solution)/shard_map/prepare/pallas_call | solution.py:307
  36.0 4.2 %forward.1 = (bf16[16,192,512]{2,1,0:T(8,128)(2,1)S(1)}, bf16[16,192,512]{2,1,0:T(8,128)(2,1)S(1)}, f32[16,16,128]{2,1,0:T(8,128)S(1)}, bf16[16,192,256]{2,1,0:T...) custom-call(bf16[16,96,256]{2,1,0:T(8,128)(2,1)S(1)} %bitcast.20, ...), custom_call_target="tpu_custom_call" | custom-call | flops 3221225472 | tf_op jit(solution)/shard_map/forward/pallas_call | solution.py:402
  40.2 13.1 %all_to_all.29.parts_ref = f32[16,16,128]{2,1,0:T(8,128)S(1)} all-to-all(f32[16,16,128]{2,1,0:T(8,128)S(1)} %get-tuple-element.38.part_ref), channel_id=1, replica_groups=mesh['ga'=4,'core'=2,'hi'=2,'lo'=2] {'ga','hi','lo'}, dimensions={0} | all-to-all | bytes 262144 | tf_op jit(solution)/shard_map/all_to_all | solution.py:538
  53.3 0.6 combine.1
  54.0 10.4 %all_to_all.30.total_ref = f32[16,16,128]{2,1,0:T(8,128)S(1)} all-to-all(f32[16,16,128]{2,1,0:T(8,128)S(1)} %combine.1), channel_id=1, replica_groups=mesh['ga'=4,'core'=2,'hi'=2,'lo'=2] {'ga','hi','lo'}, dimensions={0} | all-to-all | bytes 262144 | tf_op jit(solution)/shard_map/all_to_all | solution.py:538
  64.3 6.4 %backward.1 = (bf16[16,96,256]{2,1,0:T(8,128)(2,1)S(1)}, bf16[16,96,256]{2,1,0:T(8,128)(2,1)S(1)}, bf16[16,64,256]{2,1,0:T(8,128)(2,1)S(1)}) custom-call(f32[16,16,128]{2,1,0:T(8,128)S(1)} %all_to_all.30.total_ref, f32[16,16,128]{2,1,0:T(8,128)S(1)} %get-tuple-element.38.part_ref, bf16[16,192,512]{2,1,0:T(8,128)(2,1)S(1)} %get-tuple-element.39.expo_ref, ...), custom_call_target="tpu_custom_call" | custom-call | flops 6442450944 | tf_op jit(solution)/shard_map/backward/pallas_call | solution.py:520
  70.7 11.3 %all_to_all.31 = bf16[16,64,256]{2,1,0:T(8,128)(2,1)S(1)} all-to-all(bf16[16,64,256]{2,1,0:T(8,128)(2,1)S(1)} %get-tuple-element.46), channel_id=1, replica_groups=mesh['ga'=4,'core'=2,'hi'=2,'lo'=2] {'ga','core','lo'}, dimensions={0} | all-to-all | bytes 1048576 | tf_op jit(solution)/shard_map/all_to_all | solution.py:538
  82.0 0.4 collective-permute-start.8
  82.4 0.9 collective-permute-start.9
  83.3 4.7 %collective-permute-done.9.other_ref = bf16[64,256]{1,0:T(8,128)(2,1)S(1)} collective-permute-done((bf16[64,256]{1,0:T(8,128)(2,1)S(1)}, bf16[64,256]{1,0:T(8,128)(2,1)S(1)}, u32[]{:S(2)}, u32[]{:S(2)}) %collective-permute-start.9) | collective-permute-done | bytes 32800 | tf_op jit(solution)/shard_map/ppermute | solution.py:546
  88.0 0.8 spread.1
  88.8 3.6 %all-to-all-start.4 = ((bf16[16,64,256]{2,1,0:T(8,128)(2,1)}), bf16[16,64,256]{2,1,0:T(8,128)(2,1)S(1)}, u32[]{:S(2)}, u32[]{:S(2)}) async-start(bf16[16,64,256]{2,1,0:T(8,128)(2,1)} %spread.1), calls=%async_computation.4 | async-start | bytes 1048576 | tf_op jit(solution)/shard_map/all_to_all | solution.py:538
  92.4 0.1 reshape.37.wanted_ref
  92.5 8.0 %scatter_rows.1 = bf16[4096,256]{1,0:T(8,128)(2,1)} custom-call(s32[1,3072]{1,0:T(1,128)S(1)} %reshape.37.wanted_ref, bf16[1536,256]{1,0:T(8,128)(2,1)S(1)} %bitcast.21, bf16[1536,256]{1,0:T(8,128)(2,1)S(1)} %bitcast.17), custom_call_target="tpu_custom_call" | custom-call | flops 6442450944 | tf_op jit(solution)/shard_map/scatter_rows/pallas_call | solution.py:227
  100.5 0.5 all-to-all-done.4
  101.1 1.1 %bitcast_convert_fusion = f32[4,256,256]{2,1,0:T(8,128)} fusion(bf16[4,256,256]{2,1,0:T(8,128)(2,1)S(1)} %bitcast.22), kind=kLoop, calls=%fused_computation | loop fusion | flops 262144 | bytes 1572864 | tf_op jit(solution)/shard_map/convert_element_type | solution.py:631
  (26 shorter events, 0.4 us)
Async XLA Ops:
  2.5 14.4 %all-to-all-start = ((s32[32,1,104]{2,1,0:T(1,128)}), s32[32,1,104]{2,1,0:T(1,128)S(1)}, u32[]{:S(2)}, u32[]{:S(2)}) async-start(s32[32,1,104]{2,1,0:T(1,128)} %bitcast.1), calls=%async_computation | async-start | bytes 32768 | tf_op jit(solution)/shard_map/all_to_all | solution.py:538
  9.8 7.1 %collective-permute-start.1 = (bf16[8,16,256]{2,1,0:T(8,128)(2,1)}, bf16[8,16,256]{2,1,0:T(8,128)(2,1)S(1)}, u32[]{:S(2)}, u32[]{:S(2)}) collective-permute-start(bf16[8,16,256]{2,1,0:T(8,128)(2,1)} %refs_0_.1), channel_id=1, source_target_pairs={{0,2},{1,3},{2,0},{3,1},{4,6},{5,7},{6,4},{7,5},{8,10},{9,11},{10,... | collective-permute-start | bytes 196616 | tf_op jit(solution)/shard_map/ppermute | solution.py:572
  12.6 4.6 %collective-permute-start = (bf16[8,16,256]{2,1,0:T(8,128)(2,1)}, bf16[8,16,256]{2,1,0:T(8,128)(2,1)S(1)}, u32[]{:S(2)}, u32[]{:S(2)}) collective-permute-start(bf16[8,16,256]{2,1,0:T(8,128)(2,1)} %refs_0_.1), channel_id=1, source_target_pairs={{0,1},{1,0},{2,3},{3,2},{4,5},{5,4},{6,7},{7,6},{8,9},{9,8},{10,11... | collective-permute-start | bytes 196616 | tf_op jit(solution)/shard_map/ppermute | solution.py:572
  14.1 6.3 %collective-permute-start.2 = (bf16[8,16,256]{2,1,0:T(8,128)(2,1)}, bf16[8,16,256]{2,1,0:T(8,128)(2,1)S(1)}, u32[]{:S(2)}, u32[]{:S(2)}) collective-permute-start(bf16[8,16,256]{2,1,0:T(8,128)(2,1)} %refs_0_.1), channel_id=1, source_target_pairs={{0,3},{1,2},{2,1},{3,0},{4,7},{5,6},{6,5},{7,4},{8,11},{9,10},{10,... | collective-permute-start | bytes 196616 | tf_op jit(solution)/shard_map/ppermute | solution.py:572
  20.4 0.8 copy-start
  21.2 10.2 %collective-permute-start.7 = (bf16[4,8,16,256]{3,2,1,0:T(8,128)(2,1)S(1)}, bf16[4,8,16,256]{3,2,1,0:T(8,128)(2,1)S(1)}, u32[]{:S(2)}, u32[]{:S(2)}) collective-permute-start(bf16[4,8,16,256]{3,2,1,0:T(8,128)(2,1)S(1)} %together.1.refs_0_), channel_id=1, source_target_pairs={{0,24},{8,16},{16,8},{24,0},{1,25},{9,17},{17,9},{25,1},{2,26},{10... | collective-permute-start | bytes 786440 | tf_op jit(solution)/shard_map/ppermute | solution.py:579
  23.7 10.9 %collective-permute-start.6 = (bf16[4,8,16,256]{3,2,1,0:T(8,128)(2,1)S(1)}, bf16[4,8,16,256]{3,2,1,0:T(8,128)(2,1)S(1)}, u32[]{:S(2)}, u32[]{:S(2)}) collective-permute-start(bf16[4,8,16,256]{3,2,1,0:T(8,128)(2,1)S(1)} %together.1.refs_0_), channel_id=1, source_target_pairs={{0,16},{8,24},{16,0},{24,8},{1,17},{9,25},{17,1},{25,9},{2,18},{10... | collective-permute-start | bytes 786440 | tf_op jit(solution)/shard_map/ppermute | solution.py:579
  24.2 10.4 %collective-permute-start.5 = (bf16[4,8,16,256]{3,2,1,0:T(8,128)(2,1)S(1)}, bf16[4,8,16,256]{3,2,1,0:T(8,128)(2,1)S(1)}, u32[]{:S(2)}, u32[]{:S(2)}) collective-permute-start(bf16[4,8,16,256]{3,2,1,0:T(8,128)(2,1)S(1)} %together.1.refs_0_), channel_id=1, source_target_pairs={{0,8},{8,0},{16,24},{24,16},{1,9},{9,1},{17,25},{25,17},{2,10},{10... | collective-permute-start | bytes 786440 | tf_op jit(solution)/shard_map/ppermute | solution.py:579
  24.9 9.8 %copy-start.2 = (bf16[256,256]{1,0:T(8,128)(2,1)S(1)}, bf16[256,256]{1,0:T(8,128)(2,1)}, u32[]{:S(2)}) copy-start(bf16[256,256]{1,0:T(8,128)(2,1)} %refs_4_.1) | copy-start | bytes 393220
  24.9 9.8 %copy-start.3 = (bf16[256,256]{1,0:T(8,128)(2,1)S(1)}, bf16[256,256]{1,0:T(8,128)(2,1)}, u32[]{:S(2)}) copy-start(bf16[256,256]{1,0:T(8,128)(2,1)} %refs_5_.1) | copy-start | bytes 393220
  24.9 11.1 %copy-start.4 = (bf16[256,256]{1,0:T(8,128)(2,1)S(1)}, bf16[256,256]{1,0:T(8,128)(2,1)}, u32[]{:S(2)}) copy-start(bf16[256,256]{1,0:T(8,128)(2,1)} %wk_ref.3) | copy-start | bytes 393220
  24.9 11.1 %copy-start.5 = (bf16[256,256]{1,0:T(8,128)(2,1)S(1)}, bf16[256,256]{1,0:T(8,128)(2,1)}, u32[]{:S(2)}) copy-start(bf16[256,256]{1,0:T(8,128)(2,1)} %wv_ref.3) | copy-start | bytes 393220
  24.9 11.1 %copy-start.6 = (f32[8,16]{1,0:T(8,128)S(1)}, f32[8,16]{1,0:T(8,128)}, u32[]{:S(2)}) copy-start(f32[8,16]{1,0:T(8,128)} %labels_ref.1) | copy-start | bytes 1540
  30.4 5.5 %collective-permute-start.3 = (bf16[768,256]{1,0:T(8,128)(2,1)S(1)}, bf16[768,256]{1,0:T(8,128)(2,1)S(1)}, u32[]{:S(2)}, u32[]{:S(2)}) collective-permute-start(bf16[768,256]{1,0:T(8,128)(2,1)S(1)} %get-tuple-element.28), channel_id=1, source_target_pairs={{0,4},{4,0},{1,5},{5,1},{2,6},{6,2},{3,7},{7,3},{8,12},{12,8},{9,1... | collective-permute-start | bytes 1179656 | tf_op jit(solution)/shard_map/ppermute | solution.py:542
  30.5 5.5 %collective-permute-start.4 = (bf16[768,256]{1,0:T(8,128)(2,1)S(1)}, bf16[768,256]{1,0:T(8,128)(2,1)S(1)}, u32[]{:S(2)}, u32[]{:S(2)}) collective-permute-start(bf16[768,256]{1,0:T(8,128)(2,1)S(1)} %get-tuple-element.29), channel_id=1, source_target_pairs={{0,4},{4,0},{1,5},{5,1},{2,6},{6,2},{3,7},{7,3},{8,12},{12,8},{9,1... | collective-permute-start | bytes 1179656 | tf_op jit(solution)/shard_map/ppermute | solution.py:542
  36.0 17.3 %copy-start.1 = (s32[2]{0:T(128)S(1)}, s32[2]{0:T(128)}, u32[]{:S(2)}) copy-start(s32[2]{0:T(128)} %counts_ref.1) | copy-start | bytes 28
  82.0 10.6 %collective-permute-start.8 = (bf16[16,96,256]{2,1,0:T(8,128)(2,1)S(1)}, bf16[16,96,256]{2,1,0:T(8,128)(2,1)S(1)}, u32[]{:S(2)}, u32[]{:S(2)}) collective-permute-start(bf16[16,96,256]{2,1,0:T(8,128)(2,1)S(1)} %get-tuple-element.48), channel_id=1, source_target_pairs={{0,4},{4,0},{1,5},{5,1},{2,6},{6,2},{3,7},{7,3},{8,12},{12,8},{9,1... | collective-permute-start | bytes 2359304 | tf_op jit(solution)/shard_map/ppermute | solution.py:542
  82.4 5.5 %collective-permute-start.9 = (bf16[64,256]{1,0:T(8,128)(2,1)S(1)}, bf16[64,256]{1,0:T(8,128)(2,1)S(1)}, u32[]{:S(2)}, u32[]{:S(2)}) collective-permute-start(bf16[64,256]{1,0:T(8,128)(2,1)S(1)} %reduce_sum.12.own_ref), channel_id=1, source_target_pairs={{0,2},{2,0},{1,3},{3,1},{4,6},{6,4},{5,7},{7,5},{8,10},{10,8},{9,1... | collective-permute-start | bytes 98312 | tf_op jit(solution)/shard_map/ppermute | solution.py:546
  88.8 12.2 %all-to-all-start.4 = ((bf16[16,64,256]{2,1,0:T(8,128)(2,1)}), bf16[16,64,256]{2,1,0:T(8,128)(2,1)S(1)}, u32[]{:S(2)}, u32[]{:S(2)}) async-start(bf16[16,64,256]{2,1,0:T(8,128)(2,1)} %spread.1), calls=%async_computation.4 | async-start | bytes 1048576 | tf_op jit(solution)/shard_map/all_to_all | solution.py:538
